TPU v7x, 128 devices: a whole 4x4x4 slice. The times are simulated.
128 devices in a mesh: seq: 8 (over z, core), dp: 16 (over x, y).
Axes of the slice: x: 4, y: 4, z: 4, core: 2. Of those that a mesh axis runs over, the one named last changes fastest.
Arguments:
- layer_input: bfloat16 [32768, 1024], P(('dp', 'seq')), may hold values from -6 to 6
- out_grad: bfloat16 [32768, 1024], P(('dp', 'seq')), may hold values from -6 to 6
- lengths: int32 [16, 3], P('dp'), may hold values from 1 to 1365, 2048 in all within a row
- item_owner: int32 [32768, 1], P(('dp', 'seq')), may hold values from 0 to 127; in each aligned block of 256 rows (0 to 255, 256 to 511, ...) at most 4 rows name the same one
- item_row: int32 [32768], P(('dp', 'seq')), may hold values from 0 to 511
- w_attn: bfloat16 [1024, 3072], replicated, may hold values from -0.1875 to 0.1875
- w_gate: bfloat16 [1024, 1024], replicated, may hold values from -0.1875 to 0.1875
- w_out: bfloat16 [1024, 1024], replicated, may hold values from -0.1875 to 0.1875
- emb_table: float32 [65536, 1024], P(('seq', 'dp')), may hold values from -6 to 6
- row_accum: float32 [65536], P(('seq', 'dp')), may hold values from 0.25 to 4
Outputs:
- grad_attn: float32 [1024, 3072], P('dp', 'seq')
- grad_gate: float32 [1024, 1024], P('dp', 'seq')
- grad_out: float32 [1024, 1024], P('dp', 'seq')
- new_table: float32 [65536, 1024], P(('seq', 'dp'))
- new_accum: float32 [65536], P(('seq', 'dp'))
Inputs may be any that keep to these rules, and one draw needn't show every extreme that they name: Each group's 3 lengths sum to 2048; the largest is exactly 1365. `item_owner`: among the 256 events of one device at most 4 name one owner, a bound that some block reaches.
All inputs are finite; a program needn't handle non-finite values.
Results may differ from a plain program's by a relative error of at most 0.0092.
Values may be sent and summed in bfloat16 or wider, within the bound.
A program may use at most 128 MiB of HBM per device.

v0:
```python
import functools

import jax
import jax.numpy as jnp
from jax import lax
from jax.experimental import pallas as pl
from jax.experimental.pallas import tpu as pltpu
from jax.sharding import PartitionSpec as P

D = 1024
H = 16
DH = 64
NORM_EPS = 1e-05
LEARN_RATE = 0.1
TQ = 256
TK = 256
VMEM_BYTES = 56 * 1024 * 1024

BF = jnp.bfloat16
F32 = jnp.float32
NN = (((1,), (0,)), ((), ()))
NT = (((1,), (1,)), ((), ()))


def mm(a, b, dims=NN):
    return lax.dot_general(a, b, dims, preferred_element_type=F32)


def silu(z):
    t = 0.5 * z
    return t + t * jnp.tanh(t)


def silu_grad(z):
    t = 0.5 * z
    th = jnp.tanh(t)
    return 0.5 * ((1.0 + th) * (1.0 + t * (1.0 - th)))


def event_starts(len_ref, places):
    end0 = len_ref[0]
    end1 = end0 + len_ref[1]
    return jnp.where(places >= end1, end1, jnp.where(places >= end0, end0, 0))


def scalar_start(len_ref, place):
    end0 = len_ref[0]
    end1 = end0 + len_ref[1]
    return jnp.where(place >= end1, end1, jnp.where(place >= end0, end0, 0))


def tile_allowed(len_ref, j, i):
    keys = j * TK + lax.broadcasted_iota(jnp.int32, (TK, TQ), 0)
    places = i * TQ + lax.broadcasted_iota(jnp.int32, (1, TQ), 1)
    return (keys >= event_starts(len_ref, places)) & (keys <= places)


def fwd_kernel(pos, maxlen, len_ref, x_ref, og_ref, wt_ref, wo_ref, pre_ref, h_ref, mg_ref, st_ref, v_s, q_s, k_s):
    chunk = 512

    @pl.loop(0, pos // chunk)
    def _(c):
        at = pl.ds(pl.multiple_of(c * chunk, chunk), chunk)
        pre = mm(wt_ref[...], x_ref[at, :], NT)
        pre_ref[:, at] = pre
        act = silu(pre[: 6 * DH])
        for hd in range(2):
            base = hd * 3 * DH
            v_s[hd, :, at] = act[base : base + DH].astype(BF)
            q_s[hd, :, at] = (act[base + DH : base + 2 * DH].astype(BF) * 0.0625).astype(BF)
            k_s[hd, at, :] = act[base + 2 * DH : base + 3 * DH].astype(BF).T
        mg_ref[:, at] = mm(wo_ref[...], og_ref[at, :], NT)

    @pl.loop(0, pos // TQ)
    def _(i):
        at = pl.ds(pl.multiple_of(i * TQ, TQ), TQ)
        first = scalar_start(len_ref, i * TQ) // TK
        last = ((i + 1) * TQ - 1) // TK

        def step(j, accs):
            kat = pl.ds(pl.multiple_of(j * TK, TK), TK)
            allowed = tile_allowed(len_ref, j, i)
            outs = []
            for hd in range(2):
                t = mm(k_s[hd, kat, :], q_s[hd, :, at])
                w = jnp.where(allowed, t + t * jnp.tanh(t), 0.0).astype(BF)
                outs.append(accs[hd] + mm(v_s[hd, :, kat], w))
            return tuple(outs)

        zero = jnp.zeros((DH, TQ), F32)
        accs = lax.fori_loop(first, last + 1, step, (zero, zero))
        for hd in range(2):
            h_ref[hd * DH : (hd + 1) * DH, at] = (accs[hd] * (1.0 / maxlen)).astype(BF)

    @pl.loop(0, pos // chunk)
    def _(c):
        at = pl.ds(pl.multiple_of(c * chunk, chunk), chunk)
        h = h_ref[:, at].astype(F32)
        mean = jnp.sum(h, axis=0, keepdims=True) * (1.0 / (2 * DH))
        cen = h - mean
        ng = mg_ref[:, at] * silu(pre_ref[6 * DH :, at])
        st_ref[0:1, at] = mean
        st_ref[1:2, at] = jnp.sum(cen * cen, axis=0, keepdims=True)
        st_ref[2:3, at] = jnp.sum(ng, axis=0, keepdims=True)
        st_ref[3:4, at] = jnp.sum(ng * cen, axis=0, keepdims=True)
        st_ref[4:8, at] = jnp.zeros((4, chunk), F32)


def bwd_kernel(
    pos, maxlen, seq_count,
    len_ref, sta_ref, pre_ref, h_ref, mg_ref, wt_ref, x_hbm, og_hbm,
    ig_ref, gw_ref, go_ref,
    x_s, og_s, sems, q_s, kt_s, k_s, v_s, qn_s, ot_s, o_s, mix_s, g_s, gn_s, dv_s, dk_s, dq_s,
):
    x_copy = pltpu.make_async_copy(x_hbm, x_s, sems.at[0])
    og_copy = pltpu.make_async_copy(og_hbm, og_s, sems.at[1])
    x_copy.start()
    og_copy.start()
    chunk = 512

    @pl.loop(0, pos // chunk)
    def _(c):
        at = pl.ds(pl.multiple_of(c * chunk, chunk), chunk)
        act = silu(pre_ref[: 6 * DH, at]).astype(BF)
        means = [sta_ref[8 * d : 8 * d + 1, at] for d in range(seq_count)]
        mean = functools.reduce(jnp.add, means) * (1.0 / seq_count)
        var = jnp.zeros_like(mean)
        ng_mean = jnp.zeros_like(mean)
        ng_cov = jnp.zeros_like(mean)
        for d in range(seq_count):
            off = means[d] - mean
            ng_sum = sta_ref[8 * d + 2 : 8 * d + 3, at]
            var = var + sta_ref[8 * d + 1 : 8 * d + 2, at] + (2 * DH) * off * off
            ng_mean = ng_mean + ng_sum
            ng_cov = ng_cov + sta_ref[8 * d + 3 : 8 * d + 4, at] + off * ng_sum
        inv = lax.rsqrt(var * (1.0 / D) + NORM_EPS)
        ng_mean = ng_mean * (1.0 / D)
        proj = inv * ng_cov * (1.0 / D)
        gate_pre = pre_ref[6 * DH :, at]
        gate = silu(gate_pre)
        normed = (h_ref[:, at].astype(F32) - mean) * inv
        mix_s[:, at] = (normed * gate).astype(BF)
        mg = mg_ref[:, at]
        g_s[6 * DH :, at] = (mg * normed * silu_grad(gate_pre)).astype(BF)
        hg = (inv * (mg * gate - ng_mean - normed * proj)).astype(BF)
        for hd in range(2):
            base = hd * 3 * DH
            q16 = (act[base + DH : base + 2 * DH] * 0.0625).astype(BF)
            k = act[base + 2 * DH : base + 3 * DH]
            q_s[hd, :, at] = q16
            kt_s[hd, :, at] = k
            k_s[hd, at, :] = k.T
            v_s[hd, at, :] = act[base : base + DH].T
            qn_s[hd, at, :] = q16.T
            o = hg[hd * DH : (hd + 1) * DH]
            ot_s[hd, :, at] = o
            o_s[hd, at, :] = o.T
            dv_s[hd, at, :] = jnp.zeros((chunk, DH), F32)
            dk_s[hd, at, :] = jnp.zeros((chunk, DH), F32)

    @pl.loop(0, pos // TQ)
    def _(i):
        at = pl.ds(pl.multiple_of(i * TQ, TQ), TQ)
        first = scalar_start(len_ref, i * TQ) // TK
        last = ((i + 1) * TQ - 1) // TK

        def step(j, accs):
            kat = pl.ds(pl.multiple_of(j * TK, TK), TK)
            allowed = tile_allowed(len_ref, j, i)
            outs = []
            for hd in range(2):
                t = mm(k_s[hd, kat, :], q_s[hd, :, at])
                dw = mm(v_s[hd, kat, :], ot_s[hd, :, at])
                a = 1.0 + jnp.tanh(t)
                w = t * a
                ds = jnp.where(allowed, dw * (a + w * (2.0 - a)), 0.0).astype(BF)
                w = jnp.where(allowed, w, 0.0).astype(BF)
                dv_s[hd, kat, :] += mm(w, o_s[hd, at, :])
                dk_s[hd, kat, :] += mm(ds, qn_s[hd, at, :])
                outs.append(accs[hd] + mm(kt_s[hd, :, kat], ds))
            return tuple(outs)

        zero = jnp.zeros((DH, TQ), F32)
        accs = lax.fori_loop(first, last + 1, step, (zero, zero))
        for hd in range(2):
            dq_s[hd, :, at] = accs[hd]

    fac = 0.0625 / maxlen

    @pl.loop(0, pos // chunk)
    def _(c):
        at = pl.ds(pl.multiple_of(c * chunk, chunk), chunk)
        sg = silu_grad(pre_ref[: 6 * DH, at])
        for hd in range(2):
            base = hd * 3 * DH
            dv = (dv_s[hd, at, :] * (1.0 / maxlen)).astype(BF).T
            dk = (dk_s[hd, at, :] * (16.0 * fac)).astype(BF).T
            dq = (dq_s[hd, :, at] * fac).astype(BF)
            for part, grad in enumerate((dv, dq, dk)):
                rows = slice(base + part * DH, base + (part + 1) * DH)
                g_s[rows, at] = (grad.astype(F32) * sg[rows]).astype(BF)
        gn_s[at, :] = g_s[:, at].T
        ig_ref[at, :] = mm(gn_s[at, :], wt_ref[...]).astype(BF)

    x_copy.wait()
    gw_ref[...] = mm(g_s[...], x_s[...]).astype(BF).T
    og_copy.wait()
    go_ref[...] = mm(mix_s[...], og_s[...]).astype(BF)


def vmem(count):
    return [pl.BlockSpec(memory_space=pltpu.VMEM)] * count


def forward(lens, x_g, og_g, wt, wo, pos, maxlen):
    return pl.pallas_call(
        functools.partial(fwd_kernel, pos, maxlen),
        out_shape=(
            jax.ShapeDtypeStruct((8 * DH, pos), F32),
            jax.ShapeDtypeStruct((2 * DH, pos), BF),
            jax.ShapeDtypeStruct((2 * DH, pos), F32),
            jax.ShapeDtypeStruct((8, pos), F32),
        ),
        in_specs=[pl.BlockSpec(memory_space=pltpu.SMEM)] + vmem(4),
        out_specs=tuple(vmem(4)),
        scratch_shapes=[
            pltpu.VMEM((2, DH, pos), BF),
            pltpu.VMEM((2, DH, pos), BF),
            pltpu.VMEM((2, pos, DH), BF),
        ],
        compiler_params=pltpu.CompilerParams(vmem_limit_bytes=VMEM_BYTES),
        name="forward",
    )(lens, x_g, og_g, wt, wo)


def backward(lens, stats, pre, h, mg, wt, x_g, og_g, pos, maxlen, seq_count):
    heads_t = pltpu.VMEM((2, DH, pos), BF)
    heads_n = pltpu.VMEM((2, pos, DH), BF)
    sums_n = pltpu.VMEM((2, pos, DH), F32)
    return pl.pallas_call(
        functools.partial(bwd_kernel, pos, maxlen, seq_count),
        out_shape=(
            jax.ShapeDtypeStruct((pos, D), BF),
            jax.ShapeDtypeStruct((D, 8 * DH), BF),
            jax.ShapeDtypeStruct((2 * DH, D), BF),
        ),
        in_specs=[pl.BlockSpec(memory_space=pltpu.SMEM)] + vmem(5) + [pl.BlockSpec(memory_space=pl.ANY)] * 2,
        out_specs=tuple(vmem(3)),
        scratch_shapes=[
            pltpu.VMEM((pos, D), BF),
            pltpu.VMEM((pos, D), BF),
            pltpu.SemaphoreType.DMA((2,)),
            heads_t, heads_t, heads_n, heads_n, heads_n, heads_t, heads_n,
            pltpu.VMEM((2 * DH, pos), BF),
            pltpu.VMEM((8 * DH, pos), BF),
            pltpu.VMEM((pos, 8 * DH), BF),
            sums_n, sums_n,
            pltpu.VMEM((2, DH, pos), F32),
        ],
        compiler_params=pltpu.CompilerParams(vmem_limit_bytes=VMEM_BYTES),
        name="backward",
    )(lens, stats, pre, h, mg, wt, x_g, og_g)


def body(
    layer_input,
    out_grad,
    lengths,
    item_owner,
    item_row,
    w_attn,
    w_gate,
    w_out,
    emb_table,
    row_accum,
):
    seq_count = lax.axis_size("seq")
    dp_count = lax.axis_size("dp")
    devices = seq_count * dp_count
    me = lax.axis_index("seq")
    tokens_dev = layer_input.shape[0]
    pos = tokens_dev * seq_count
    maxlen = 2 * pos // 3
    wt = jnp.concatenate(
        [
            lax.dynamic_slice_in_dim(w_attn, me * 6 * DH, 6 * DH, 1).T,
            lax.dynamic_slice_in_dim(w_gate, me * 2 * DH, 2 * DH, 1).T,
        ],
        axis=0,
    )
    wo = lax.dynamic_slice_in_dim(w_out, me * 2 * DH, 2 * DH, 0)
    lens = lengths[0]
    x_g = lax.all_gather(layer_input, "seq", axis=0, tiled=True)
    og_g = lax.all_gather(out_grad, "seq", axis=0, tiled=True)
    pre, h, mg, stats = forward(lens, x_g, og_g, wt, wo, pos, maxlen)
    stats = lax.all_gather(stats, "seq", axis=0, tiled=True)
    ig, gw, go = backward(lens, stats, pre, h, mg, wt, x_g, og_g, pos, maxlen, seq_count)
    ig = lax.all_to_all(ig.reshape(seq_count, tokens_dev, D), "seq", 0, 0, tiled=True)
    input_grad = jnp.sum(ig.astype(F32), axis=0) + out_grad.astype(F32)
    gw = lax.all_to_all(gw.reshape(dp_count, D // dp_count, 8 * DH), "dp", 0, 0, tiled=True)
    gw = jnp.sum(gw.astype(F32), axis=0)
    go = lax.all_to_all(go, "seq", 1, 0, tiled=True)
    go = lax.all_to_all(go.reshape(dp_count, D // dp_count, 2 * DH), "dp", 0, 0, tiled=True)
    go = jnp.sum(go.astype(F32), axis=0)

    rows_own = emb_table.shape[0]
    capacity = max(2, 2 * tokens_dev // devices)
    owners = item_owner[:, 0]
    hits = (owners[:, None] == jnp.arange(devices, dtype=jnp.int32)[None, :]).astype(jnp.int32)
    slots = jnp.sum((jnp.cumsum(hits, axis=0) - hits) * hits, axis=1)
    flat_slot = owners * capacity + slots
    total = devices * capacity
    place = (jnp.arange(total, dtype=jnp.int32)[:, None] == flat_slot[None, :])
    send_rows = mm(place.astype(BF), input_grad.astype(BF)).astype(BF)
    send_ids = jnp.sum(jnp.where(place, item_row[None, :] + 1, 0), axis=1) - 1
    got_rows = lax.all_to_all(send_rows.reshape(devices, capacity, D), ("seq", "dp"), 0, 0, tiled=True)
    got_ids = lax.all_to_all(send_ids.reshape(devices, capacity), ("seq", "dp"), 0, 0, tiled=True)
    pick = (jnp.arange(rows_own, dtype=jnp.int32)[:, None] == got_ids.reshape(1, total)).astype(BF)
    table_grad = mm(pick, got_rows.reshape(total, D))
    new_accum = row_accum + jnp.mean(table_grad * table_grad, axis=1)
    new_table = emb_table - LEARN_RATE * table_grad * lax.rsqrt(new_accum)[:, None]
    return (gw[:, : 6 * DH], gw[:, 6 * DH :], go, new_table, new_accum)


def solution(mesh):
    placed = (
        P(("dp", "seq"), None),
        P(("dp", "seq"), None),
        P("dp", None),
        P(("dp", "seq"), None),
        P(("dp", "seq")),
        P(),
        P(),
        P(),
        P(("seq", "dp"), None),
        P(("seq", "dp")),
    )
    return jax.shard_map(
        body,
        mesh=mesh,
        in_specs=placed,
        out_specs=(
            P("dp", "seq"),
            P("dp", "seq"),
            P("dp", "seq"),
            P(("seq", "dp"), None),
            P(("seq", "dp")),
        ),
        check_vma=False,
    )
```

profile of v0, /device:TPU:0, one launch (start us, length us, event | category | flops | bytes accessed | tf_op | source)
XLA Modules:
  0.0 290.4 jit_solution(8795147717485450019)
XLA Ops:
  7.2 0.0 copy-start
  7.2 0.0 all-gather.3.cloned.1.call-start
  7.2 0.7 all-gather.3.cloned.1.call-update
  7.9 0.0 all-gather.5.cloned.1.call-start
  8.0 0.7 all-gather.5.cloned.1.call-update
  8.7 0.8 copy.32
  9.5 0.2 fusion.3
  9.8 0.9 fusion.5
  10.6 0.7 broadcast_add_fusion.2
  11.3 0.7 multiply_add_fusion.1
  12.0 0.1 select_reduce_fusion
  12.1 0.7 sub.14
  12.9 11.1 %all-to-all-start.3 = ((s32[128,1,4]{2,1,0:T(1,128)}), s32[128,1,4]{2,1,0:T(1,128)S(1)}, u32[]{:S(2)}, u32[]{:S(2)}) async-start(s32[128,1,4]{2,1,0:T(1,128)} %bitcast.11), calls=%async_computation.3 | async-start | bytes 131072 | tf_op jit(solution)/shard_map/all_to_all | solution.py:317
  24.0 0.1 constant_dynamic-slice_fusion.1
  24.1 0.1 copy.36
  24.3 1.2 constant_dynamic-slice_fusion.2
  25.5 1.2 copy.35
  26.7 1.7 constant_dynamic-slice_fusion.wo_ref
  28.4 2.2 pad_maximum_fusion.wt_ref
  30.6 14.7 %all-gather.3.cloned.1.call-done.x_ref.x_hbm = bf16[2048,1024]{1,0:T(8,128)(2,1)} async-done(((bf16[256,1024]{1,0:T(8,128)(2,1)}), bf16[2048,1024]{1,0:T(8,128)(2,1)}) %all-gather.3.cloned.1.call-update) | async-done | bytes 4194320 | tf_op jit(solution)/shard_map/all_gather | solution.py:293
  45.3 33.9 %all-gather.5.cloned.1.call-done.og_ref.og_hbm = bf16[2048,1024]{1,0:T(8,128)(2,1)} async-done(((bf16[256,1024]{1,0:T(8,128)(2,1)}), bf16[2048,1024]{1,0:T(8,128)(2,1)}) %all-gather.5.cloned.1.call-update) | async-done | bytes 4194320 | tf_op jit(solution)/shard_map/all_gather | solution.py:294
  79.1 25.1 %forward.1 = (f32[512,2048]{1,0:T(8,128)}, bf16[128,2048]{1,0:T(8,128)(2,1)}, f32[128,2048]{1,0:T(8,128)}, f32[8,2048]{1,0:T(8,128)}) custom-call(s32[3]{0:T(128)} %bitcast.40, bf16[2048,1024]{1,0:T(8,128)(2,1)} %all-gather.3.cloned.1.call-done.x_ref.x_hbm, bf16[2048,1024]{1,0:T(8,128)(2,1)} %all-gather.5.cloned.1.call-done.og_ref.og_hbm, ...), custom_call_target="tpu_custom_call" | custom-call | tf_op jit(solution)/shard_map/forward/pallas_call | solution.py:216
  104.2 14.4 %all_gather.11.sta_ref = f32[64,2048]{1,0:T(8,128)} all-gather(f32[8,2048]{1,0:T(8,128)} %get-tuple-element.12), channel_id=1, replica_groups=mesh['seq'=8,'dp'=16] {'seq'}, dimensions={0}, use_global_device_ids=true | all-gather | bytes 589824 | tf_op jit(solution)/shard_map/all_gather | solution.py:296
  118.6 29.6 %backward.1 = (bf16[2048,1024]{1,0:T(8,128)(2,1)}, bf16[1024,512]{1,0:T(8,128)(2,1)}, bf16[128,1024]{1,0:T(8,128)(2,1)}) custom-call(s32[3]{0:T(128)} %bitcast.41, f32[64,2048]{1,0:T(8,128)} %all_gather.11.sta_ref, f32[512,2048]{1,0:T(8,128)} %get-tuple-element.13.pre_ref, bf16[128,2048]{1,0:T(8,128)(2,1)} %get-tuple-element.14.h_ref, ...), custom_call_target="tpu_custom_call" | custom-call | tf_op jit(solution)/shard_map/backward/pallas_call | solution.py:240
  148.2 1.0 copy_bitcast_fusion
  149.2 0.0 all-to-all-done.3
  149.2 10.1 %all_to_all.42 = bf16[128,8,128]{2,0,1:T(8,128)(2,1)S(1)} all-to-all(bf16[128,8,128]{2,0,1:T(8,128)(2,1)S(1)} %copy_bitcast_fusion), channel_id=1, replica_groups=mesh['seq'=8,'dp'=16] {'seq'}, dimensions={1} | all-to-all | bytes 524288 | tf_op jit(solution)/shard_map/all_to_all | solution.py:302
  159.3 18.4 %all_to_all.43 = bf16[16,64,128]{2,1,0:T(8,128)(2,1)S(1)} all-to-all(bf16[16,64,128]{2,1,0:T(8,128)(2,1)S(1)} %bitcast.32), channel_id=1, replica_groups=mesh['seq'=8,'dp'=16] {'dp'}, dimensions={0} | all-to-all | bytes 524288 | tf_op jit(solution)/shard_map/all_to_all | solution.py:303
  177.8 54.8 %all_to_all.44 = bf16[8,256,1024]{2,1,0:T(8,128)(2,1)} all-to-all(bf16[8,256,1024]{2,1,0:T(8,128)(2,1)} %bitcast.30), channel_id=1, replica_groups=mesh['seq'=8,'dp'=16] {'seq'}, dimensions={0} | all-to-all | bytes 8388608 | tf_op jit(solution)/shard_map/all_to_all | solution.py:298
  232.6 4.4 %all-to-all-start = ((bf16[16,64,512]{2,1,0:T(8,128)(2,1)}), bf16[16,64,512]{2,1,0:T(8,128)(2,1)}, u32[]{:S(2)}, u32[]{:S(2)}) async-start(bf16[16,64,512]{2,1,0:T(8,128)(2,1)} %bitcast.3), calls=%async_computation | async-start | bytes 2097152 | tf_op jit(solution)/shard_map/all_to_all | solution.py:300
  236.9 0.0 copy-start.1
  236.9 3.2 %convert_reduce_fusion = f32[256,1024]{1,0:T(8,128)S(1)} fusion(bf16[8,256,1024]{2,1,0:T(8,128)(2,1)} %all_to_all.44), kind=kLoop, calls=%fused_computation | loop fusion | flops 3932160 | bytes 5242880 | tf_op jit(solution)/shard_map/reduce_sum | solution.py:299
  240.1 0.5 convolution_convert_fusion
  240.6 1.2 reshape.79
  241.8 12.6 %all-to-all-done = bf16[16,64,512]{2,1,0:T(8,128)(2,1)} async-done(((bf16[16,64,512]{2,1,0:T(8,128)(2,1)}), bf16[16,64,512]{2,1,0:T(8,128)(2,1)}, u32[]{:S(2)}, u32[]{:S(2)}) %all-to-all-start) | async-done | bytes 1048608 | tf_op jit(solution)/shard_map/all_to_all | solution.py:300
  254.5 4.6 %all-to-all-start.5 = ((bf16[128,4,1024]{2,1,0:T(4,128)(2,1)}), bf16[128,4,1024]{2,1,0:T(4,128)(2,1)S(1)}, u32[]{:S(2)}, u32[]{:S(2)}) async-start(bf16[128,4,1024]{2,1,0:T(4,128)(2,1)} %reshape.79), calls=%async_computation.5 | async-start | bytes 2097152 | tf_op jit(solution)/shard_map/all_to_all | solution.py:316
  259.1 0.5 broadcast.45
  259.6 0.8 reduce.3
  260.4 0.1 eq.62
  260.5 0.7 convert_reduce_fusion.2
  261.2 1.4 convert_reduce_fusion.1
  262.6 0.6 slice.16
  263.2 0.6 slice.17
  263.8 14.3 %all-to-all-done.5 = bf16[128,4,1024]{2,1,0:T(4,128)(2,1)S(1)} async-done(((bf16[128,4,1024]{2,1,0:T(4,128)(2,1)}), bf16[128,4,1024]{2,1,0:T(4,128)(2,1)S(1)}, u32[]{:S(2)}, u32[]{:S(2)}) %all-to-all-start.5) | async-done | bytes 1048608 | tf_op jit(solution)/shard_map/all_to_all | solution.py:316
  278.1 1.1 reshape.80
  279.2 2.2 multiply_reduce_fusion
  281.4 0.6 rsqrt_multiply_fusion
  282.0 1.6 multiply_subtract_fusion
  (13 shorter events, 0.1 us)
Async XLA Ops:
  7.2 16.9 %copy-start = (bf16[1024,1024]{1,0:T(8,128)(2,1)S(1)}, bf16[1024,1024]{1,0:T(8,128)(2,1)}, u32[]{:S(2)}) copy-start(bf16[1024,1024]{1,0:T(8,128)(2,1)} %param.16) | copy-start | bytes 6291460
  7.2 38.1 %all-gather.3.cloned.1.call-start = ((), (), s32[]{:S(2)}) async-start(), calls=%async_computation.6 | async-start | bytes 4718592 | tf_op jit(solution)/shard_map/all_gather | solution.py:293
  7.9 71.2 %all-gather.5.cloned.1.call-start = ((), (), s32[]{:S(2)}) async-start(), calls=%async_computation.7 | async-start | bytes 4718592 | tf_op jit(solution)/shard_map/all_gather | solution.py:294
  12.9 136.4 %all-to-all-start.3 = ((s32[128,1,4]{2,1,0:T(1,128)}), s32[128,1,4]{2,1,0:T(1,128)S(1)}, u32[]{:S(2)}, u32[]{:S(2)}) async-start(s32[128,1,4]{2,1,0:T(1,128)} %bitcast.11), calls=%async_computation.3 | async-start | bytes 131072 | tf_op jit(solution)/shard_map/all_to_all | solution.py:317
  232.6 21.9 %all-to-all-start = ((bf16[16,64,512]{2,1,0:T(8,128)(2,1)}), bf16[16,64,512]{2,1,0:T(8,128)(2,1)}, u32[]{:S(2)}, u32[]{:S(2)}) async-start(bf16[16,64,512]{2,1,0:T(8,128)(2,1)} %bitcast.3), calls=%async_computation | async-start | bytes 2097152 | tf_op jit(solution)/shard_map/all_to_all | solution.py:300
  236.9 3.2 %copy-start.1 = (bf16[256,1024]{1,0:T(8,128)(2,1)S(1)}, bf16[256,1024]{1,0:T(8,128)(2,1)}, u32[]{:S(2)}) copy-start(bf16[256,1024]{1,0:T(8,128)(2,1)} %param.11) | copy-start | bytes 1572868
  254.5 23.7 %all-to-all-start.5 = ((bf16[128,4,1024]{2,1,0:T(4,128)(2,1)}), bf16[128,4,1024]{2,1,0:T(4,128)(2,1)S(1)}, u32[]{:S(2)}, u32[]{:S(2)}) async-start(bf16[128,4,1024]{2,1,0:T(4,128)(2,1)} %reshape.79), calls=%async_computation.5 | async-start | bytes 2097152 | tf_op jit(solution)/shard_map/all_to_all | solution.py:316
  279.2 2.2 copy-start.3
  279.2 2.8 copy-start.2
Sparse Core Ops, SparseCore 0:
  9.7 35.4 all-gather.2
  47.0 32.1 all-gather.4
where the time goes:
time: 291 us; the launch traced here: 290 us
  blocking collectives  97.7 us (34%)
  waiting for transfers between devices  76.9 us (26%)
  Pallas kernels  54.7 us (19%)
  starting transfers between devices  20.2 us (7%)
  between operations  14.2 us (5%)
  other arithmetic  13 us (4%)
  local copies, waits for them, and re-layouts  11.1 us (4%)
    all_to_all x1, blocking collectives, body(): lax.all_to_all(ig.reshape(seq_count, tokens_dev, D), 'seq', 0, 0, tiled=T...  54.8 us
    all_gather x1, waiting for transfers between devices, body(): og_g = lax.all_gather(out_grad, 'seq', axis=0, tiled=True)  33.9 us
    pallas_call x1, Pallas kernels, backward(): pl.pallas_call(functools.partial(bwd_kernel, pos, maxlen, seq_count), out...  29.6 us
    pallas_call x1, Pallas kernels, forward(): pl.pallas_call(functools.partial(fwd_kernel, pos, maxlen), out_shape=(jax...  25.1 us
    all_to_all x1, blocking collectives, body(): lax.all_to_all(go.reshape(dp_count, D // dp_count, 2 * DH), 'dp', 0, 0, t...  18.4 us
    all_gather x1, waiting for transfers between devices, body(): x_g = lax.all_gather(layer_input, 'seq', axis=0, tiled=True)  14.7 us
    all_gather x1, blocking collectives, body(): stats = lax.all_gather(stats, 'seq', axis=0, tiled=True)  14.4 us
    all_to_all x1, waiting for transfers between devices, body(): lax.all_to_all(send_rows.reshape(devices, capacity, D), ('seq', 'dp'), 0,...  14.3 us
  transfers between devices with their start and end apart: 5, of which 4 were waited for; matrix products, arithmetic and copies ran while one was open for 7% of the time, Pallas kernels for 19%

commit v1 on v0

--- a/solution.py
+++ b/solution.py
@@ -20,6 +20,7 @@
 F32 = jnp.float32
 NN = (((1,), (0,)), ((), ()))
 NT = (((1,), (1,)), ((), ()))
+MESH = pl.DeviceIdType.MESH
 
 
 def mm(a, b, dims=NN):
@@ -55,21 +56,18 @@
     return (keys >= event_starts(len_ref, places)) & (keys <= places)
 
 
-def fwd_kernel(pos, maxlen, len_ref, x_ref, og_ref, wt_ref, wo_ref, pre_ref, h_ref, mg_ref, st_ref, v_s, q_s, k_s):
+def fwd_kernel(pos, maxlen, len_ref, pre_ref, mg_ref, h_ref, st_ref, v_s, q_s, k_s):
     chunk = 512
 
     @pl.loop(0, pos // chunk)
     def _(c):
         at = pl.ds(pl.multiple_of(c * chunk, chunk), chunk)
-        pre = mm(wt_ref[...], x_ref[at, :], NT)
-        pre_ref[:, at] = pre
-        act = silu(pre[: 6 * DH])
+        act = silu(pre_ref[: 6 * DH, at])
         for hd in range(2):
             base = hd * 3 * DH
             v_s[hd, :, at] = act[base : base + DH].astype(BF)
             q_s[hd, :, at] = (act[base + DH : base + 2 * DH].astype(BF) * 0.0625).astype(BF)
             k_s[hd, at, :] = act[base + 2 * DH : base + 3 * DH].astype(BF).T
-        mg_ref[:, at] = mm(wo_ref[...], og_ref[at, :], NT)
 
     @pl.loop(0, pos // TQ)
     def _(i):
@@ -92,18 +90,24 @@
         for hd in range(2):
             h_ref[hd * DH : (hd + 1) * DH, at] = (accs[hd] * (1.0 / maxlen)).astype(BF)
 
-    @pl.loop(0, pos // chunk)
-    def _(c):
-        at = pl.ds(pl.multiple_of(c * chunk, chunk), chunk)
+    for c in range(pos // chunk):
+        at = slice(c * chunk, (c + 1) * chunk)
+        row, lane = stat_place(pos, chunk, c)
         h = h_ref[:, at].astype(F32)
         mean = jnp.sum(h, axis=0, keepdims=True) * (1.0 / (2 * DH))
         cen = h - mean
-        ng = mg_ref[:, at] * silu(pre_ref[6 * DH :, at])
-        st_ref[0:1, at] = mean
-        st_ref[1:2, at] = jnp.sum(cen * cen, axis=0, keepdims=True)
-        st_ref[2:3, at] = jnp.sum(ng, axis=0, keepdims=True)
-        st_ref[3:4, at] = jnp.sum(ng * cen, axis=0, keepdims=True)
-        st_ref[4:8, at] = jnp.zeros((4, chunk), F32)
+        ng = mg_ref[:, at].astype(F32) * silu(pre_ref[6 * DH :, at])
+        st_ref[row : row + 1, lane] = mean
+        st_ref[row + 1 : row + 2, lane] = jnp.sum(cen * cen, axis=0, keepdims=True)
+        st_ref[row + 2 : row + 3, lane] = jnp.sum(ng, axis=0, keepdims=True)
+        st_ref[row + 3 : row + 4, lane] = jnp.sum(ng * cen, axis=0, keepdims=True)
+
+
+def stat_place(pos, chunk, c):
+    first = c * chunk
+    row = 4 * (first // (pos // 2))
+    lane = first % (pos // 2)
+    return row, slice(lane, lane + chunk)
 
 
 def bwd_kernel(
@@ -118,21 +122,21 @@
     og_copy.start()
     chunk = 512
 
-    @pl.loop(0, pos // chunk)
-    def _(c):
-        at = pl.ds(pl.multiple_of(c * chunk, chunk), chunk)
+    for c in range(pos // chunk):
+        at = slice(c * chunk, (c + 1) * chunk)
+        row, lane = stat_place(pos, chunk, c)
         act = silu(pre_ref[: 6 * DH, at]).astype(BF)
-        means = [sta_ref[8 * d : 8 * d + 1, at] for d in range(seq_count)]
+        means = [sta_ref[d, row : row + 1, lane] for d in range(seq_count)]
         mean = functools.reduce(jnp.add, means) * (1.0 / seq_count)
         var = jnp.zeros_like(mean)
         ng_mean = jnp.zeros_like(mean)
         ng_cov = jnp.zeros_like(mean)
         for d in range(seq_count):
             off = means[d] - mean
-            ng_sum = sta_ref[8 * d + 2 : 8 * d + 3, at]
-            var = var + sta_ref[8 * d + 1 : 8 * d + 2, at] + (2 * DH) * off * off
+            ng_sum = sta_ref[d, row + 2 : row + 3, lane]
+            var = var + sta_ref[d, row + 1 : row + 2, lane] + (2 * DH) * off * off
             ng_mean = ng_mean + ng_sum
-            ng_cov = ng_cov + sta_ref[8 * d + 3 : 8 * d + 4, at] + off * ng_sum
+            ng_cov = ng_cov + sta_ref[d, row + 3 : row + 4, lane] + off * ng_sum
         inv = lax.rsqrt(var * (1.0 / D) + NORM_EPS)
         ng_mean = ng_mean * (1.0 / D)
         proj = inv * ng_cov * (1.0 / D)
@@ -140,7 +144,7 @@
         gate = silu(gate_pre)
         normed = (h_ref[:, at].astype(F32) - mean) * inv
         mix_s[:, at] = (normed * gate).astype(BF)
-        mg = mg_ref[:, at]
+        mg = mg_ref[:, at].astype(F32)
         g_s[6 * DH :, at] = (mg * normed * silu_grad(gate_pre)).astype(BF)
         hg = (inv * (mg * gate - ng_mean - normed * proj)).astype(BF)
         for hd in range(2):
@@ -212,17 +216,15 @@
     return [pl.BlockSpec(memory_space=pltpu.VMEM)] * count
 
 
-def forward(lens, x_g, og_g, wt, wo, pos, maxlen):
+def forward(lens, pre, mg, pos, maxlen):
     return pl.pallas_call(
         functools.partial(fwd_kernel, pos, maxlen),
         out_shape=(
-            jax.ShapeDtypeStruct((8 * DH, pos), F32),
             jax.ShapeDtypeStruct((2 * DH, pos), BF),
-            jax.ShapeDtypeStruct((2 * DH, pos), F32),
-            jax.ShapeDtypeStruct((8, pos), F32),
+            jax.ShapeDtypeStruct((8, pos // 2), F32),
         ),
-        in_specs=[pl.BlockSpec(memory_space=pltpu.SMEM)] + vmem(4),
-        out_specs=tuple(vmem(4)),
+        in_specs=[pl.BlockSpec(memory_space=pltpu.SMEM)] + vmem(2),
+        out_specs=tuple(vmem(2)),
         scratch_shapes=[
             pltpu.VMEM((2, DH, pos), BF),
             pltpu.VMEM((2, DH, pos), BF),
@@ -230,7 +232,7 @@
         ],
         compiler_params=pltpu.CompilerParams(vmem_limit_bytes=VMEM_BYTES),
         name="forward",
-    )(lens, x_g, og_g, wt, wo)
+    )(lens, pre, mg)
 
 
 def backward(lens, stats, pre, h, mg, wt, x_g, og_g, pos, maxlen, seq_count):
@@ -262,6 +264,346 @@
     )(lens, stats, pre, h, mg, wt, x_g, og_g)
 
 
+def seq_peers():
+    me = lax.axis_index("seq")
+    z, c = me // 2, me % 2
+    at = lambda step: lax.rem(z + step, 4) * 2
+    return me, at(0) + 1 - c, at(1) + c, at(3) + c, at(2) + c, c
+
+
+def gather_kernel(
+    tokens,
+    x_ref, og_ref, wa_hbm, wg_hbm, wo_ref,
+    xg_ref, pre_ref, mg_ref, wt_ref,
+    x_s, w_s, mine_s, load_sem, keep_sem, send_sem, recv_sem, mg_send, mg_recv,
+):
+    me, sib, right, left, far, c = seq_peers()
+    half = tokens // 2
+    loads = [
+        pltpu.make_async_copy(wa_hbm.at[:, pl.ds(pl.multiple_of(me * 6 * DH, 128), 6 * DH)], w_s.at[:, : 6 * DH], load_sem.at[0]),
+        pltpu.make_async_copy(wg_hbm.at[:, pl.ds(pl.multiple_of(me * 2 * DH, 128), 2 * DH)], w_s.at[:, 6 * DH :], load_sem.at[1]),
+        pltpu.make_async_copy(x_ref, x_s.at[me], load_sem.at[2]),
+    ]
+    for load in loads:
+        load.start()
+
+    barrier = pltpu.get_barrier_semaphore()
+    for step in range(1, 8):
+        pl.semaphore_signal(barrier, inc=1, device_id={"seq": lax.rem(me + step, 8)}, device_id_type=MESH)
+    pl.semaphore_wait(barrier, 7)
+
+    def send(index, shard, part, to):
+        if part is None:
+            ref = x_s.at[shard]
+        else:
+            ref = x_s.at[shard, pl.ds(part * half, half)]
+        copy = pltpu.make_async_remote_copy(
+            src_ref=ref, dst_ref=ref, send_sem=send_sem.at[index], recv_sem=recv_sem.at[index],
+            device_id={"seq": to}, device_id_type=MESH,
+        )
+        copy.start()
+        return copy
+
+    def project(shard):
+        at = pl.ds(pl.multiple_of(shard * tokens, tokens), tokens)
+        pre_ref[:, at] = mm(wt_ref[...], x_s[shard], NT)
+        keep(shard)
+
+    keeps = []
+
+    def keep(shard):
+        copy = pltpu.make_async_copy(x_s.at[shard], xg_ref.at[shard], keep_sem.at[len(keeps)])
+        copy.start()
+        keeps.append(copy)
+
+    loads[2].wait()
+    to_right = [send(0, me, 0, right), None]
+    to_left = [None, send(1, me, 1, left)]
+    to_right[1] = send(2, me, 1, right)
+    to_left[0] = send(3, me, 0, left)
+    to_sib = send(4, me, None, sib)
+
+    mine_s[...] = mm(wo_ref[...], og_ref[...], NT).astype(BF)
+    mine = pl.ds(pl.multiple_of(me * tokens, tokens), tokens)
+    mg_copies = []
+    for step in range(1, 8):
+        to = lax.rem(me + step, 8)
+        copy = pltpu.make_async_remote_copy(
+            src_ref=mine_s.at[pl.ds(pl.multiple_of(to * 2 * DH, 2 * DH), 2 * DH)],
+            dst_ref=mg_ref.at[:, mine],
+            send_sem=mg_send.at[step], recv_sem=mg_recv.at[step],
+            device_id={"seq": to}, device_id_type=MESH,
+        )
+        copy.start()
+        mg_copies.append(copy)
+    mg_ref[:, mine] = mine_s[pl.ds(pl.multiple_of(me * 2 * DH, 2 * DH), 2 * DH), :]
+    loads[0].wait()
+    loads[1].wait()
+    wt_ref[...] = w_s[...].T
+    project(me)
+
+    z = me // 2
+    s_left, s_right, s_far = left, right, far
+    to_right[0].wait_recv()
+    fwd_r = send(5, s_left, 0, right)
+    to_left[1].wait_recv()
+    fwd_l = send(6, s_right, 1, left)
+    to_right[1].wait_recv()
+    sib_left = send(7, s_left, None, sib)
+    to_left[0].wait_recv()
+    sib_right = send(8, s_right, None, sib)
+    project(s_left)
+    project(s_right)
+    to_sib.wait_recv()
+    project(sib)
+    fwd_r.wait_recv()
+    sib_far0 = send(9, s_far, 0, sib)
+    fwd_l.wait_recv()
+    sib_far1 = send(10, s_far, 1, sib)
+    project(s_far)
+    other = 1 - 2 * c
+    sib_left.wait_recv()
+    project(s_left + other)
+    sib_right.wait_recv()
+    project(s_right + other)
+    sib_far0.wait_recv()
+    sib_far1.wait_recv()
+    project(s_far + other)
+    for copy in mg_copies:
+        copy.wait()
+    for copy in to_right + to_left + [to_sib, fwd_r, fwd_l, sib_left, sib_right, sib_far0, sib_far1]:
+        copy.wait_send()
+    for copy in keeps:
+        copy.wait()
+
+
+def gather(x, og, w_attn, w_gate, w_out, tokens, seq_count):
+    pos = tokens * seq_count
+    hbm = pl.BlockSpec(memory_space=pl.ANY)
+    x_g, pre, mg, wt = pl.pallas_call(
+        functools.partial(gather_kernel, tokens),
+        out_shape=(
+            jax.ShapeDtypeStruct((seq_count, tokens, D), BF),
+            jax.ShapeDtypeStruct((8 * DH, pos), F32),
+            jax.ShapeDtypeStruct((2 * DH, pos), BF),
+            jax.ShapeDtypeStruct((8 * DH, D), BF),
+        ),
+        in_specs=[hbm] + vmem(1) + [hbm, hbm] + vmem(1),
+        out_specs=tuple([hbm] + vmem(3)),
+        scratch_shapes=[
+            pltpu.VMEM((seq_count, tokens, D), BF),
+            pltpu.VMEM((D, 8 * DH), BF),
+            pltpu.VMEM((D, tokens), BF),
+            pltpu.SemaphoreType.DMA((3,)),
+            pltpu.SemaphoreType.DMA((seq_count,)),
+            pltpu.SemaphoreType.DMA((11,)),
+            pltpu.SemaphoreType.DMA((11,)),
+            pltpu.SemaphoreType.DMA((8,)),
+            pltpu.SemaphoreType.DMA((8,)),
+        ],
+        compiler_params=pltpu.CompilerParams(
+            vmem_limit_bytes=VMEM_BYTES, collective_id=0, has_side_effects=True
+        ),
+        name="gather",
+    )(x, og, w_attn, w_gate, w_out)
+    return x_g.reshape(pos, D), pre, mg, wt
+
+
+def stats_kernel(st_ref, all_ref, buf_s, send_sem, recv_sem):
+    me = lax.axis_index("seq")
+    barrier = pltpu.get_barrier_semaphore()
+    for step in range(1, 8):
+        pl.semaphore_signal(barrier, inc=1, device_id={"seq": lax.rem(me + step, 8)}, device_id_type=MESH)
+    pl.semaphore_wait(barrier, 7)
+    copies = []
+    for step in range(1, 8):
+        copy = pltpu.make_async_remote_copy(
+            src_ref=st_ref, dst_ref=buf_s.at[me], send_sem=send_sem.at[step], recv_sem=recv_sem.at[step],
+            device_id={"seq": lax.rem(me + step, 8)}, device_id_type=MESH,
+        )
+        copy.start()
+        copies.append(copy)
+    buf_s[me] = st_ref[...]
+    for copy in copies:
+        copy.wait()
+    all_ref[...] = buf_s[...]
+
+
+def share_stats(stats, seq_count):
+    shape = (seq_count,) + stats.shape
+    return pl.pallas_call(
+        stats_kernel,
+        out_shape=jax.ShapeDtypeStruct(shape, F32),
+        in_specs=vmem(1),
+        out_specs=vmem(1)[0],
+        scratch_shapes=[
+            pltpu.VMEM(shape, F32),
+            pltpu.SemaphoreType.DMA((8,)),
+            pltpu.SemaphoreType.DMA((8,)),
+        ],
+        compiler_params=pltpu.CompilerParams(collective_id=1, has_side_effects=True),
+        name="share_stats",
+    )(stats)
+
+
+def reduce_kernel(
+    tokens, dp_count, capacity,
+    ig_hbm, gw_hbm, go_hbm, og_ref, owner_col_ref, owner_row_ref, row_ref,
+    gsum_ref, gosum_ref, send_ref,
+    own_s, pair_s, sum_s, far_s, ring_s, gw_s, col_s, go_s,
+    load_sem, pair_send, pair_recv, ring_send, ring_recv, gw_send, gw_recv, col_send, col_recv, go_send, go_recv,
+):
+    me, sib, right, left, far, c = seq_peers()
+    z = me // 2
+    dp = lax.axis_index("dp")
+    half = tokens // 2
+    block = D // dp_count
+
+    loads = []
+    for k in (2, 1, 3, 0):
+        load = pltpu.make_async_copy(ig_hbm.at[lax.rem(z + k, 4) * 2 + c], own_s.at[k], load_sem.at[k])
+        load.start()
+        loads.append(load)
+    own_col = pltpu.make_async_copy(go_hbm.at[:, pl.ds(pl.multiple_of(me * 2 * DH, 2 * DH), 2 * DH)], col_s.at[me], load_sem.at[4])
+    own_col.start()
+    own_gw = pltpu.make_async_copy(gw_hbm.at[pl.ds(pl.multiple_of(dp * block, block), block)], gw_s.at[dp], load_sem.at[5])
+    own_gw.start()
+
+    barrier = pltpu.get_barrier_semaphore()
+    for step in range(1, 8):
+        pl.semaphore_signal(barrier, inc=1, device_id={"seq": lax.rem(me + step, 8)}, device_id_type=MESH)
+    for step in range(1, dp_count):
+        pl.semaphore_signal(barrier, inc=1, device_id={"dp": lax.rem(dp + step, dp_count)}, device_id_type=MESH)
+    pl.semaphore_wait(barrier, 7 + dp_count - 1)
+
+    def remote(src, dst, send_sem, recv_sem, to):
+        copy = pltpu.make_async_remote_copy(
+            src_ref=src, dst_ref=dst, send_sem=send_sem, recv_sem=recv_sem, device_id=to, device_id_type=MESH
+        )
+        copy.start()
+        return copy
+
+    pairs = {}
+    for k in (2, 1, 3, 0):
+        pairs[k] = remote(
+            ig_hbm.at[lax.rem(z + k, 4) * 2 + 1 - c], pair_s.at[k], pair_send.at[k], pair_recv.at[k], {"seq": sib}
+        )
+    cols = []
+    for step in range(1, 8):
+        to = lax.rem(me + step, 8)
+        cols.append(remote(
+            go_hbm.at[:, pl.ds(pl.multiple_of(to * 2 * DH, 2 * DH), 2 * DH)], col_s.at[me],
+            col_send.at[step], col_recv.at[step], {"seq": to},
+        ))
+    blocks = []
+    for step in range(1, dp_count):
+        to = lax.rem(dp + step, dp_count)
+        blocks.append(remote(
+            gw_hbm.at[pl.ds(pl.multiple_of(to * block, block), block)], gw_s.at[dp],
+            gw_send.at[step], gw_recv.at[step], {"dp": to},
+        ))
+
+    def pair_sum(k):
+        loads[(2, 1, 3, 0).index(k)].wait()
+        pairs[k].wait_recv()
+        return own_s[k].astype(F32) + pair_s[k].astype(F32)
+
+    low, high = pl.ds(0, half), pl.ds(half, half)
+    sum_s[2] = pair_sum(2).astype(BF)
+    far_r = remote(sum_s.at[2, low], far_s.at[0], ring_send.at[0], ring_recv.at[0], {"seq": right})
+    far_l = remote(sum_s.at[2, high], far_s.at[1], ring_send.at[1], ring_recv.at[1], {"seq": left})
+    sum_s[1] = pair_sum(1).astype(BF)
+    near_r = remote(sum_s.at[1, high], ring_s.at[0, high], ring_send.at[2], ring_recv.at[2], {"seq": right})
+    sum_s[3] = pair_sum(3).astype(BF)
+    near_l = remote(sum_s.at[3, low], ring_s.at[1, low], ring_send.at[3], ring_recv.at[3], {"seq": left})
+
+    own_col.wait()
+    for copy in cols:
+        copy.wait_recv()
+    gos = []
+    for step in range(1, dp_count):
+        to = lax.rem(dp + step, dp_count)
+        gos.append(remote(
+            col_s.at[to // 2, pl.ds(pl.multiple_of(lax.rem(to, 2) * block, block), block)], go_s.at[dp],
+            go_send.at[step], go_recv.at[step], {"dp": to},
+        ))
+    go_s[dp] = col_s[dp // 2, pl.ds(pl.multiple_of(lax.rem(dp, 2) * block, block), block), :]
+
+    far_r.wait_recv()
+    sum_s[0, low] = (sum_s[1, low].astype(F32) + far_s[0].astype(F32)).astype(BF)
+    end_r = remote(sum_s.at[0, low], ring_s.at[0, low], ring_send.at[4], ring_recv.at[4], {"seq": right})
+    far_l.wait_recv()
+    sum_s[0, high] = (sum_s[3, high].astype(F32) + far_s[1].astype(F32)).astype(BF)
+    end_l = remote(sum_s.at[0, high], ring_s.at[1, high], ring_send.at[5], ring_recv.at[5], {"seq": left})
+
+    mine = pair_sum(0) + og_ref[...].astype(F32)
+    earlier = (lax.broadcasted_iota(jnp.int32, (tokens, tokens), 0) < lax.broadcasted_iota(jnp.int32, (tokens, tokens), 1))
+    same = owner_col_ref[...] == owner_row_ref[...]
+    rank = jnp.sum(jnp.where(earlier & same, 1.0, 0.0), axis=0, keepdims=True).astype(jnp.int32)
+    slot = owner_row_ref[...] * capacity + rank
+    total = send_ref.shape[0]
+    hit = lax.broadcasted_iota(jnp.int32, (total, tokens), 0) == slot
+    ident = jnp.sum(jnp.where(hit, (row_ref[...] + 1).astype(F32), 0.0), axis=1, keepdims=True).astype(jnp.int32)
+    lanes = lax.broadcasted_iota(jnp.int32, (total, 128), 1)
+    code = jnp.where(lanes == 0, ident // 32, jnp.where(lanes == 1, ident % 32, 0))
+    send_ref[:, D:] = code.astype(F32).astype(BF)
+    place = jnp.where(hit, 1.0, 0.0).astype(BF)
+
+    for copy in blocks:
+        copy.wait_recv()
+    own_gw.wait()
+    acc = gw_s[0].astype(F32)
+    for d in range(1, dp_count):
+        acc = acc + gw_s[d].astype(F32)
+    gsum_ref[...] = acc
+    for copy in gos:
+        copy.wait_recv()
+    acc = go_s[0].astype(F32)
+    for d in range(1, dp_count):
+        acc = acc + go_s[d].astype(F32)
+    gosum_ref[...] = acc
+
+    near_r.wait_recv()
+    near_l.wait_recv()
+    end_r.wait_recv()
+    end_l.wait_recv()
+    total_grad = (mine + ring_s[0].astype(F32) + ring_s[1].astype(F32)).astype(BF)
+    send_ref[:, :D] = mm(place, total_grad).astype(BF)
+
+    for copy in list(pairs.values()) + cols + blocks + gos + [far_r, far_l, near_r, near_l, end_r, end_l]:
+        copy.wait_send()
+
+
+def reduce_all(ig, gw, go, og, item_owner, item_row, dp_count, capacity, devices):
+    seq_count, tokens = ig.shape[0], ig.shape[1]
+    hbm = pl.BlockSpec(memory_space=pl.ANY)
+    block = D // dp_count
+    shard = lambda n: pltpu.VMEM((n, tokens, D), BF)
+    dma = lambda n: pltpu.SemaphoreType.DMA((n,))
+    return pl.pallas_call(
+        functools.partial(reduce_kernel, tokens, dp_count, capacity),
+        out_shape=(
+            jax.ShapeDtypeStruct((block, 8 * DH), F32),
+            jax.ShapeDtypeStruct((block, 2 * DH), F32),
+            jax.ShapeDtypeStruct((devices * capacity, D + 128), BF),
+        ),
+        in_specs=[hbm] * 3 + vmem(4),
+        out_specs=tuple(vmem(3)),
+        scratch_shapes=[
+            shard(4), shard(4), shard(4),
+            pltpu.VMEM((2, tokens // 2, D), BF),
+            shard(2),
+            pltpu.VMEM((dp_count, block, 8 * DH), BF),
+            pltpu.VMEM((seq_count, 2 * DH, 2 * DH), BF),
+            pltpu.VMEM((dp_count, block, 2 * DH), BF),
+            dma(6), dma(4), dma(4), dma(6), dma(6), dma(dp_count), dma(dp_count),
+            dma(seq_count), dma(seq_count), dma(dp_count), dma(dp_count),
+        ],
+        compiler_params=pltpu.CompilerParams(vmem_limit_bytes=VMEM_BYTES, collective_id=2, has_side_effects=True),
+        name="reduce_all",
+    )(ig, gw, go, og, item_owner, item_owner.reshape(1, tokens), item_row.reshape(1, tokens))
+
+
 def body(
     layer_input,
     out_grad,
@@ -277,46 +619,27 @@
     seq_count = lax.axis_size("seq")
     dp_count = lax.axis_size("dp")
     devices = seq_count * dp_count
-    me = lax.axis_index("seq")
     tokens_dev = layer_input.shape[0]
     pos = tokens_dev * seq_count
     maxlen = 2 * pos // 3
-    wt = jnp.concatenate(
-        [
-            lax.dynamic_slice_in_dim(w_attn, me * 6 * DH, 6 * DH, 1).T,
-            lax.dynamic_slice_in_dim(w_gate, me * 2 * DH, 2 * DH, 1).T,
-        ],
-        axis=0,
+    capacity = max(2, 2 * tokens_dev // devices)
+    lens = lengths[0]
+    x_g, pre, mg, wt = gather(layer_input, out_grad, w_attn, w_gate, w_out, tokens_dev, seq_count)
+    og_late, mg = lax.optimization_barrier((out_grad, mg))
+    og_g = lax.all_gather(og_late, "seq", axis=0, tiled=True)
+    h, stats = forward(lens, pre, mg, pos, maxlen)
+    stats = share_stats(stats, seq_count)
+    ig, gw, go = backward(lens, stats, pre, h, mg, wt, x_g, og_g, pos, maxlen, seq_count)
+    gw, go, send_rows = reduce_all(
+        ig.reshape(seq_count, tokens_dev, D), gw, go, out_grad, item_owner, item_row, dp_count, capacity, devices
     )
-    wo = lax.dynamic_slice_in_dim(w_out, me * 2 * DH, 2 * DH, 0)
-    lens = lengths[0]
-    x_g = lax.all_gather(layer_input, "seq", axis=0, tiled=True)
-    og_g = lax.all_gather(out_grad, "seq", axis=0, tiled=True)
-    pre, h, mg, stats = forward(lens, x_g, og_g, wt, wo, pos, maxlen)
-    stats = lax.all_gather(stats, "seq", axis=0, tiled=True)
-    ig, gw, go = backward(lens, stats, pre, h, mg, wt, x_g, og_g, pos, maxlen, seq_count)
-    ig = lax.all_to_all(ig.reshape(seq_count, tokens_dev, D), "seq", 0, 0, tiled=True)
-    input_grad = jnp.sum(ig.astype(F32), axis=0) + out_grad.astype(F32)
-    gw = lax.all_to_all(gw.reshape(dp_count, D // dp_count, 8 * DH), "dp", 0, 0, tiled=True)
-    gw = jnp.sum(gw.astype(F32), axis=0)
-    go = lax.all_to_all(go, "seq", 1, 0, tiled=True)
-    go = lax.all_to_all(go.reshape(dp_count, D // dp_count, 2 * DH), "dp", 0, 0, tiled=True)
-    go = jnp.sum(go.astype(F32), axis=0)
-
+    got = lax.all_to_all(send_rows.reshape(devices, capacity, D + 128), ("seq", "dp"), 0, 0, tiled=True)
+    total = devices * capacity
+    got = got.reshape(total, D + 128)
+    got_ids = (got[:, D].astype(F32) * 32.0 + got[:, D + 1].astype(F32)).astype(jnp.int32) - 1
     rows_own = emb_table.shape[0]
-    capacity = max(2, 2 * tokens_dev // devices)
-    owners = item_owner[:, 0]
-    hits = (owners[:, None] == jnp.arange(devices, dtype=jnp.int32)[None, :]).astype(jnp.int32)
-    slots = jnp.sum((jnp.cumsum(hits, axis=0) - hits) * hits, axis=1)
-    flat_slot = owners * capacity + slots
-    total = devices * capacity
-    place = (jnp.arange(total, dtype=jnp.int32)[:, None] == flat_slot[None, :])
-    send_rows = mm(place.astype(BF), input_grad.astype(BF)).astype(BF)
-    send_ids = jnp.sum(jnp.where(place, item_row[None, :] + 1, 0), axis=1) - 1
-    got_rows = lax.all_to_all(send_rows.reshape(devices, capacity, D), ("seq", "dp"), 0, 0, tiled=True)
-    got_ids = lax.all_to_all(send_ids.reshape(devices, capacity), ("seq", "dp"), 0, 0, tiled=True)
-    pick = (jnp.arange(rows_own, dtype=jnp.int32)[:, None] == got_ids.reshape(1, total)).astype(BF)
-    table_grad = mm(pick, got_rows.reshape(total, D))
+    pick = (jnp.arange(rows_own, dtype=jnp.int32)[:, None] == got_ids[None, :]).astype(BF)
+    table_grad = mm(pick, got[:, :D])
     new_accum = row_accum + jnp.mean(table_grad * table_grad, axis=1)
     new_table = emb_table - LEARN_RATE * table_grad * lax.rsqrt(new_accum)[:, None]
     return (gw[:, : 6 * DH], gw[:, 6 * DH :], go, new_table, new_accum)

time: 291 us -> 183 us (0.63)
  blocking collectives: 97.7 us -> 0 us
  Pallas kernels: 54.7 us -> 128 us
  waiting for transfers between devices: 76.9 us -> 24.5 us
  starting transfers between devices: 20.2 us -> 6.79 us
  other arithmetic: 13 us -> 2.19 us
  local copies, waits for them, and re-layouts: 11.1 us -> 6.59 us
    all_to_all x3 -> x0, blocking collectives: 83.3 us -> none  [the longest x1 54.8 us: body(): lax.all_to_all(ig.reshape(seq_count, tokens_dev, D), 'seq', 0, 0, tiled=T...]
    pallas_call x0 -> x3, Pallas kernels: none -> 79.8 us  [the longest x1 36.3 us: gather(): pl.pallas_call(functools.partial(gather_kernel, tokens), out_shape=(jax.S...]
    all_gather x2 -> x1, waiting for transfers between devices: 48.6 us -> 5.33 us  [body(): og_g = lax.all_gather(og_late, 'seq', axis=0, tiled=True)]
    all_gather x1 -> x0, blocking collectives: 14.4 us -> none  [body(): stats = lax.all_gather(stats, 'seq', axis=0, tiled=True)]
    all_to_all x3 -> x1, starting transfers between devices: 20.1 us -> 6.76 us  [body(): lax.all_to_all(send_rows.reshape(devices, capacity, D + 128), ('seq', 'dp...]
    all_to_all x3 -> x1, waiting for transfers between devices: 26.9 us -> 19.1 us  [body(): lax.all_to_all(send_rows.reshape(devices, capacity, D + 128), ('seq', 'dp...]
    pallas_call x1, Pallas kernels: 25.1 us -> 18.7 us  [forward(): pl.pallas_call(functools.partial(fwd_kernel, pos, maxlen), out_shape=(jax...]
    reduce_sum x5 -> x0, other arithmetic: 6.25 us -> none  [the longest x1 3.2 us: body(): input_grad = jnp.sum(ig.astype(F32), axis=0) + out_grad.astype(F32)]
  transfers between devices with their start and end apart: 5 -> 2, of which waited for: 4 -> 2; matrix products, arithmetic and copies ran while one was open for 7% -> 1% of each run, Pallas kernels for 19% -> 16%
where the time goes in v1:
time: 183 us
  Pallas kernels  128 us (70%)
  waiting for transfers between devices  24.5 us (13%)
  between operations  14.1 us (8%)
  starting transfers between devices  6.79 us (4%)
  local copies, waits for them, and re-layouts  6.59 us (4%)
  other arithmetic  2.19 us (1%)
    pallas_call x1, Pallas kernels, gather(): pl.pallas_call(functools.partial(gather_kernel, tokens), out_shape=(jax.S...  36.3 us
    pallas_call x1, Pallas kernels, reduce_all(): pl.pallas_call(functools.partial(reduce_kernel, tokens, dp_count, capacit...  32.5 us
    pallas_call x1, Pallas kernels, backward(): pl.pallas_call(functools.partial(bwd_kernel, pos, maxlen, seq_count), out...  29.3 us
    all_to_all x1, waiting for transfers between devices, body(): lax.all_to_all(send_rows.reshape(devices, capacity, D + 128), ('seq', 'dp...  19.1 us
    pallas_call x1, Pallas kernels, forward(): pl.pallas_call(functools.partial(fwd_kernel, pos, maxlen), out_shape=(jax...  18.7 us
    pallas_call x1, Pallas kernels, share_stats(): pl.pallas_call(stats_kernel, out_shape=jax.ShapeDtypeStruct(shape, F32),...  11 us
    all_to_all x1, starting transfers between devices, body(): lax.all_to_all(send_rows.reshape(devices, capacity, D + 128), ('seq', 'dp...  6.76 us
    all_gather x1, waiting for transfers between devices, body(): og_g = lax.all_gather(og_late, 'seq', axis=0, tiled=True)  5.33 us
  transfers between devices with their start and end apart: 2, of which 2 were waited for; matrix products, arithmetic and copies ran while one was open for 1% of the time, Pallas kernels for 16%

profile of v1, /device:TPU:0, one launch (start us, length us, event | category | flops | bytes accessed | tf_op | source)
XLA Modules:
  0.0 182.8 jit_solution(13016934806999099468)
XLA Ops:
  7.2 0.0 all-gather.2.cloned.1.call-start
  7.2 36.3 %gather.1 = (bf16[8,256,1024]{2,1,0:T(8,128)(2,1)}, f32[512,2048]{1,0:T(8,128)}, bf16[128,2048]{1,0:T(8,128)(2,1)}, bf16[512,1024]{1,0:T(8,128)(2,1)}) custom-call(bf16[256,1024]{1,0:T(8,128)(2,1)} %x_ref.1, bf16[256,1024]{1,0:T(8,128)(2,1)} %og_ref.3, bf16[1024,3072]{1,0:T(8,128)(2,1)} %wa_hbm.1, bf16[1024,1024]{1,0:T(8,128)(2,1)} %wg_hbm.1, ...), custom_call_target="tpu_custom_call" | custom-call | tf_op jit(solution)/shard_map/gather/pallas_call | solution.py:383
  43.6 0.0 all-gather.2.cloned.1.call-update
  43.6 0.0 copy-start.3
  43.6 18.7 %forward.1 = (bf16[128,2048]{1,0:T(8,128)(2,1)}, f32[8,1024]{1,0:T(8,128)}) custom-call(s32[3]{0:T(128)} %bitcast.9, f32[512,2048]{1,0:T(8,128)} %get-tuple-element.19.pre_ref, bf16[128,2048]{1,0:T(8,128)(2,1)} %get-tuple-element.21.mg_ref), custom_call_target="tpu_custom_call" | custom-call | tf_op jit(solution)/shard_map/forward/pallas_call | solution.py:220
  62.3 11.0 %share_stats.1.sta_ref = f32[8,8,1024]{2,1,0:T(8,128)} custom-call(f32[8,1024]{1,0:T(8,128)} %get-tuple-element.22.st_ref), custom_call_target="tpu_custom_call" | custom-call | tf_op jit(solution)/shard_map/share_stats/pallas_call | solution.py:434
  73.3 0.0 copy-done.3
  73.3 0.8 copy.19.owner_col_ref
  74.1 5.3 %all-gather.2.cloned.1.call-done.og_hbm = bf16[2048,1024]{1,0:T(8,128)(2,1)} async-done(((bf16[256,1024]{1,0:T(8,128)(2,1)}), bf16[2048,1024]{1,0:T(8,128)(2,1)}) %all-gather.2.cloned.1.call-update) | async-done | bytes 4194320 | tf_op jit(solution)/shard_map/all_gather | solution.py:629
  79.5 29.3 %backward.1 = (bf16[2048,1024]{1,0:T(8,128)(2,1)}, bf16[1024,512]{1,0:T(8,128)(2,1)}, bf16[128,1024]{1,0:T(8,128)(2,1)}) custom-call(s32[3]{0:T(128)} %bitcast.10, f32[8,8,1024]{2,1,0:T(8,128)} %share_stats.1.sta_ref, f32[512,2048]{1,0:T(8,128)} %get-tuple-element.19.pre_ref, bf16[128,2048]{1,0:T(8,128)(2,1)} %get-tuple-element.23.h_ref, ...), custom_call_target="tpu_custom_call" | custom-call | tf_op jit(solution)/shard_map/backward/pallas_call | solution.py:242
  108.8 32.5 %reduce_all.1 = (f32[64,512]{1,0:T(8,128)}, f32[64,128]{1,0:T(8,128)}, bf16[512,1152]{1,0:T(8,128)(2,1)}) custom-call(bf16[8,256,1024]{2,1,0:T(8,128)(2,1)} %bitcast.7, bf16[1024,512]{1,0:T(8,128)(2,1)} %get-tuple-element.28.gw_hbm, bf16[128,1024]{1,0:T(8,128)(2,1)} %get-tuple-element.29.go_hbm, bf16[256,1024]{1,0:T(8,128)(2,1)} %og_ref.3, ...), custom_call_target="tpu_custom_call" | custom-call | tf_op jit(solution)/shard_map/reduce_all/pallas_call | solution.py:583
  141.3 0.0 copy-start.1
  141.3 3.3 %reshape.53 = bf16[128,4,1152]{2,1,0:T(4,128)(2,1)} reshape(bf16[512,1152]{1,0:T(8,128)(2,1)} %get-tuple-element.32) | data formatting | bytes 2359296 | tf_op jit(solution)/shard_map/reshape | solution.py:636
  144.5 6.8 %all-to-all-start = ((bf16[128,4,1152]{2,1,0:T(4,128)(2,1)}), bf16[128,4,1152]{2,1,0:T(4,128)(2,1)S(1)}, u32[]{:S(2)}, u32[]{:S(2)}) async-start(bf16[128,4,1152]{2,1,0:T(4,128)(2,1)} %reshape.53), calls=%async_computation | async-start | bytes 2359296 | tf_op jit(solution)/shard_map/all_to_all | solution.py:636
  151.3 0.0 copy-done.1
  151.3 0.6 slice.15
  152.0 0.6 slice.16
  152.6 19.1 %all-to-all-done = bf16[128,4,1152]{2,1,0:T(4,128)(2,1)S(1)} async-done(((bf16[128,4,1152]{2,1,0:T(4,128)(2,1)}), bf16[128,4,1152]{2,1,0:T(4,128)(2,1)S(1)}, u32[]{:S(2)}, u32[]{:S(2)}) %all-to-all-start) | async-done | bytes 1179680 | tf_op jit(solution)/shard_map/all_to_all | solution.py:636
  171.7 0.3 reshape.54
  172.0 0.1 fusion.3
  172.1 0.0 copy-start.4
  172.1 0.0 copy-start
  172.1 0.1 copy.22
  172.3 0.1 copy.23
  172.4 0.8 multiply_reduce_fusion
  173.2 0.0 copy-done.4
  173.2 0.6 rsqrt_multiply_fusion
  173.8 0.0 copy-done
  173.8 0.0 copy-start.2
  173.8 1.6 multiply_subtract_fusion
  175.4 0.0 copy-done.2
  175.4 0.6 copy.25
  (1 shorter events, 0.0 us)
Async XLA Ops:
  7.2 72.3 %all-gather.2.cloned.1.call-start = ((), (), s32[]{:S(2)}) async-start(), calls=%async_computation.1 | async-start | bytes 4718592 | tf_op jit(solution)/shard_map/all_gather | solution.py:629
  43.6 29.8 %copy-start.3 = (s32[256,1]{0,1:T(1,128)S(1)}, s32[256,1]{0,1:T(1,128)}, u32[]{:S(2)}) copy-start(s32[256,1]{0,1:T(1,128)} %param.13) | copy-start | bytes 3076
  141.3 10.0 %copy-start.1 = (f32[64,512]{1,0:T(8,128)S(1)}, f32[64,512]{1,0:T(8,128)}, u32[]{:S(2)}) copy-start(f32[64,512]{1,0:T(8,128)} %get-tuple-element.30) | copy-start | bytes 393220
  144.5 27.2 %all-to-all-start = ((bf16[128,4,1152]{2,1,0:T(4,128)(2,1)}), bf16[128,4,1152]{2,1,0:T(4,128)(2,1)S(1)}, u32[]{:S(2)}, u32[]{:S(2)}) async-start(bf16[128,4,1152]{2,1,0:T(4,128)(2,1)} %reshape.53), calls=%async_computation | async-start | bytes 2359296 | tf_op jit(solution)/shard_map/all_to_all | solution.py:636
  172.1 1.1 copy-start.4
  172.1 1.7 copy-start
  173.8 1.6 copy-start.2
Sparse Core Ops, SparseCore 0:
  43.7 35.7 all-gather.1

commit v2 on v1

v2 whole, which is shorter than its diff:
```python
import functools

import jax
import jax.numpy as jnp
from jax import lax
from jax.experimental import pallas as pl
from jax.experimental.pallas import tpu as pltpu
from jax.sharding import PartitionSpec as P

D = 1024
H = 16
DH = 64
NORM_EPS = 1e-05
LEARN_RATE = 0.1
TQ = 512
TK = 512
VMEM_BYTES = 56 * 1024 * 1024

BF = jnp.bfloat16
F32 = jnp.float32
NN = (((1,), (0,)), ((), ()))
NT = (((1,), (1,)), ((), ()))
MESH = pl.DeviceIdType.MESH


def mm(a, b, dims=NN):
    return lax.dot_general(a, b, dims, preferred_element_type=F32)


def silu(z):
    t = 0.5 * z
    return t + t * jnp.tanh(t)


def silu_grad(z):
    t = 0.5 * z
    th = jnp.tanh(t)
    return 0.5 * ((1.0 + th) * (1.0 + t * (1.0 - th)))


def event_starts(len_ref, places):
    end0 = len_ref[0]
    end1 = end0 + len_ref[1]
    return jnp.where(places >= end1, end1, jnp.where(places >= end0, end0, 0))


def scalar_start(len_ref, place):
    end0 = len_ref[0]
    end1 = end0 + len_ref[1]
    return jnp.where(place >= end1, end1, jnp.where(place >= end0, end0, 0))


def tile_allowed(len_ref, j, i):
    keys = j * TK + lax.broadcasted_iota(jnp.int32, (TK, TQ), 0)
    places = i * TQ + lax.broadcasted_iota(jnp.int32, (1, TQ), 1)
    return (keys >= event_starts(len_ref, places)) & (keys <= places)


def stat_place(pos, chunk, c):
    first = c * chunk
    row = 4 * (first // (pos // 2))
    lane = first % (pos // 2)
    return row, slice(lane, lane + chunk)


def bwd_kernel(
    pos, maxlen, seq_count,
    len_ref, sta_ref, h_ref, gate_ref, gsg_ref, mg_ref, q_ref, kt_ref, k_ref, v_ref, sg_hbm,
    g_ref, mix_ref,
    sg_s, sem, ot_s, dv_s, dk_s,
):
    sg_copy = pltpu.make_async_copy(sg_hbm, sg_s, sem)
    sg_copy.start()
    chunk = 512
    for c in range(pos // chunk):
        at = slice(c * chunk, (c + 1) * chunk)
        row, lane = stat_place(pos, chunk, c)
        means = [sta_ref[d, row : row + 1, lane] for d in range(seq_count)]
        mean = functools.reduce(jnp.add, means) * (1.0 / seq_count)
        var = jnp.zeros_like(mean)
        ng_mean = jnp.zeros_like(mean)
        ng_cov = jnp.zeros_like(mean)
        for d in range(seq_count):
            off = means[d] - mean
            ng_sum = sta_ref[d, row + 2 : row + 3, lane]
            var = var + sta_ref[d, row + 1 : row + 2, lane] + (2 * DH) * off * off
            ng_mean = ng_mean + ng_sum
            ng_cov = ng_cov + sta_ref[d, row + 3 : row + 4, lane] + off * ng_sum
        inv = lax.rsqrt(var * (1.0 / D) + NORM_EPS)
        ng_mean = ng_mean * (1.0 / D)
        proj = inv * ng_cov * (1.0 / D)
        gate = gate_ref[:, at]
        normed = (h_ref[:, at].astype(F32) - mean) * inv
        mix_ref[:, at] = (normed * gate).astype(BF)
        mg = mg_ref[:, at].astype(F32)
        g_ref[6 * DH :, at] = (mg * normed * gsg_ref[:, at]).astype(BF)
        hg = (inv * (mg * gate - ng_mean - normed * proj)).astype(BF)
        for hd in range(2):
            ot_s[hd, :, at] = hg[hd * DH : (hd + 1) * DH]
    dv_s[...] = jnp.zeros_like(dv_s)
    dk_s[...] = jnp.zeros_like(dk_s)
    fac = 0.0625 / maxlen

    @pl.loop(0, pos // TQ)
    def _(i):
        at = pl.ds(pl.multiple_of(i * TQ, TQ), TQ)
        first = scalar_start(len_ref, i * TQ) // TK
        last = ((i + 1) * TQ - 1) // TK

        def step(j, accs):
            kat = pl.ds(pl.multiple_of(j * TK, TK), TK)
            allowed = tile_allowed(len_ref, j, i)
            outs = []
            for hd in range(2):
                t = mm(k_ref[hd, kat, :], q_ref[hd, :, at])
                dw = mm(v_ref[hd, kat, :], ot_s[hd, :, at])
                a = 1.0 + jnp.tanh(t)
                w = t * a
                ds = jnp.where(allowed, dw * (a + w * (2.0 - a)), 0.0).astype(BF)
                w = jnp.where(allowed, w, 0.0).astype(BF)
                dv_s[hd, :, kat] += mm(ot_s[hd, :, at], w, NT)
                dk_s[hd, :, kat] += mm(q_ref[hd, :, at], ds, NT)
                outs.append(accs[hd] + mm(kt_ref[hd, :, kat], ds))
            return tuple(outs)

        zero = jnp.zeros((DH, TQ), F32)
        accs = lax.fori_loop(first, last + 1, step, (zero, zero))
        for hd in range(2):
            base = hd * 3 * DH + DH
            g_ref[base : base + DH, at] = (accs[hd] * fac).astype(BF)

    sg_copy.wait()

    @pl.loop(0, pos // chunk)
    def _(c):
        at = pl.ds(pl.multiple_of(c * chunk, chunk), chunk)
        for hd in range(2):
            base = hd * 3 * DH
            dv = (dv_s[hd, :, at] * (1.0 / maxlen)).astype(BF)
            dk = (dk_s[hd, :, at] * (16.0 * fac)).astype(BF)
            dq = g_ref[base + DH : base + 2 * DH, at]
            for part, grad in enumerate((dv, dq, dk)):
                rows = slice(base + part * DH, base + (part + 1) * DH)
                g_ref[rows, at] = (grad.astype(F32) * sg_s[rows, at]).astype(BF)


def vmem(count):
    return [pl.BlockSpec(memory_space=pltpu.VMEM)] * count


def backward(lens, stats, h, acts, pos, maxlen, seq_count):
    heads = pltpu.VMEM((2, DH, pos), BF)
    sums = pltpu.VMEM((2, DH, pos), F32)
    return pl.pallas_call(
        functools.partial(bwd_kernel, pos, maxlen, seq_count),
        out_shape=(
            jax.ShapeDtypeStruct((8 * DH, pos), BF),
            jax.ShapeDtypeStruct((2 * DH, pos), BF),
        ),
        in_specs=[pl.BlockSpec(memory_space=pltpu.SMEM)] + vmem(9) + [pl.BlockSpec(memory_space=pl.ANY)],
        out_specs=tuple(vmem(2)),
        scratch_shapes=[
            pltpu.VMEM((6 * DH, pos), F32),
            pltpu.SemaphoreType.DMA,
            heads, sums, sums,
        ],
        compiler_params=pltpu.CompilerParams(vmem_limit_bytes=VMEM_BYTES),
        name="backward",
    )(
        lens, stats, h, acts["gate"], acts["gsg"], acts["mg"],
        acts["q"], acts["kt"], acts["k"], acts["v"], acts["sg"],
    )


def seq_peers():
    me = lax.axis_index("seq")
    z, c = me // 2, me % 2
    at = lambda step: lax.rem(z + step, 4) * 2
    return me, at(0) + 1 - c, at(1) + c, at(3) + c, at(2) + c, c


def block_step(m):
    return lax.rem(3 * m + 3 * (m // 2) + 2 * (m // 3), 4)


def gather_kernel(
    tokens, maxlen,
    len_ref, x_ref, og_ref, wa_hbm, wg_hbm, wo_hbm,
    xg_ref, w_out, q_out, kt_out, k_out, v_out, sg_out, gate_out, gsg_out, mg_ref, h_ref, sta_ref,
    w_s, q_s, kt_s, k_s, v_s, sg_s, gate_s, gsg_s,
    x_s, wt_s, wo_s, mine_s, vt_s, acc_s, st_s,
    load_sem, keep_sem, send_sem, recv_sem, mg_send, mg_recv, st_send, st_recv,
):
    me, sib, right, left, far, c = seq_peers()
    z = me // 2
    pos = 8 * tokens
    half = tokens // 2
    loads = [
        pltpu.make_async_copy(x_ref, x_s.at[me], load_sem.at[0]),
        pltpu.make_async_copy(wa_hbm.at[:, pl.ds(pl.multiple_of(me * 6 * DH, 128), 6 * DH)], w_s.at[:, : 6 * DH], load_sem.at[1]),
        pltpu.make_async_copy(wg_hbm.at[:, pl.ds(pl.multiple_of(me * 2 * DH, 128), 2 * DH)], w_s.at[:, 6 * DH :], load_sem.at[2]),
        pltpu.make_async_copy(wo_hbm, wo_s, load_sem.at[3]),
    ]
    for load in loads:
        load.start()

    barrier = pltpu.get_barrier_semaphore()
    for step in range(1, 8):
        pl.semaphore_signal(barrier, inc=1, device_id={"seq": lax.rem(me + step, 8)}, device_id_type=MESH)
    acc_s[...] = jnp.zeros_like(acc_s)
    loads[0].wait()
    pl.semaphore_wait(barrier, 7)

    def remote(src, dst, send_sem, recv_sem, to):
        copy = pltpu.make_async_remote_copy(
            src_ref=src, dst_ref=dst, send_sem=send_sem, recv_sem=recv_sem, device_id={"seq": to}, device_id_type=MESH
        )
        copy.start()
        return copy

    def send(index, shard, part, to):
        ref = x_s.at[shard] if part is None else x_s.at[shard, pl.ds(part * half, half)]
        return remote(ref, ref, send_sem.at[index], recv_sem.at[index], to)

    keeps = []

    def keep(src, dst):
        copy = pltpu.make_async_copy(src, dst, keep_sem.at[len(keeps)])
        copy.start()
        keeps.append(copy)

    def project(shard):
        at = pl.ds(pl.multiple_of(shard * tokens, tokens), tokens)
        keep(x_s.at[shard], xg_ref.at[shard])
        pre = mm(wt_s[...], x_s[shard], NT)
        attn = pre[: 6 * DH]
        act = silu(attn).astype(BF)
        sg_s[:, at] = silu_grad(attn)
        gate = pre[6 * DH :]
        gate_s[:, at] = silu(gate)
        gsg_s[:, at] = silu_grad(gate)
        act_n = silu(mm(x_s[shard], w_s[:, : 6 * DH]))
        for hd in range(2):
            base = hd * 3 * DH
            vt_s[hd, :, at] = act[base : base + DH]
            q_s[hd, :, at] = (act[base + DH : base + 2 * DH] * 0.0625).astype(BF)
            kt_s[hd, :, at] = act[base + 2 * DH : base + 3 * DH]
            v_s[hd, at, :] = act_n[:, base : base + DH].astype(BF)
            k_s[hd, at, :] = act_n[:, base + 2 * DH : base + 3 * DH].astype(BF)

    def attend(n):
        new = lax.rem(z + block_step(n), 4)

        def tile(m, carry):
            old = lax.rem(z + block_step(m), 4)
            later = (new - old + 4) // 4
            i = later * new + (1 - later) * old
            j = new + old - i
            at = pl.ds(pl.multiple_of(i * TQ, TQ), TQ)
            kat = pl.ds(pl.multiple_of(j * TK, TK), TK)
            allowed = tile_allowed(len_ref, j, i)
            for hd in range(2):
                t = mm(k_s[hd, kat, :], q_s[hd, :, at])
                w = jnp.where(allowed, t + t * jnp.tanh(t), 0.0).astype(BF)
                acc_s[hd, :, at] += mm(vt_s[hd, :, kat], w)
            return carry

        lax.fori_loop(0, n + 1, tile, 0)

    to_right = [send(0, me, 0, right), None]
    to_left = [None, send(1, me, 1, left)]
    to_right[1] = send(2, me, 1, right)
    to_left[0] = send(3, me, 0, left)
    to_sib = send(4, me, None, sib)

    loads[1].wait()
    loads[2].wait()
    wt_s[...] = w_s[...].T
    keep(w_s, w_out)
    project(me)
    loads[3].wait()
    mine_s[...] = mm(wo_s[...], og_ref[...], NT).astype(BF)
    mine = pl.ds(pl.multiple_of(me * tokens, tokens), tokens)
    mg_ref[:, mine] = mine_s[pl.ds(pl.multiple_of(me * 2 * DH, 2 * DH), 2 * DH), :]
    to_sib.wait_recv()
    project(sib)

    to_right[0].wait_recv()
    fwd_r = send(5, left, 0, right)
    to_left[1].wait_recv()
    fwd_l = send(6, right, 1, left)
    attend(0)
    to_right[1].wait_recv()
    sib_left = send(7, left, None, sib)
    to_left[0].wait_recv()
    sib_right = send(8, right, None, sib)
    mg_copies = []
    for step in range(1, 8):
        to = lax.rem(me + step, 8)
        mg_copies.append(remote(
            mine_s.at[pl.ds(pl.multiple_of(to * 2 * DH, 2 * DH), 2 * DH)], mg_ref.at[:, mine],
            mg_send.at[step], mg_recv.at[step], to,
        ))
    other = 1 - 2 * c
    project(left)
    sib_left.wait_recv()
    project(left + other)
    attend(1)
    project(right)
    sib_right.wait_recv()
    project(right + other)
    fwd_r.wait_recv()
    sib_far0 = send(9, far, 0, sib)
    fwd_l.wait_recv()
    sib_far1 = send(10, far, 1, sib)
    attend(2)
    project(far)
    sib_far0.wait_recv()
    sib_far1.wait_recv()
    project(far + other)
    for src, dst in (
        (q_s, q_out), (kt_s, kt_out), (k_s, k_out), (v_s, v_out), (sg_s, sg_out), (gate_s, gate_out), (gsg_s, gsg_out)
    ):
        keep(src, dst)
    attend(3)
    for copy in mg_copies:
        copy.wait_recv()

    chunk = 512
    for ch in range(pos // chunk):
        at = slice(ch * chunk, (ch + 1) * chunk)
        row, lane = stat_place(pos, chunk, ch)
        for hd in range(2):
            h_ref[hd * DH : (hd + 1) * DH, at] = (acc_s[hd, :, at] * (1.0 / maxlen)).astype(BF)
        h = h_ref[:, at].astype(F32)
        mean = jnp.sum(h, axis=0, keepdims=True) * (1.0 / (2 * DH))
        cen = h - mean
        ng = mg_ref[:, at].astype(F32) * gate_s[:, at]
        st_s[row : row + 1, lane] = mean
        st_s[row + 1 : row + 2, lane] = jnp.sum(cen * cen, axis=0, keepdims=True)
        st_s[row + 2 : row + 3, lane] = jnp.sum(ng, axis=0, keepdims=True)
        st_s[row + 3 : row + 4, lane] = jnp.sum(ng * cen, axis=0, keepdims=True)
    st_copies = []
    for step in range(1, 8):
        st_copies.append(remote(st_s, sta_ref.at[me], st_send.at[step], st_recv.at[step], lax.rem(me + step, 8)))
    sta_ref[me] = st_s[...]
    for copy in st_copies:
        copy.wait()

    for copy in mg_copies + to_right + to_left + [to_sib, fwd_r, fwd_l, sib_left, sib_right, sib_far0, sib_far1]:
        copy.wait_send()
    for copy in keeps:
        copy.wait()


def gather(lens, x, og, w_attn, w_gate, w_out, tokens, seq_count, maxlen):
    pos = tokens * seq_count
    hbm = pl.BlockSpec(memory_space=pl.ANY)
    kept = [
        ((D, 8 * DH), BF),
        ((2, DH, pos), BF),
        ((2, DH, pos), BF),
        ((2, pos, DH), BF),
        ((2, pos, DH), BF),
        ((6 * DH, pos), F32),
        ((2 * DH, pos), F32),
        ((2 * DH, pos), F32),
    ]
    names = ("x", "w", "q", "kt", "k", "v", "sg", "gate", "gsg", "mg", "h", "stats")
    dma = lambda n: pltpu.SemaphoreType.DMA((n,))
    outs = pl.pallas_call(
        functools.partial(gather_kernel, tokens, maxlen),
        out_shape=tuple(
            [jax.ShapeDtypeStruct((seq_count, tokens, D), BF)]
            + [jax.ShapeDtypeStruct(shape, dtype) for shape, dtype in kept]
            + [
                jax.ShapeDtypeStruct((2 * DH, pos), BF),
                jax.ShapeDtypeStruct((2 * DH, pos), BF),
                jax.ShapeDtypeStruct((seq_count, 8, pos // 2), F32),
            ]
        ),
        in_specs=[pl.BlockSpec(memory_space=pltpu.SMEM), hbm] + vmem(1) + [hbm] * 3,
        out_specs=tuple([hbm] * 9 + vmem(3)),
        scratch_shapes=[pltpu.VMEM(shape, dtype) for shape, dtype in kept]
        + [
            pltpu.VMEM((seq_count, tokens, D), BF),
            pltpu.VMEM((8 * DH, D), BF),
            pltpu.VMEM((D, D), BF),
            pltpu.VMEM((D, tokens), BF),
            pltpu.VMEM((2, DH, pos), BF),
            pltpu.VMEM((2, DH, pos), F32),
            pltpu.VMEM((8, pos // 2), F32),
            dma(4), dma(16), dma(11), dma(11), dma(8), dma(8), dma(8), dma(8),
        ],
        compiler_params=pltpu.CompilerParams(
            vmem_limit_bytes=VMEM_BYTES, collective_id=0, has_side_effects=True
        ),
        name="gather",
    )(lens, x, og, w_attn, w_gate, w_out)
    return dict(zip(names, outs))


def reduce_kernel(
    tokens, dp_count, capacity,
    g_ref, w_ref, mix_ref, x_hbm, og_hbm, og_ref, owner_col_ref, owner_row_ref, row_ref,
    gsum_ref, gosum_ref, send_ref,
    x_s, og_s, out_s, pair_s, sum_s, far_s, ring_s, gsrc_s, gw_s, gosrc_s, col_s, go_s,
    load_sem, pair_send, pair_recv, ring_send, ring_recv, gw_send, gw_recv, col_send, col_recv, go_send, go_recv,
):
    me, sib, right, left, far, c = seq_peers()
    z = me // 2
    dp = lax.axis_index("dp")
    half = D // 2
    block = D // dp_count

    x_load = pltpu.make_async_copy(x_hbm, x_s, load_sem.at[0])
    og_load = pltpu.make_async_copy(og_hbm, og_s, load_sem.at[1])
    og_load.start()
    x_load.start()

    barrier = pltpu.get_barrier_semaphore()
    for step in range(1, 8):
        pl.semaphore_signal(barrier, inc=1, device_id={"seq": lax.rem(me + step, 8)}, device_id_type=MESH)
    for step in range(1, dp_count):
        pl.semaphore_signal(barrier, inc=1, device_id={"dp": lax.rem(dp + step, dp_count)}, device_id_type=MESH)
    pl.semaphore_wait(barrier, 7 + dp_count - 1)

    def remote(src, dst, send_sem, recv_sem, to):
        copy = pltpu.make_async_remote_copy(
            src_ref=src, dst_ref=dst, send_sem=send_sem, recv_sem=recv_sem, device_id=to, device_id_type=MESH
        )
        copy.start()
        return copy

    def partial_grad(shard):
        return mm(w_ref[...], g_ref[:, pl.ds(pl.multiple_of(shard * tokens, tokens), tokens)])

    pairs = {}
    for k in (2, 1, 3, 0):
        out_s[k] = partial_grad(lax.rem(z + k, 4) * 2 + 1 - c).astype(BF)
        pairs[k] = remote(out_s.at[k], pair_s.at[k], pair_send.at[k], pair_recv.at[k], {"seq": sib})

    def pair_sum(k):
        own = partial_grad(lax.rem(z + k, 4) * 2 + c)
        pairs[k].wait_recv()
        return own + pair_s[k].astype(F32)

    low, high = pl.ds(0, half), pl.ds(half, half)
    sum_s[2] = pair_sum(2).astype(BF)
    far_r = remote(sum_s.at[2, low], far_s.at[0], ring_send.at[0], ring_recv.at[0], {"seq": right})
    far_l = remote(sum_s.at[2, high], far_s.at[1], ring_send.at[1], ring_recv.at[1], {"seq": left})
    sum_s[1] = pair_sum(1).astype(BF)
    near_r = remote(sum_s.at[1, high], ring_s.at[0, high], ring_send.at[2], ring_recv.at[2], {"seq": right})
    sum_s[3] = pair_sum(3).astype(BF)
    near_l = remote(sum_s.at[3, low], ring_s.at[1, low], ring_send.at[3], ring_recv.at[3], {"seq": left})

    og_load.wait()
    gosrc_s[...] = mm(mix_ref[...], og_s[...]).astype(BF)
    cols = []
    for step in range(1, 8):
        to = lax.rem(me + step, 8)
        cols.append(remote(
            gosrc_s.at[:, pl.ds(pl.multiple_of(to * 2 * DH, 2 * DH), 2 * DH)], col_s.at[me],
            col_send.at[step], col_recv.at[step], {"seq": to},
        ))
    col_s[me] = gosrc_s[:, pl.ds(pl.multiple_of(me * 2 * DH, 2 * DH), 2 * DH)]
    x_load.wait()
    gsrc_s[...] = mm(g_ref[...], x_s[...]).astype(BF).T
    blocks = []
    for step in range(1, dp_count):
        to = lax.rem(dp + step, dp_count)
        blocks.append(remote(
            gsrc_s.at[pl.ds(pl.multiple_of(to * block, block), block)], gw_s.at[dp],
            gw_send.at[step], gw_recv.at[step], {"dp": to},
        ))
    gw_s[dp] = gsrc_s[pl.ds(pl.multiple_of(dp * block, block), block), :]

    far_r.wait_recv()
    sum_s[0, low] = (sum_s[1, low].astype(F32) + far_s[0].astype(F32)).astype(BF)
    end_r = remote(sum_s.at[0, low], ring_s.at[0, low], ring_send.at[4], ring_recv.at[4], {"seq": right})
    far_l.wait_recv()
    sum_s[0, high] = (sum_s[3, high].astype(F32) + far_s[1].astype(F32)).astype(BF)
    end_l = remote(sum_s.at[0, high], ring_s.at[1, high], ring_send.at[5], ring_recv.at[5], {"seq": left})

    for copy in cols:
        copy.wait_recv()
    gos = []
    for step in range(1, dp_count):
        to = lax.rem(dp + step, dp_count)
        gos.append(remote(
            col_s.at[to // 2, pl.ds(pl.multiple_of(lax.rem(to, 2) * block, block), block)], go_s.at[dp],
            go_send.at[step], go_recv.at[step], {"dp": to},
        ))
    go_s[dp] = col_s[dp // 2, pl.ds(pl.multiple_of(lax.rem(dp, 2) * block, block), block), :]

    mine = pair_sum(0)
    earlier = (lax.broadcasted_iota(jnp.int32, (tokens, tokens), 0) < lax.broadcasted_iota(jnp.int32, (tokens, tokens), 1))
    same = owner_col_ref[...] == owner_row_ref[...]
    rank = jnp.sum(jnp.where(earlier & same, 1.0, 0.0), axis=0, keepdims=True).astype(jnp.int32)
    slot = owner_row_ref[...] * capacity + rank
    total = send_ref.shape[0]
    hit = lax.broadcasted_iota(jnp.int32, (total, tokens), 0) == slot
    ident = jnp.sum(jnp.where(hit, (row_ref[...] + 1).astype(F32), 0.0), axis=1, keepdims=True).astype(jnp.int32)
    lanes = lax.broadcasted_iota(jnp.int32, (total, 128), 1)
    code = jnp.where(lanes == 0, ident // 32, jnp.where(lanes == 1, ident % 32, 0))
    send_ref[:, D:] = code.astype(F32).astype(BF)
    place = jnp.where(hit, 1.0, 0.0).astype(BF)

    for copy in blocks:
        copy.wait_recv()
    acc = gw_s[0].astype(F32)
    for d in range(1, dp_count):
        acc = acc + gw_s[d].astype(F32)
    gsum_ref[...] = acc
    for copy in gos:
        copy.wait_recv()
    acc = go_s[0].astype(F32)
    for d in range(1, dp_count):
        acc = acc + go_s[d].astype(F32)
    gosum_ref[...] = acc

    near_r.wait_recv()
    near_l.wait_recv()
    end_r.wait_recv()
    end_l.wait_recv()
    total_grad = (mine + ring_s[0].astype(F32) + ring_s[1].astype(F32)).astype(BF)
    send_ref[:, :D] = (mm(place, total_grad, NT) + mm(place, og_ref[...])).astype(BF)

    for copy in list(pairs.values()) + cols + blocks + gos + [far_r, far_l, near_r, near_l, end_r, end_l]:
        copy.wait_send()


def reduce_all(
    g, w, mix, x_g, og_g, og, item_owner, item_row, seq_count, dp_count, capacity, devices
):
    tokens = og.shape[0]
    pos = tokens * seq_count
    hbm = pl.BlockSpec(memory_space=pl.ANY)
    block = D // dp_count
    shard = lambda n: pltpu.VMEM((n, D, tokens), BF)
    dma = lambda n: pltpu.SemaphoreType.DMA((n,))
    return pl.pallas_call(
        functools.partial(reduce_kernel, tokens, dp_count, capacity),
        out_shape=(
            jax.ShapeDtypeStruct((block, 8 * DH), F32),
            jax.ShapeDtypeStruct((block, 2 * DH), F32),
            jax.ShapeDtypeStruct((devices * capacity, D + 128), BF),
        ),
        in_specs=vmem(3) + [hbm] * 2 + vmem(4),
        out_specs=tuple(vmem(3)),
        scratch_shapes=[
            pltpu.VMEM((pos, D), BF),
            pltpu.VMEM((pos, D), BF),
            shard(4), shard(4), shard(4),
            pltpu.VMEM((2, D // 2, tokens), BF),
            shard(2),
            pltpu.VMEM((D, 8 * DH), BF),
            pltpu.VMEM((dp_count, block, 8 * DH), BF),
            pltpu.VMEM((2 * DH, D), BF),
            pltpu.VMEM((seq_count, 2 * DH, 2 * DH), BF),
            pltpu.VMEM((dp_count, block, 2 * DH), BF),
            dma(2), dma(4), dma(4), dma(6), dma(6), dma(dp_count), dma(dp_count),
            dma(seq_count), dma(seq_count), dma(dp_count), dma(dp_count),
        ],
        compiler_params=pltpu.CompilerParams(vmem_limit_bytes=VMEM_BYTES, collective_id=2, has_side_effects=True),
        name="reduce_all",
    )(g, w, mix, x_g, og_g, og, item_owner, item_owner.reshape(1, tokens), item_row.reshape(1, tokens))


def body(
    layer_input,
    out_grad,
    lengths,
    item_owner,
    item_row,
    w_attn,
    w_gate,
    w_out,
    emb_table,
    row_accum,
):
    seq_count = lax.axis_size("seq")
    dp_count = lax.axis_size("dp")
    devices = seq_count * dp_count
    tokens_dev = layer_input.shape[0]
    pos = tokens_dev * seq_count
    maxlen = 2 * pos // 3
    capacity = max(2, 2 * tokens_dev // devices)
    lens = lengths[0]
    acts = gather(lens, layer_input, out_grad, w_attn, w_gate, w_out, tokens_dev, seq_count, maxlen)
    og_late, acts["mg"] = lax.optimization_barrier((out_grad, acts["mg"]))
    og_g = lax.all_gather(og_late, "seq", axis=0, tiled=True)
    g, mix = backward(lens, acts["stats"], acts["h"], acts, pos, maxlen, seq_count)
    gw, go, send_rows = reduce_all(
        g, acts["w"], mix, acts["x"].reshape(pos, D), og_g, out_grad, item_owner, item_row,
        seq_count, dp_count, capacity, devices,
    )
    got = lax.all_to_all(send_rows.reshape(devices, capacity, D + 128), ("seq", "dp"), 0, 0, tiled=True)
    total = devices * capacity
    got = got.reshape(total, D + 128)
    got_ids = (got[:, D].astype(F32) * 32.0 + got[:, D + 1].astype(F32)).astype(jnp.int32) - 1
    rows_own = emb_table.shape[0]
    pick = (jnp.arange(rows_own, dtype=jnp.int32)[:, None] == got_ids[None, :]).astype(BF)
    table_grad = mm(pick, got[:, :D])
    new_accum = row_accum + jnp.mean(table_grad * table_grad, axis=1)
    new_table = emb_table - LEARN_RATE * table_grad * lax.rsqrt(new_accum)[:, None]
    return (gw[:, : 6 * DH], gw[:, 6 * DH :], go, new_table, new_accum)


def solution(mesh):
    placed = (
        P(("dp", "seq"), None),
        P(("dp", "seq"), None),
        P("dp", None),
        P(("dp", "seq"), None),
        P(("dp", "seq")),
        P(),
        P(),
        P(),
        P(("seq", "dp"), None),
        P(("seq", "dp")),
    )
    return jax.shard_map(
        body,
        mesh=mesh,
        in_specs=placed,
        out_specs=(
            P("dp", "seq"),
            P("dp", "seq"),
            P("dp", "seq"),
            P(("seq", "dp"), None),
            P(("seq", "dp")),
        ),
        check_vma=False,
    )
```

time: 183 us -> 165 us (0.902)
  Pallas kernels: 128 us -> 100 us
  waiting for transfers between devices: 24.5 us -> 31.2 us
  starting transfers between devices: 6.79 us -> 9.17 us
    pallas_call x3 -> x1, Pallas kernels: 66.1 us -> 42 us  [gather(): pl.pallas_call(functools.partial(gather_kernel, tokens, maxlen), out_shap...]
    pallas_call x1, Pallas kernels: 29.3 us -> 20 us  [backward(): pl.pallas_call(functools.partial(bwd_kernel, pos, maxlen, seq_count), out...]
    all_gather x1, waiting for transfers between devices: 5.33 us -> 12 us  [body(): og_g = lax.all_gather(og_late, 'seq', axis=0, tiled=True)]
    pallas_call x1, Pallas kernels: 32.5 us -> 38.4 us  [reduce_all(): pl.pallas_call(functools.partial(reduce_kernel, tokens, dp_count, capacit...]
    all_to_all x1, starting transfers between devices: 6.76 us -> 9.13 us  [body(): lax.all_to_all(send_rows.reshape(devices, capacity, D + 128), ('seq', 'dp...]
  transfers between devices with their start and end apart: 2 -> 2, of which waited for: 2 -> 2; matrix products, arithmetic and copies ran while one was open for 1% -> 1% of each run, Pallas kernels for 16% -> 12%
where the time goes in v2:
time: 165 us; the launch traced here: 164 us
  Pallas kernels  100 us (61%)
  waiting for transfers between devices  31.2 us (19%)
  between operations  14.1 us (9%)
  starting transfers between devices  9.17 us (6%)
  local copies, waits for them, and re-layouts  6.59 us (4%)
  other arithmetic  2.19 us (1%)
    pallas_call x1, Pallas kernels, gather(): pl.pallas_call(functools.partial(gather_kernel, tokens, maxlen), out_shap...  42 us
    pallas_call x1, Pallas kernels, reduce_all(): pl.pallas_call(functools.partial(reduce_kernel, tokens, dp_count, capacit...  38.4 us
    pallas_call x1, Pallas kernels, backward(): pl.pallas_call(functools.partial(bwd_kernel, pos, maxlen, seq_count), out...  20 us
    all_to_all x1, waiting for transfers between devices, body(): lax.all_to_all(send_rows.reshape(devices, capacity, D + 128), ('seq', 'dp...  19.1 us
    all_gather x1, waiting for transfers between devices, body(): og_g = lax.all_gather(og_late, 'seq', axis=0, tiled=True)  12 us
    all_to_all x1, starting transfers between devices, body(): lax.all_to_all(send_rows.reshape(devices, capacity, D + 128), ('seq', 'dp...  9.13 us
  transfers between devices with their start and end apart: 2, of which 2 were waited for; matrix products, arithmetic and copies ran while one was open for 1% of the time, Pallas kernels for 12%

profile of v2, /device:TPU:0, one launch (start us, length us, event | category | flops | bytes accessed | tf_op | source)
XLA Modules:
  0.0 164.5 jit_solution(778443265088450168)
XLA Ops:
  7.2 0.0 all-gather.2.cloned.1.call-start
  7.2 0.0 copy-start.3
  7.2 42.0 %gather.1 = (bf16[8,256,1024]{2,1,0:T(8,128)(2,1)}, bf16[1024,512]{1,0:T(8,128)(2,1)}, bf16[2,64,2048]{2,1,0:T(8,128)(2,1)}, bf16[2,64,2048]{2,1,0:T(8,128)(2,1)...) custom-call(s32[3]{0:T(128)} %bitcast.7, ...), custom_call_target="tpu_custom_call" | custom-call | tf_op jit(solution)/shard_map/gather/pallas_call | solution.py:371
  49.2 0.0 all-gather.2.cloned.1.call-update
  49.2 0.0 copy-done.3
  49.3 0.8 copy.19.owner_col_ref
  50.1 20.0 %backward.1 = (bf16[512,2048]{1,0:T(8,128)(2,1)}, bf16[128,2048]{1,0:T(8,128)(2,1)}) custom-call(s32[3]{0:T(128)} %bitcast.8, f32[8,8,1024]{2,1,0:T(8,128)} %get-tuple-element.24.sta_ref, bf16[128,2048]{1,0:T(8,128)(2,1)} %get-tuple-element.25.h_ref, f32[128,2048]{1,0:T(8,128)} %get-tuple-element.26.gate_ref, f32[128,2048]{1,0:T(8,128)} %get-tuple-element.27.gsg_ref, ...), custom_call_target="tpu_custom_call" | custom-call | tf_op jit(solution)/shard_map/backward/pallas_call | solution.py:154
  70.1 12.0 %all-gather.2.cloned.1.call-done.og_hbm = bf16[2048,1024]{1,0:T(8,128)(2,1)} async-done(((bf16[256,1024]{1,0:T(8,128)(2,1)}), bf16[2048,1024]{1,0:T(8,128)(2,1)}) %all-gather.2.cloned.1.call-update) | async-done | bytes 4194320 | tf_op jit(solution)/shard_map/all_gather | solution.py:592
  82.1 38.4 %reduce_all.1 = (f32[64,512]{1,0:T(8,128)}, f32[64,128]{1,0:T(8,128)}, bf16[512,1152]{1,0:T(8,128)(2,1)}) custom-call(bf16[512,2048]{1,0:T(8,128)(2,1)} %get-tuple-element.35.g_ref, bf16[1024,512]{1,0:T(8,128)(2,1)} %get-tuple-element.36.w_ref, bf16[128,2048]{1,0:T(8,128)(2,1)} %get-tuple-element.37.mix_ref, bf16[2048,1024]{1,0:T(8,128)(2,1)} %bitcast.5, ...), custom_call_target="tpu_custom_call" | custom-call | tf_op jit(solution)/shard_map/reduce_all/pallas_call | solution.py:542
  120.5 0.0 copy-start.1
  120.5 3.3 %reshape.49 = bf16[128,4,1152]{2,1,0:T(4,128)(2,1)} reshape(bf16[512,1152]{1,0:T(8,128)(2,1)} %get-tuple-element.42) | data formatting | bytes 2359296 | tf_op jit(solution)/shard_map/reshape | solution.py:598
  123.8 9.1 %all-to-all-start = ((bf16[128,4,1152]{2,1,0:T(4,128)(2,1)}), bf16[128,4,1152]{2,1,0:T(4,128)(2,1)S(1)}, u32[]{:S(2)}, u32[]{:S(2)}) async-start(bf16[128,4,1152]{2,1,0:T(4,128)(2,1)} %reshape.49), calls=%async_computation | async-start | bytes 2359296 | tf_op jit(solution)/shard_map/all_to_all | solution.py:598
  132.9 0.0 copy-done.1
  132.9 0.6 slice.15
  133.6 0.6 slice.16
  134.2 19.1 %all-to-all-done = bf16[128,4,1152]{2,1,0:T(4,128)(2,1)S(1)} async-done(((bf16[128,4,1152]{2,1,0:T(4,128)(2,1)}), bf16[128,4,1152]{2,1,0:T(4,128)(2,1)S(1)}, u32[]{:S(2)}, u32[]{:S(2)}) %all-to-all-start) | async-done | bytes 1179680 | tf_op jit(solution)/shard_map/all_to_all | solution.py:598
  153.3 0.3 reshape.50
  153.6 0.1 fusion.3
  153.7 0.0 copy-start.4
  153.8 0.0 copy-start
  153.8 0.1 copy.22
  153.9 0.1 copy.23
  154.0 0.8 multiply_reduce_fusion
  154.8 0.0 copy-done.4
  154.8 0.6 rsqrt_multiply_fusion
  155.4 0.0 copy-done
  155.4 0.0 copy-start.2
  155.4 1.6 multiply_subtract_fusion
  157.0 0.0 copy-done.2
  157.0 0.6 copy.25
  (1 shorter events, 0.0 us)
Async XLA Ops:
  7.2 74.9 %all-gather.2.cloned.1.call-start = ((), (), s32[]{:S(2)}) async-start(), calls=%async_computation.1 | async-start | bytes 4718592 | tf_op jit(solution)/shard_map/all_gather | solution.py:592
  7.2 42.0 %copy-start.3 = (s32[256,1]{0,1:T(1,128)S(1)}, s32[256,1]{0,1:T(1,128)}, u32[]{:S(2)}) copy-start(s32[256,1]{0,1:T(1,128)} %param.13) | copy-start | bytes 3076
  120.5 12.4 %copy-start.1 = (f32[64,512]{1,0:T(8,128)S(1)}, f32[64,512]{1,0:T(8,128)}, u32[]{:S(2)}) copy-start(f32[64,512]{1,0:T(8,128)} %get-tuple-element.40) | copy-start | bytes 393220
  123.8 29.5 %all-to-all-start = ((bf16[128,4,1152]{2,1,0:T(4,128)(2,1)}), bf16[128,4,1152]{2,1,0:T(4,128)(2,1)S(1)}, u32[]{:S(2)}, u32[]{:S(2)}) async-start(bf16[128,4,1152]{2,1,0:T(4,128)(2,1)} %reshape.49), calls=%async_computation | async-start | bytes 2359296 | tf_op jit(solution)/shard_map/all_to_all | solution.py:598
  153.7 1.1 copy-start.4
  153.8 1.6 %copy-start = (f32[512,1024]{1,0:T(8,128)S(1)}, f32[512,1024]{1,0:T(8,128)}, u32[]{:S(2)}) copy-start(f32[512,1024]{1,0:T(8,128)} %param.18) | copy-start | bytes 6291460
  155.4 1.6 copy-start.2
Sparse Core Ops, SparseCore 0:
  49.4 32.6 all-gather.1

commit v3 on v2

--- a/solution.py
+++ b/solution.py
@@ -63,113 +63,8 @@
     return row, slice(lane, lane + chunk)
 
 
-def bwd_kernel(
-    pos, maxlen, seq_count,
-    len_ref, sta_ref, h_ref, gate_ref, gsg_ref, mg_ref, q_ref, kt_ref, k_ref, v_ref, sg_hbm,
-    g_ref, mix_ref,
-    sg_s, sem, ot_s, dv_s, dk_s,
-):
-    sg_copy = pltpu.make_async_copy(sg_hbm, sg_s, sem)
-    sg_copy.start()
-    chunk = 512
-    for c in range(pos // chunk):
-        at = slice(c * chunk, (c + 1) * chunk)
-        row, lane = stat_place(pos, chunk, c)
-        means = [sta_ref[d, row : row + 1, lane] for d in range(seq_count)]
-        mean = functools.reduce(jnp.add, means) * (1.0 / seq_count)
-        var = jnp.zeros_like(mean)
-        ng_mean = jnp.zeros_like(mean)
-        ng_cov = jnp.zeros_like(mean)
-        for d in range(seq_count):
-            off = means[d] - mean
-            ng_sum = sta_ref[d, row + 2 : row + 3, lane]
-            var = var + sta_ref[d, row + 1 : row + 2, lane] + (2 * DH) * off * off
-            ng_mean = ng_mean + ng_sum
-            ng_cov = ng_cov + sta_ref[d, row + 3 : row + 4, lane] + off * ng_sum
-        inv = lax.rsqrt(var * (1.0 / D) + NORM_EPS)
-        ng_mean = ng_mean * (1.0 / D)
-        proj = inv * ng_cov * (1.0 / D)
-        gate = gate_ref[:, at]
-        normed = (h_ref[:, at].astype(F32) - mean) * inv
-        mix_ref[:, at] = (normed * gate).astype(BF)
-        mg = mg_ref[:, at].astype(F32)
-        g_ref[6 * DH :, at] = (mg * normed * gsg_ref[:, at]).astype(BF)
-        hg = (inv * (mg * gate - ng_mean - normed * proj)).astype(BF)
-        for hd in range(2):
-            ot_s[hd, :, at] = hg[hd * DH : (hd + 1) * DH]
-    dv_s[...] = jnp.zeros_like(dv_s)
-    dk_s[...] = jnp.zeros_like(dk_s)
-    fac = 0.0625 / maxlen
-
-    @pl.loop(0, pos // TQ)
-    def _(i):
-        at = pl.ds(pl.multiple_of(i * TQ, TQ), TQ)
-        first = scalar_start(len_ref, i * TQ) // TK
-        last = ((i + 1) * TQ - 1) // TK
-
-        def step(j, accs):
-            kat = pl.ds(pl.multiple_of(j * TK, TK), TK)
-            allowed = tile_allowed(len_ref, j, i)
-            outs = []
-            for hd in range(2):
-                t = mm(k_ref[hd, kat, :], q_ref[hd, :, at])
-                dw = mm(v_ref[hd, kat, :], ot_s[hd, :, at])
-                a = 1.0 + jnp.tanh(t)
-                w = t * a
-                ds = jnp.where(allowed, dw * (a + w * (2.0 - a)), 0.0).astype(BF)
-                w = jnp.where(allowed, w, 0.0).astype(BF)
-                dv_s[hd, :, kat] += mm(ot_s[hd, :, at], w, NT)
-                dk_s[hd, :, kat] += mm(q_ref[hd, :, at], ds, NT)
-                outs.append(accs[hd] + mm(kt_ref[hd, :, kat], ds))
-            return tuple(outs)
-
-        zero = jnp.zeros((DH, TQ), F32)
-        accs = lax.fori_loop(first, last + 1, step, (zero, zero))
-        for hd in range(2):
-            base = hd * 3 * DH + DH
-            g_ref[base : base + DH, at] = (accs[hd] * fac).astype(BF)
-
-    sg_copy.wait()
-
-    @pl.loop(0, pos // chunk)
-    def _(c):
-        at = pl.ds(pl.multiple_of(c * chunk, chunk), chunk)
-        for hd in range(2):
-            base = hd * 3 * DH
-            dv = (dv_s[hd, :, at] * (1.0 / maxlen)).astype(BF)
-            dk = (dk_s[hd, :, at] * (16.0 * fac)).astype(BF)
-            dq = g_ref[base + DH : base + 2 * DH, at]
-            for part, grad in enumerate((dv, dq, dk)):
-                rows = slice(base + part * DH, base + (part + 1) * DH)
-                g_ref[rows, at] = (grad.astype(F32) * sg_s[rows, at]).astype(BF)
-
-
 def vmem(count):
     return [pl.BlockSpec(memory_space=pltpu.VMEM)] * count
-
-
-def backward(lens, stats, h, acts, pos, maxlen, seq_count):
-    heads = pltpu.VMEM((2, DH, pos), BF)
-    sums = pltpu.VMEM((2, DH, pos), F32)
-    return pl.pallas_call(
-        functools.partial(bwd_kernel, pos, maxlen, seq_count),
-        out_shape=(
-            jax.ShapeDtypeStruct((8 * DH, pos), BF),
-            jax.ShapeDtypeStruct((2 * DH, pos), BF),
-        ),
-        in_specs=[pl.BlockSpec(memory_space=pltpu.SMEM)] + vmem(9) + [pl.BlockSpec(memory_space=pl.ANY)],
-        out_specs=tuple(vmem(2)),
-        scratch_shapes=[
-            pltpu.VMEM((6 * DH, pos), F32),
-            pltpu.SemaphoreType.DMA,
-            heads, sums, sums,
-        ],
-        compiler_params=pltpu.CompilerParams(vmem_limit_bytes=VMEM_BYTES),
-        name="backward",
-    )(
-        lens, stats, h, acts["gate"], acts["gsg"], acts["mg"],
-        acts["q"], acts["kt"], acts["k"], acts["v"], acts["sg"],
-    )
 
 
 def seq_peers():
@@ -294,13 +189,6 @@
     sib_left = send(7, left, None, sib)
     to_left[0].wait_recv()
     sib_right = send(8, right, None, sib)
-    mg_copies = []
-    for step in range(1, 8):
-        to = lax.rem(me + step, 8)
-        mg_copies.append(remote(
-            mine_s.at[pl.ds(pl.multiple_of(to * 2 * DH, 2 * DH), 2 * DH)], mg_ref.at[:, mine],
-            mg_send.at[step], mg_recv.at[step], to,
-        ))
     other = 1 - 2 * c
     project(left)
     sib_left.wait_recv()
@@ -313,6 +201,13 @@
     sib_far0 = send(9, far, 0, sib)
     fwd_l.wait_recv()
     sib_far1 = send(10, far, 1, sib)
+    mg_copies = []
+    for step in range(1, 8):
+        to = lax.rem(me + step, 8)
+        mg_copies.append(remote(
+            mine_s.at[pl.ds(pl.multiple_of(to * 2 * DH, 2 * DH), 2 * DH)], mg_ref.at[:, mine],
+            mg_send.at[step], mg_recv.at[step], to,
+        ))
     attend(2)
     project(far)
     sib_far0.wait_recv()
@@ -400,72 +295,196 @@
     return dict(zip(names, outs))
 
 
-def reduce_kernel(
-    tokens, dp_count, capacity,
-    g_ref, w_ref, mix_ref, x_hbm, og_hbm, og_ref, owner_col_ref, owner_row_ref, row_ref,
+def grads_kernel(
+    tokens, maxlen, dp_count, capacity,
+    len_ref, sta_ref, h_ref, gate_ref, gsg_ref, mg_ref, q_ref, kt_ref, k_ref, v_ref, w_ref, sg_hbm, x_hbm,
+    og_ref, owner_col_ref, owner_row_ref, row_ref,
     gsum_ref, gosum_ref, send_ref,
-    x_s, og_s, out_s, pair_s, sum_s, far_s, ring_s, gsrc_s, gw_s, gosrc_s, col_s, go_s,
-    load_sem, pair_send, pair_recv, ring_send, ring_recv, gw_send, gw_recv, col_send, col_recv, go_send, go_recv,
+    sg_s, x_s, mix_s, ot_s, dv_s, dk_s, dq_s, g_s, gacc_s,
+    out_s, pair_s, sum_s, far_s, ring_s,
+    mixr_s, gop_s, gopair_s, gosum_s, gor_s, goout_s, gocol_s, gsrc_s, gw_s,
+    load_sem, mix_send, mix_recv, pair_send, pair_recv, ring_send, ring_recv,
+    gp_send, gp_recv, go_send, go_recv, gc_send, gc_recv, gw_send, gw_recv,
 ):
-    me, sib, right, left, far, c = seq_peers()
+    me, sib, right, left, _, c = seq_peers()
     z = me // 2
     dp = lax.axis_index("dp")
+    seq_count = 8
+    pos = seq_count * tokens
+    span = 2 * tokens
     half = D // 2
     block = D // dp_count
-
-    x_load = pltpu.make_async_copy(x_hbm, x_s, load_sem.at[0])
-    og_load = pltpu.make_async_copy(og_hbm, og_s, load_sem.at[1])
-    og_load.start()
+    hb = block // 2
+
+    sg_load = pltpu.make_async_copy(sg_hbm, sg_s, load_sem.at[0])
+    x_load = pltpu.make_async_copy(x_hbm, x_s, load_sem.at[1])
+    sg_load.start()
     x_load.start()
-
     barrier = pltpu.get_barrier_semaphore()
-    for step in range(1, 8):
-        pl.semaphore_signal(barrier, inc=1, device_id={"seq": lax.rem(me + step, 8)}, device_id_type=MESH)
+    for step in range(1, seq_count):
+        pl.semaphore_signal(barrier, inc=1, device_id={"seq": lax.rem(me + step, seq_count)}, device_id_type=MESH)
     for step in range(1, dp_count):
         pl.semaphore_signal(barrier, inc=1, device_id={"dp": lax.rem(dp + step, dp_count)}, device_id_type=MESH)
-    pl.semaphore_wait(barrier, 7 + dp_count - 1)
-
-    def remote(src, dst, send_sem, recv_sem, to):
-        copy = pltpu.make_async_remote_copy(
+
+    def describe(src, dst, send_sem, recv_sem, to):
+        return pltpu.make_async_remote_copy(
             src_ref=src, dst_ref=dst, send_sem=send_sem, recv_sem=recv_sem, device_id=to, device_id_type=MESH
         )
+
+    def remote(*args):
+        copy = describe(*args)
         copy.start()
         return copy
 
-    def partial_grad(shard):
-        return mm(w_ref[...], g_ref[:, pl.ds(pl.multiple_of(shard * tokens, tokens), tokens)])
+    for ch in range(pos // span):
+        at = slice(ch * span, (ch + 1) * span)
+        row, lane = stat_place(pos, span, ch)
+        means = [sta_ref[d, row : row + 1, lane] for d in range(seq_count)]
+        mean = functools.reduce(jnp.add, means) * (1.0 / seq_count)
+        var = jnp.zeros_like(mean)
+        ng_mean = jnp.zeros_like(mean)
+        ng_cov = jnp.zeros_like(mean)
+        for d in range(seq_count):
+            off = means[d] - mean
+            ng_sum = sta_ref[d, row + 2 : row + 3, lane]
+            var = var + sta_ref[d, row + 1 : row + 2, lane] + (2 * DH) * off * off
+            ng_mean = ng_mean + ng_sum
+            ng_cov = ng_cov + sta_ref[d, row + 3 : row + 4, lane] + off * ng_sum
+        inv = lax.rsqrt(var * (1.0 / D) + NORM_EPS)
+        ng_mean = ng_mean * (1.0 / D)
+        proj = inv * ng_cov * (1.0 / D)
+        gate = gate_ref[:, at]
+        normed = (h_ref[:, at].astype(F32) - mean) * inv
+        mix_s[:, at] = (normed * gate).astype(BF)
+        mg = mg_ref[:, at].astype(F32)
+        g_s[6 * DH :, at] = (mg * normed * gsg_ref[:, at]).astype(BF)
+        hg = (inv * (mg * gate - ng_mean - normed * proj)).astype(BF)
+        for hd in range(2):
+            ot_s[hd, :, at] = hg[hd * DH : (hd + 1) * DH]
+    dv_s[...] = jnp.zeros_like(dv_s)
+    dk_s[...] = jnp.zeros_like(dk_s)
+    dq_s[...] = jnp.zeros_like(dq_s)
+    fac = 0.0625 / maxlen
+
+    pl.semaphore_wait(barrier, seq_count - 1 + dp_count - 1)
+    feats = pl.ds(pl.multiple_of(me * 2 * DH, 2 * DH), 2 * DH)
+    mixes = []
+    for step in range(1, seq_count):
+        to = lax.rem(me + step, seq_count)
+        mixes.append(remote(
+            mix_s.at[:, pl.ds(pl.multiple_of(to * tokens, tokens), tokens)], mixr_s.at[feats],
+            mix_send.at[step], mix_recv.at[step], {"seq": to},
+        ))
+    mixr_s[feats, :] = mix_s[:, pl.ds(pl.multiple_of(me * tokens, tokens), tokens)]
+
+    def chip_block(k):
+        return lax.rem(z + k, 4)
+
+    def lanes_of(b):
+        return pl.ds(pl.multiple_of(b * span, span), span)
+
+    def attend(n):
+        new = chip_block(block_step(3 - n))
+
+        def tile(m, carry):
+            old = chip_block(block_step(3 - m))
+            later = (new - old + 4) // 4
+            i = later * new + (1 - later) * old
+            j = new + old - i
+            at, kat = lanes_of(i), lanes_of(j)
+            allowed = tile_allowed(len_ref, j, i)
+            for hd in range(2):
+                t = mm(k_ref[hd, kat, :], q_ref[hd, :, at])
+                dw = mm(v_ref[hd, kat, :], ot_s[hd, :, at])
+                a = 1.0 + jnp.tanh(t)
+                w = t * a
+                ds = jnp.where(allowed, dw * (a + w * (2.0 - a)), 0.0).astype(BF)
+                w = jnp.where(allowed, w, 0.0).astype(BF)
+                dv_s[hd, :, kat] += mm(ot_s[hd, :, at], w, NT)
+                dk_s[hd, :, kat] += mm(q_ref[hd, :, at], ds, NT)
+                dq_s[hd, :, at] += mm(kt_ref[hd, :, kat], ds)
+            return carry
+
+        lax.fori_loop(n, 4, tile, 0)
+        at = lanes_of(new)
+        for hd in range(2):
+            base = hd * 3 * DH
+            dv = (dv_s[hd, :, at] * (1.0 / maxlen)).astype(BF)
+            dk = (dk_s[hd, :, at] * (16.0 * fac)).astype(BF)
+            dq = (dq_s[hd, :, at] * fac).astype(BF)
+            for part, grad in enumerate((dv, dq, dk)):
+                rows = slice(base + part * DH, base + (part + 1) * DH)
+                g_s[rows, at] = (grad.astype(F32) * sg_s[rows, at]).astype(BF)
+
+    def partial_grad(k, core):
+        first = chip_block(k) * span + core * tokens
+        return mm(w_ref[...], g_s[:, pl.ds(pl.multiple_of(first, tokens), tokens)])
 
     pairs = {}
-    for k in (2, 1, 3, 0):
-        out_s[k] = partial_grad(lax.rem(z + k, 4) * 2 + 1 - c).astype(BF)
+
+    def share(k):
+        out_s[k] = partial_grad(k, 1 - c).astype(BF)
         pairs[k] = remote(out_s.at[k], pair_s.at[k], pair_send.at[k], pair_recv.at[k], {"seq": sib})
-
-    def pair_sum(k):
-        own = partial_grad(lax.rem(z + k, 4) * 2 + c)
+        at = lanes_of(chip_block(k))
+        part = mm(g_s[:, at], x_s[at, :])
+        gacc_s[...] = part if k == 2 else gacc_s[...] + part
+
+    low, high = pl.ds(0, half), pl.ds(half, half)
+    hops = [
+        describe(sum_s.at[2, low], far_s.at[0], ring_send.at[0], ring_recv.at[0], {"seq": right}),
+        describe(sum_s.at[2, high], far_s.at[1], ring_send.at[1], ring_recv.at[1], {"seq": left}),
+        describe(sum_s.at[1, high], ring_s.at[0, high], ring_send.at[2], ring_recv.at[2], {"seq": right}),
+        describe(sum_s.at[3, low], ring_s.at[1, low], ring_send.at[3], ring_recv.at[3], {"seq": left}),
+        describe(sum_s.at[1, low], ring_s.at[0, low], ring_send.at[4], ring_recv.at[4], {"seq": right}),
+        describe(sum_s.at[3, high], ring_s.at[1, high], ring_send.at[5], ring_recv.at[5], {"seq": left}),
+    ]
+
+    def settle(k):
+        own = partial_grad(k, c)
         pairs[k].wait_recv()
-        return own + pair_s[k].astype(F32)
-
-    low, high = pl.ds(0, half), pl.ds(half, half)
-    sum_s[2] = pair_sum(2).astype(BF)
-    far_r = remote(sum_s.at[2, low], far_s.at[0], ring_send.at[0], ring_recv.at[0], {"seq": right})
-    far_l = remote(sum_s.at[2, high], far_s.at[1], ring_send.at[1], ring_recv.at[1], {"seq": left})
-    sum_s[1] = pair_sum(1).astype(BF)
-    near_r = remote(sum_s.at[1, high], ring_s.at[0, high], ring_send.at[2], ring_recv.at[2], {"seq": right})
-    sum_s[3] = pair_sum(3).astype(BF)
-    near_l = remote(sum_s.at[3, low], ring_s.at[1, low], ring_send.at[3], ring_recv.at[3], {"seq": left})
-
-    og_load.wait()
-    gosrc_s[...] = mm(mix_ref[...], og_s[...]).astype(BF)
-    cols = []
-    for step in range(1, 8):
-        to = lax.rem(me + step, 8)
-        cols.append(remote(
-            gosrc_s.at[:, pl.ds(pl.multiple_of(to * 2 * DH, 2 * DH), 2 * DH)], col_s.at[me],
-            col_send.at[step], col_recv.at[step], {"seq": to},
-        ))
-    col_s[me] = gosrc_s[:, pl.ds(pl.multiple_of(me * 2 * DH, 2 * DH), 2 * DH)]
+        sum_s[k] = (own + pair_s[k].astype(F32)).astype(BF)
+
+    sg_load.wait()
+    attend(0)
     x_load.wait()
-    gsrc_s[...] = mm(g_ref[...], x_s[...]).astype(BF).T
+    share(2)
+    settle(2)
+    hops[0].start()
+    hops[1].start()
+
+    for copy in mixes:
+        copy.wait_recv()
+    gop_s[...] = mm(mixr_s[...], og_ref[...]).astype(BF).reshape(dp_count, block, D)
+    mine = pl.ds(pl.multiple_of(c * hb, hb), hb)
+    theirs = pl.ds(pl.multiple_of((1 - c) * hb, hb), hb)
+    go_pair = remote(gop_s.at[:, theirs], gopair_s, gp_send.at[0], gp_recv.at[0], {"seq": sib})
+
+    attend(1)
+    share(1)
+    settle(1)
+    hops[2].start()
+    go_pair.wait_recv()
+    gosum_s[...] = (gop_s[:, mine, :].astype(F32) + gopair_s[...].astype(F32)).astype(BF)
+    gos = []
+    for step in range(1, dp_count):
+        to = lax.rem(dp + step, dp_count)
+        gos.append(remote(gosum_s.at[to], gor_s.at[dp], go_send.at[step], go_recv.at[step], {"dp": to}))
+    gor_s[dp] = gosum_s[dp]
+    hops[0].wait_recv()
+    sum_s[1, low] = (sum_s[1, low].astype(F32) + far_s[0].astype(F32)).astype(BF)
+    hops[4].start()
+
+    attend(2)
+    share(3)
+    settle(3)
+    hops[3].start()
+    hops[1].wait_recv()
+    sum_s[3, high] = (sum_s[3, high].astype(F32) + far_s[1].astype(F32)).astype(BF)
+    hops[5].start()
+
+    attend(3)
+    share(0)
+    gsrc_s[...] = gacc_s[...].astype(BF).T
     blocks = []
     for step in range(1, dp_count):
         to = lax.rem(dp + step, dp_count)
@@ -474,26 +493,8 @@
             gw_send.at[step], gw_recv.at[step], {"dp": to},
         ))
     gw_s[dp] = gsrc_s[pl.ds(pl.multiple_of(dp * block, block), block), :]
-
-    far_r.wait_recv()
-    sum_s[0, low] = (sum_s[1, low].astype(F32) + far_s[0].astype(F32)).astype(BF)
-    end_r = remote(sum_s.at[0, low], ring_s.at[0, low], ring_send.at[4], ring_recv.at[4], {"seq": right})
-    far_l.wait_recv()
-    sum_s[0, high] = (sum_s[3, high].astype(F32) + far_s[1].astype(F32)).astype(BF)
-    end_l = remote(sum_s.at[0, high], ring_s.at[1, high], ring_send.at[5], ring_recv.at[5], {"seq": left})
-
-    for copy in cols:
-        copy.wait_recv()
-    gos = []
-    for step in range(1, dp_count):
-        to = lax.rem(dp + step, dp_count)
-        gos.append(remote(
-            col_s.at[to // 2, pl.ds(pl.multiple_of(lax.rem(to, 2) * block, block), block)], go_s.at[dp],
-            go_send.at[step], go_recv.at[step], {"dp": to},
-        ))
-    go_s[dp] = col_s[dp // 2, pl.ds(pl.multiple_of(lax.rem(dp, 2) * block, block), block), :]
-
-    mine = pair_sum(0)
+    settle(0)
+
     earlier = (lax.broadcasted_iota(jnp.int32, (tokens, tokens), 0) < lax.broadcasted_iota(jnp.int32, (tokens, tokens), 1))
     same = owner_col_ref[...] == owner_row_ref[...]
     rank = jnp.sum(jnp.where(earlier & same, 1.0, 0.0), axis=0, keepdims=True).astype(jnp.int32)
@@ -506,65 +507,78 @@
     send_ref[:, D:] = code.astype(F32).astype(BF)
     place = jnp.where(hit, 1.0, 0.0).astype(BF)
 
+    for copy in gos:
+        copy.wait_recv()
+    acc = gor_s[0].astype(F32)
+    for d in range(1, dp_count):
+        acc = acc + gor_s[d].astype(F32)
+    goout_s[...] = acc.astype(BF)
+    cols = []
+    for step in range(1, seq_count):
+        to = lax.rem(me + step, seq_count)
+        cols.append(remote(
+            goout_s.at[:, pl.ds(pl.multiple_of(to * 2 * DH, 2 * DH), 2 * DH)], gocol_s.at[me],
+            gc_send.at[step], gc_recv.at[step], {"seq": to},
+        ))
+    gocol_s[me] = goout_s[:, pl.ds(pl.multiple_of(me * 2 * DH, 2 * DH), 2 * DH)]
+
+    for hop in hops[2:]:
+        hop.wait_recv()
+    total_grad = (sum_s[0].astype(F32) + ring_s[0].astype(F32) + ring_s[1].astype(F32)).astype(BF)
+    send_ref[:, :D] = (mm(place, total_grad, NT) + mm(place, og_ref[...])).astype(BF)
+
+    for copy in cols:
+        copy.wait_recv()
+    for core in range(2):
+        acc = gocol_s[core].astype(F32)
+        for chip in range(1, 4):
+            acc = acc + gocol_s[2 * chip + core].astype(F32)
+        gosum_ref[core * hb : (core + 1) * hb, :] = acc
     for copy in blocks:
         copy.wait_recv()
     acc = gw_s[0].astype(F32)
     for d in range(1, dp_count):
         acc = acc + gw_s[d].astype(F32)
     gsum_ref[...] = acc
-    for copy in gos:
-        copy.wait_recv()
-    acc = go_s[0].astype(F32)
-    for d in range(1, dp_count):
-        acc = acc + go_s[d].astype(F32)
-    gosum_ref[...] = acc
-
-    near_r.wait_recv()
-    near_l.wait_recv()
-    end_r.wait_recv()
-    end_l.wait_recv()
-    total_grad = (mine + ring_s[0].astype(F32) + ring_s[1].astype(F32)).astype(BF)
-    send_ref[:, :D] = (mm(place, total_grad, NT) + mm(place, og_ref[...])).astype(BF)
-
-    for copy in list(pairs.values()) + cols + blocks + gos + [far_r, far_l, near_r, near_l, end_r, end_l]:
+
+    for copy in mixes + list(pairs.values()) + hops + [go_pair] + gos + cols + blocks:
         copy.wait_send()
 
 
-def reduce_all(
-    g, w, mix, x_g, og_g, og, item_owner, item_row, seq_count, dp_count, capacity, devices
-):
+def grads(lens, acts, og, item_owner, item_row, seq_count, dp_count, capacity, devices, maxlen):
     tokens = og.shape[0]
     pos = tokens * seq_count
     hbm = pl.BlockSpec(memory_space=pl.ANY)
     block = D // dp_count
-    shard = lambda n: pltpu.VMEM((n, D, tokens), BF)
+    bf = lambda *shape: pltpu.VMEM(shape, BF)
+    f32 = lambda *shape: pltpu.VMEM(shape, F32)
     dma = lambda n: pltpu.SemaphoreType.DMA((n,))
     return pl.pallas_call(
-        functools.partial(reduce_kernel, tokens, dp_count, capacity),
+        functools.partial(grads_kernel, tokens, maxlen, dp_count, capacity),
         out_shape=(
             jax.ShapeDtypeStruct((block, 8 * DH), F32),
             jax.ShapeDtypeStruct((block, 2 * DH), F32),
             jax.ShapeDtypeStruct((devices * capacity, D + 128), BF),
         ),
-        in_specs=vmem(3) + [hbm] * 2 + vmem(4),
+        in_specs=[pl.BlockSpec(memory_space=pltpu.SMEM)] + vmem(10) + [hbm] * 2 + vmem(4),
         out_specs=tuple(vmem(3)),
         scratch_shapes=[
-            pltpu.VMEM((pos, D), BF),
-            pltpu.VMEM((pos, D), BF),
-            shard(4), shard(4), shard(4),
-            pltpu.VMEM((2, D // 2, tokens), BF),
-            shard(2),
-            pltpu.VMEM((D, 8 * DH), BF),
-            pltpu.VMEM((dp_count, block, 8 * DH), BF),
-            pltpu.VMEM((2 * DH, D), BF),
-            pltpu.VMEM((seq_count, 2 * DH, 2 * DH), BF),
-            pltpu.VMEM((dp_count, block, 2 * DH), BF),
-            dma(2), dma(4), dma(4), dma(6), dma(6), dma(dp_count), dma(dp_count),
-            dma(seq_count), dma(seq_count), dma(dp_count), dma(dp_count),
+            f32(6 * DH, pos), bf(pos, D), bf(2 * DH, pos), bf(2, DH, pos),
+            f32(2, DH, pos), f32(2, DH, pos), f32(2, DH, pos), bf(8 * DH, pos), f32(8 * DH, D),
+            bf(4, D, tokens), bf(4, D, tokens), bf(4, D, tokens), bf(2, D // 2, tokens), bf(2, D, tokens),
+            bf(D, tokens), bf(dp_count, block, D), bf(dp_count, block // 2, D), bf(dp_count, block // 2, D),
+            bf(dp_count, block // 2, D), bf(block // 2, D), bf(seq_count, block // 2, 2 * DH),
+            bf(D, 8 * DH), bf(dp_count, block, 8 * DH),
+            dma(2), dma(seq_count), dma(seq_count), dma(4), dma(4), dma(6), dma(6),
+            dma(1), dma(1), dma(dp_count), dma(dp_count), dma(seq_count), dma(seq_count), dma(dp_count), dma(dp_count),
         ],
         compiler_params=pltpu.CompilerParams(vmem_limit_bytes=VMEM_BYTES, collective_id=2, has_side_effects=True),
-        name="reduce_all",
-    )(g, w, mix, x_g, og_g, og, item_owner, item_owner.reshape(1, tokens), item_row.reshape(1, tokens))
+        name="grads",
+    )(
+        lens, acts["stats"], acts["h"], acts["gate"], acts["gsg"], acts["mg"], acts["q"], acts["kt"], acts["k"],
+        acts["v"], acts["w"], acts["sg"], acts["x"].reshape(pos, D),
+        og, item_owner, item_owner.reshape(1, tokens), item_row.reshape(1, tokens),
+    )
 
 
 def body(
@@ -588,12 +602,8 @@
     capacity = max(2, 2 * tokens_dev // devices)
     lens = lengths[0]
     acts = gather(lens, layer_input, out_grad, w_attn, w_gate, w_out, tokens_dev, seq_count, maxlen)
-    og_late, acts["mg"] = lax.optimization_barrier((out_grad, acts["mg"]))
-    og_g = lax.all_gather(og_late, "seq", axis=0, tiled=True)
-    g, mix = backward(lens, acts["stats"], acts["h"], acts, pos, maxlen, seq_count)
-    gw, go, send_rows = reduce_all(
-        g, acts["w"], mix, acts["x"].reshape(pos, D), og_g, out_grad, item_owner, item_row,
-        seq_count, dp_count, capacity, devices,
+    gw, go, send_rows = grads(
+        lens, acts, out_grad, item_owner, item_row, seq_count, dp_count, capacity, devices, maxlen
     )
     got = lax.all_to_all(send_rows.reshape(devices, capacity, D + 128), ("seq", "dp"), 0, 0, tiled=True)
     total = devices * capacity

time: 165 us -> 140 us (0.85)
  between operations: 14.1 us -> 0.71 us
  waiting for transfers between devices: 31.2 us -> 19.1 us
    all_gather x1 -> x0, waiting for transfers between devices: 12 us -> none  [body(): og_g = lax.all_gather(og_late, 'seq', axis=0, tiled=True)]
    pallas_call x2 -> x1, Pallas kernels: 58.4 us -> 57.9 us  [grads(): pl.pallas_call(functools.partial(grads_kernel, tokens, maxlen, dp_count,...]
  transfers between devices with their start and end apart: 2 -> 1, of which waited for: 2 -> 1; matrix products, arithmetic and copies ran while one was open for 1% -> 1% of each run, Pallas kernels for 12% -> 0%
where the time goes in v3:
time: 140 us; the launch traced here: 139 us
  Pallas kernels  99.1 us (71%)
  waiting for transfers between devices  19.1 us (14%)
  starting transfers between devices  10.1 us (7%)
  local copies, waits for them, and re-layouts  7.27 us (5%)
  other arithmetic  2.19 us (2%)
    pallas_call x1, Pallas kernels, grads(): pl.pallas_call(functools.partial(grads_kernel, tokens, maxlen, dp_count,...  57.9 us
    pallas_call x1, Pallas kernels, gather(): pl.pallas_call(functools.partial(gather_kernel, tokens, maxlen), out_shap...  41.1 us
    all_to_all x1, waiting for transfers between devices, body(): lax.all_to_all(send_rows.reshape(devices, capacity, D + 128), ('seq', 'dp...  19.1 us
    all_to_all x1, starting transfers between devices, body(): lax.all_to_all(send_rows.reshape(devices, capacity, D + 128), ('seq', 'dp...  10.1 us
    reshape x1, local copies, waits for them, and re-layouts, body(): send_rows.reshape(devices, capacity, D + 128)  3.26 us
  transfers between devices with their start and end apart: 1, of which 1 were waited for; matrix products, arithmetic and copies ran while one was open for 1% of the time, Pallas kernels for 0%

profile of v3, /device:TPU:0, one launch (start us, length us, event | category | flops | bytes accessed | tf_op | source)
XLA Modules:
  0.0 139.2 jit_solution(17716222727636418343)
XLA Ops:
  0.6 1.5 %copy.19.owner_col_ref = s32[256,1]{1,0:T(8,128)} copy(s32[256,1]{0,1:T(1,128)} %param.13) | data formatting | bytes 2048 | tf_op args[3]
  2.1 41.1 %gather.1 = (bf16[8,256,1024]{2,1,0:T(8,128)(2,1)}, bf16[1024,512]{1,0:T(8,128)(2,1)}, bf16[2,64,2048]{2,1,0:T(8,128)(2,1)}, bf16[2,64,2048]{2,1,0:T(8,128)(2,1)...) custom-call(s32[3]{0:T(128)} %bitcast.7, ...), custom_call_target="tpu_custom_call" | custom-call | tf_op jit(solution)/shard_map/gather/pallas_call | solution.py:266
  43.3 57.9 %grads.1 = (f32[64,512]{1,0:T(8,128)}, f32[64,128]{1,0:T(8,128)}, bf16[512,1152]{1,0:T(8,128)(2,1)}) custom-call(s32[3]{0:T(128)} %bitcast.8, f32[8,8,1024]{2,1,0:T(8,128)} %get-tuple-element.20.sta_ref, bf16[128,2048]{1,0:T(8,128)(2,1)} %get-tuple-element.21.h_ref, f32[128,2048]{1,0:T(8,128)} %get-tuple-element.22.gate_ref, ...), custom_call_target="tpu_custom_call" | custom-call | tf_op jit(solution)/shard_map/grads/pallas_call | solution.py:556
  101.2 0.0 copy-start.1
  101.2 3.3 %reshape.49 = bf16[128,4,1152]{2,1,0:T(4,128)(2,1)} reshape(bf16[512,1152]{1,0:T(8,128)(2,1)} %get-tuple-element.34) | data formatting | bytes 2359296 | tf_op jit(solution)/shard_map/reshape | solution.py:608
  104.5 10.1 %all-to-all-start = ((bf16[128,4,1152]{2,1,0:T(4,128)(2,1)}), bf16[128,4,1152]{2,1,0:T(4,128)(2,1)S(1)}, u32[]{:S(2)}, u32[]{:S(2)}) async-start(bf16[128,4,1152]{2,1,0:T(4,128)(2,1)} %reshape.49), calls=%async_computation | async-start | bytes 2359296 | tf_op jit(solution)/shard_map/all_to_all | solution.py:608
  114.5 0.0 copy-done.1
  114.5 0.6 slice.16
  115.2 0.6 slice.15
  115.8 19.1 %all-to-all-done = bf16[128,4,1152]{2,1,0:T(4,128)(2,1)S(1)} async-done(((bf16[128,4,1152]{2,1,0:T(4,128)(2,1)}), bf16[128,4,1152]{2,1,0:T(4,128)(2,1)S(1)}, u32[]{:S(2)}, u32[]{:S(2)}) %all-to-all-start) | async-done | bytes 1179680 | tf_op jit(solution)/shard_map/all_to_all | solution.py:608
  134.9 0.3 reshape.50
  135.2 0.1 fusion.3
  135.3 0.0 copy-start.3
  135.4 0.0 copy-start
  135.4 0.1 copy.22
  135.5 0.1 copy.23
  135.6 0.8 multiply_reduce_fusion
  136.4 0.0 copy-done.3
  136.4 0.6 rsqrt_multiply_fusion
  137.0 0.0 copy-done
  137.0 0.0 copy-start.2
  137.0 1.6 %multiply_subtract_fusion = f32[512,1024]{1,0:T(8,128)} fusion(f32[512,1024]{1,0:T(8,128)S(1)} %copy-done, f32[512,1024]{1,0:T(8,128)S(1)} %get-tuple-element.40, f32[512]{0:T(512)S(1)} %get-tuple-element.35), kind=kLoop, calls=%fused_computation | loop fusion | flops 1048576 | bytes 6293504 | tf_op jit(solution)/shard_map/sub | solution.py:616
  138.6 0.0 copy-done.2
  138.6 0.6 copy.25
  (1 shorter events, 0.0 us)
Async XLA Ops:
  101.2 13.3 %copy-start.1 = (f32[64,512]{1,0:T(8,128)S(1)}, f32[64,512]{1,0:T(8,128)}, u32[]{:S(2)}) copy-start(f32[64,512]{1,0:T(8,128)} %get-tuple-element.32) | copy-start | bytes 393220
  104.5 30.5 %all-to-all-start = ((bf16[128,4,1152]{2,1,0:T(4,128)(2,1)}), bf16[128,4,1152]{2,1,0:T(4,128)(2,1)S(1)}, u32[]{:S(2)}, u32[]{:S(2)}) async-start(bf16[128,4,1152]{2,1,0:T(4,128)(2,1)} %reshape.49), calls=%async_computation | async-start | bytes 2359296 | tf_op jit(solution)/shard_map/all_to_all | solution.py:608
  135.3 1.1 copy-start.3
  135.4 1.7 %copy-start = (f32[512,1024]{1,0:T(8,128)S(1)}, f32[512,1024]{1,0:T(8,128)}, u32[]{:S(2)}) copy-start(f32[512,1024]{1,0:T(8,128)} %param.18) | copy-start | bytes 6291460
  137.0 1.6 %copy-start.2 = (f32[64,128]{1,0:T(8,128)S(1)}, f32[64,128]{1,0:T(8,128)}, u32[]{:S(2)}) copy-start(f32[64,128]{1,0:T(8,128)} %get-tuple-element.48) | copy-start | bytes 98308

commit v4 on v3

--- a/solution.py
+++ b/solution.py
@@ -80,11 +80,11 @@
 
 def gather_kernel(
     tokens, maxlen,
-    len_ref, x_ref, og_ref, wa_hbm, wg_hbm, wo_hbm,
-    xg_ref, w_out, q_out, kt_out, k_out, v_out, sg_out, gate_out, gsg_out, mg_ref, h_ref, sta_ref,
+    len_ref, id_ref, x_ref, og_ref, wa_hbm, wg_hbm, wo_hbm,
+    xg_ref, w_out, q_out, kt_out, k_out, v_out, sg_out, gate_out, gsg_out, mg_ref, h_ref, sta_ref, idg_ref,
     w_s, q_s, kt_s, k_s, v_s, sg_s, gate_s, gsg_s,
     x_s, wt_s, wo_s, mine_s, vt_s, acc_s, st_s,
-    load_sem, keep_sem, send_sem, recv_sem, mg_send, mg_recv, st_send, st_recv,
+    load_sem, keep_sem, send_sem, recv_sem, mg_send, mg_recv, st_send, st_recv, id_send, id_recv,
 ):
     me, sib, right, left, far, c = seq_peers()
     z = me // 2
@@ -167,6 +167,10 @@
     to_right[1] = send(2, me, 1, right)
     to_left[0] = send(3, me, 0, left)
     to_sib = send(4, me, None, sib)
+    id_copies = []
+    for step in range(1, 8):
+        id_copies.append(remote(id_ref, idg_ref.at[me], id_send.at[step], id_recv.at[step], lax.rem(me + step, 8)))
+    idg_ref[me] = id_ref[...]
 
     loads[1].wait()
     loads[2].wait()
@@ -239,7 +243,7 @@
     for step in range(1, 8):
         st_copies.append(remote(st_s, sta_ref.at[me], st_send.at[step], st_recv.at[step], lax.rem(me + step, 8)))
     sta_ref[me] = st_s[...]
-    for copy in st_copies:
+    for copy in st_copies + id_copies:
         copy.wait()
 
     for copy in mg_copies + to_right + to_left + [to_sib, fwd_r, fwd_l, sib_left, sib_right, sib_far0, sib_far1]:
@@ -248,7 +252,7 @@
         copy.wait()
 
 
-def gather(lens, x, og, w_attn, w_gate, w_out, tokens, seq_count, maxlen):
+def gather(lens, ids, x, og, w_attn, w_gate, w_out, tokens, seq_count, maxlen):
     pos = tokens * seq_count
     hbm = pl.BlockSpec(memory_space=pl.ANY)
     kept = [
@@ -261,7 +265,7 @@
         ((2 * DH, pos), F32),
         ((2 * DH, pos), F32),
     ]
-    names = ("x", "w", "q", "kt", "k", "v", "sg", "gate", "gsg", "mg", "h", "stats")
+    names = ("x", "w", "q", "kt", "k", "v", "sg", "gate", "gsg", "mg", "h", "stats", "ids")
     dma = lambda n: pltpu.SemaphoreType.DMA((n,))
     outs = pl.pallas_call(
         functools.partial(gather_kernel, tokens, maxlen),
@@ -272,10 +276,11 @@
                 jax.ShapeDtypeStruct((2 * DH, pos), BF),
                 jax.ShapeDtypeStruct((2 * DH, pos), BF),
                 jax.ShapeDtypeStruct((seq_count, 8, pos // 2), F32),
+                jax.ShapeDtypeStruct((seq_count,) + ids.shape, jnp.int32),
             ]
         ),
-        in_specs=[pl.BlockSpec(memory_space=pltpu.SMEM), hbm] + vmem(1) + [hbm] * 3,
-        out_specs=tuple([hbm] * 9 + vmem(3)),
+        in_specs=[pl.BlockSpec(memory_space=pltpu.SMEM)] + vmem(1) + [hbm] + vmem(1) + [hbm] * 3,
+        out_specs=tuple([hbm] * 9 + vmem(4)),
         scratch_shapes=[pltpu.VMEM(shape, dtype) for shape, dtype in kept]
         + [
             pltpu.VMEM((seq_count, tokens, D), BF),
@@ -285,26 +290,26 @@
             pltpu.VMEM((2, DH, pos), BF),
             pltpu.VMEM((2, DH, pos), F32),
             pltpu.VMEM((8, pos // 2), F32),
-            dma(4), dma(16), dma(11), dma(11), dma(8), dma(8), dma(8), dma(8),
+            dma(4), dma(16), dma(11), dma(11), dma(8), dma(8), dma(8), dma(8), dma(8), dma(8),
         ],
         compiler_params=pltpu.CompilerParams(
             vmem_limit_bytes=VMEM_BYTES, collective_id=0, has_side_effects=True
         ),
         name="gather",
-    )(lens, x, og, w_attn, w_gate, w_out)
+    )(lens, ids, x, og, w_attn, w_gate, w_out)
     return dict(zip(names, outs))
 
 
 def grads_kernel(
-    tokens, maxlen, dp_count, capacity,
+    tokens, maxlen, dp_count,
     len_ref, sta_ref, h_ref, gate_ref, gsg_ref, mg_ref, q_ref, kt_ref, k_ref, v_ref, w_ref, sg_hbm, x_hbm,
-    og_ref, owner_col_ref, owner_row_ref, row_ref,
-    gsum_ref, gosum_ref, send_ref,
+    og_ref, id_ref,
+    gattn_ref, ggate_ref, gosum_ref, tot_ref, idall_ref,
     sg_s, x_s, mix_s, ot_s, dv_s, dk_s, dq_s, g_s, gacc_s,
     out_s, pair_s, sum_s, far_s, ring_s,
-    mixr_s, gop_s, gopair_s, gosum_s, gor_s, goout_s, gocol_s, gsrc_s, gw_s,
+    mixr_s, gop_s, gopair_s, gosum_s, gor_s, goout_s, gocol_s, gsrc_s, gw_s, gtsrc_s, gt_s,
     load_sem, mix_send, mix_recv, pair_send, pair_recv, ring_send, ring_recv,
-    gp_send, gp_recv, go_send, go_recv, gc_send, gc_recv, gw_send, gw_recv,
+    gp_send, gp_recv, go_send, go_recv, gc_send, gc_recv, gw_send, gw_recv, id_send, id_recv, gt_send, gt_recv,
 ):
     me, sib, right, left, _, c = seq_peers()
     z = me // 2
@@ -375,7 +380,22 @@
             mix_s.at[:, pl.ds(pl.multiple_of(to * tokens, tokens), tokens)], mixr_s.at[feats],
             mix_send.at[step], mix_recv.at[step], {"seq": to},
         ))
+    id_copies = []
+    for step in range(1, dp_count):
+        to = lax.rem(dp + step, dp_count)
+        id_copies.append(remote(id_ref, idall_ref.at[dp], id_send.at[step], id_recv.at[step], {"dp": to}))
+    idall_ref[dp] = id_ref[...]
     mixr_s[feats, :] = mix_s[:, pl.ds(pl.multiple_of(me * tokens, tokens), tokens)]
+    x_load.wait()
+    gtsrc_s[...] = mm(g_s[6 * DH :, :], x_s[...]).astype(BF).T
+    gates = []
+    for step in range(1, dp_count):
+        to = lax.rem(dp + step, dp_count)
+        gates.append(remote(
+            gtsrc_s.at[pl.ds(pl.multiple_of(to * block, block), block)], gt_s.at[dp],
+            gt_send.at[step], gt_recv.at[step], {"dp": to},
+        ))
+    gt_s[dp] = gtsrc_s[pl.ds(pl.multiple_of(dp * block, block), block), :]
 
     def chip_block(k):
         return lax.rem(z + k, 4)
@@ -426,7 +446,7 @@
         out_s[k] = partial_grad(k, 1 - c).astype(BF)
         pairs[k] = remote(out_s.at[k], pair_s.at[k], pair_send.at[k], pair_recv.at[k], {"seq": sib})
         at = lanes_of(chip_block(k))
-        part = mm(g_s[:, at], x_s[at, :])
+        part = mm(g_s[: 6 * DH, at], x_s[at, :])
         gacc_s[...] = part if k == 2 else gacc_s[...] + part
 
     low, high = pl.ds(0, half), pl.ds(half, half)
@@ -446,23 +466,16 @@
 
     sg_load.wait()
     attend(0)
-    x_load.wait()
-    share(2)
-    settle(2)
-    hops[0].start()
-    hops[1].start()
-
     for copy in mixes:
         copy.wait_recv()
     gop_s[...] = mm(mixr_s[...], og_ref[...]).astype(BF).reshape(dp_count, block, D)
     mine = pl.ds(pl.multiple_of(c * hb, hb), hb)
     theirs = pl.ds(pl.multiple_of((1 - c) * hb, hb), hb)
     go_pair = remote(gop_s.at[:, theirs], gopair_s, gp_send.at[0], gp_recv.at[0], {"seq": sib})
-
-    attend(1)
-    share(1)
-    settle(1)
-    hops[2].start()
+    share(2)
+    settle(2)
+    hops[0].start()
+    hops[1].start()
     go_pair.wait_recv()
     gosum_s[...] = (gop_s[:, mine, :].astype(F32) + gopair_s[...].astype(F32)).astype(BF)
     gos = []
@@ -470,6 +483,11 @@
         to = lax.rem(dp + step, dp_count)
         gos.append(remote(gosum_s.at[to], gor_s.at[dp], go_send.at[step], go_recv.at[step], {"dp": to}))
     gor_s[dp] = gosum_s[dp]
+
+    attend(1)
+    share(1)
+    settle(1)
+    hops[2].start()
     hops[0].wait_recv()
     sum_s[1, low] = (sum_s[1, low].astype(F32) + far_s[0].astype(F32)).astype(BF)
     hops[4].start()
@@ -494,18 +512,6 @@
         ))
     gw_s[dp] = gsrc_s[pl.ds(pl.multiple_of(dp * block, block), block), :]
     settle(0)
-
-    earlier = (lax.broadcasted_iota(jnp.int32, (tokens, tokens), 0) < lax.broadcasted_iota(jnp.int32, (tokens, tokens), 1))
-    same = owner_col_ref[...] == owner_row_ref[...]
-    rank = jnp.sum(jnp.where(earlier & same, 1.0, 0.0), axis=0, keepdims=True).astype(jnp.int32)
-    slot = owner_row_ref[...] * capacity + rank
-    total = send_ref.shape[0]
-    hit = lax.broadcasted_iota(jnp.int32, (total, tokens), 0) == slot
-    ident = jnp.sum(jnp.where(hit, (row_ref[...] + 1).astype(F32), 0.0), axis=1, keepdims=True).astype(jnp.int32)
-    lanes = lax.broadcasted_iota(jnp.int32, (total, 128), 1)
-    code = jnp.where(lanes == 0, ident // 32, jnp.where(lanes == 1, ident % 32, 0))
-    send_ref[:, D:] = code.astype(F32).astype(BF)
-    place = jnp.where(hit, 1.0, 0.0).astype(BF)
 
     for copy in gos:
         copy.wait_recv()
@@ -524,8 +530,7 @@
 
     for hop in hops[2:]:
         hop.wait_recv()
-    total_grad = (sum_s[0].astype(F32) + ring_s[0].astype(F32) + ring_s[1].astype(F32)).astype(BF)
-    send_ref[:, :D] = (mm(place, total_grad, NT) + mm(place, og_ref[...])).astype(BF)
+    tot_ref[...] = (sum_s[0].astype(F32) + ring_s[0].astype(F32) + ring_s[1].astype(F32)).astype(BF)
 
     for copy in cols:
         copy.wait_recv()
@@ -539,13 +544,21 @@
     acc = gw_s[0].astype(F32)
     for d in range(1, dp_count):
         acc = acc + gw_s[d].astype(F32)
-    gsum_ref[...] = acc
-
-    for copy in mixes + list(pairs.values()) + hops + [go_pair] + gos + cols + blocks:
+    gattn_ref[...] = acc
+    for copy in gates:
+        copy.wait_recv()
+    acc = gt_s[0].astype(F32)
+    for d in range(1, dp_count):
+        acc = acc + gt_s[d].astype(F32)
+    ggate_ref[...] = acc
+
+    for copy in id_copies:
+        copy.wait_recv()
+    for copy in id_copies + gates + mixes + list(pairs.values()) + hops + [go_pair] + gos + cols + blocks:
         copy.wait_send()
 
 
-def grads(lens, acts, og, item_owner, item_row, seq_count, dp_count, capacity, devices, maxlen):
+def grads(lens, acts, og, seq_count, dp_count, maxlen):
     tokens = og.shape[0]
     pos = tokens * seq_count
     hbm = pl.BlockSpec(memory_space=pl.ANY)
@@ -554,31 +567,173 @@
     f32 = lambda *shape: pltpu.VMEM(shape, F32)
     dma = lambda n: pltpu.SemaphoreType.DMA((n,))
     return pl.pallas_call(
-        functools.partial(grads_kernel, tokens, maxlen, dp_count, capacity),
+        functools.partial(grads_kernel, tokens, maxlen, dp_count),
         out_shape=(
-            jax.ShapeDtypeStruct((block, 8 * DH), F32),
+            jax.ShapeDtypeStruct((block, 6 * DH), F32),
             jax.ShapeDtypeStruct((block, 2 * DH), F32),
-            jax.ShapeDtypeStruct((devices * capacity, D + 128), BF),
+            jax.ShapeDtypeStruct((block, 2 * DH), F32),
+            jax.ShapeDtypeStruct((D, tokens), BF),
+            jax.ShapeDtypeStruct((dp_count,) + acts["ids"].shape, jnp.int32),
         ),
-        in_specs=[pl.BlockSpec(memory_space=pltpu.SMEM)] + vmem(10) + [hbm] * 2 + vmem(4),
-        out_specs=tuple(vmem(3)),
+        in_specs=[pl.BlockSpec(memory_space=pltpu.SMEM)] + vmem(10) + [hbm] * 2 + vmem(2),
+        out_specs=tuple(vmem(5)),
         scratch_shapes=[
             f32(6 * DH, pos), bf(pos, D), bf(2 * DH, pos), bf(2, DH, pos),
-            f32(2, DH, pos), f32(2, DH, pos), f32(2, DH, pos), bf(8 * DH, pos), f32(8 * DH, D),
+            f32(2, DH, pos), f32(2, DH, pos), f32(2, DH, pos), bf(8 * DH, pos), f32(6 * DH, D),
             bf(4, D, tokens), bf(4, D, tokens), bf(4, D, tokens), bf(2, D // 2, tokens), bf(2, D, tokens),
             bf(D, tokens), bf(dp_count, block, D), bf(dp_count, block // 2, D), bf(dp_count, block // 2, D),
             bf(dp_count, block // 2, D), bf(block // 2, D), bf(seq_count, block // 2, 2 * DH),
-            bf(D, 8 * DH), bf(dp_count, block, 8 * DH),
+            bf(D, 6 * DH), bf(dp_count, block, 6 * DH), bf(D, 2 * DH), bf(dp_count, block, 2 * DH),
             dma(2), dma(seq_count), dma(seq_count), dma(4), dma(4), dma(6), dma(6),
-            dma(1), dma(1), dma(dp_count), dma(dp_count), dma(seq_count), dma(seq_count), dma(dp_count), dma(dp_count),
+            dma(1), dma(1), dma(dp_count), dma(dp_count), dma(seq_count), dma(seq_count), dma(dp_count), dma(dp_count), dma(dp_count), dma(dp_count), dma(dp_count), dma(dp_count),
         ],
         compiler_params=pltpu.CompilerParams(vmem_limit_bytes=VMEM_BYTES, collective_id=2, has_side_effects=True),
         name="grads",
     )(
         lens, acts["stats"], acts["h"], acts["gate"], acts["gsg"], acts["mg"], acts["q"], acts["kt"], acts["k"],
         acts["v"], acts["w"], acts["sg"], acts["x"].reshape(pos, D),
-        og, item_owner, item_owner.reshape(1, tokens), item_row.reshape(1, tokens),
+        og, acts["ids"],
     )
+
+
+def route_kernel(
+    dp_count, devices, capacity,
+    tot_ref, og_ref, owner_col_ref, owner_row_ref,
+    got_ref,
+    wide_s, msg_s, send_sem, recv_sem,
+):
+    tokens = og_ref.shape[0]
+    me = lax.axis_index("seq") * dp_count + lax.axis_index("dp")
+    lines = D // 128
+    barrier = pltpu.get_barrier_semaphore()
+
+    def place_of(step):
+        to = lax.rem(me + step, devices)
+        return to, {"seq": to // dp_count, "dp": lax.rem(to, dp_count)}
+
+    def greet(step, carry):
+        pl.semaphore_signal(barrier, inc=1, device_id=place_of(step)[1], device_id_type=MESH)
+        return carry
+
+    lax.fori_loop(1, devices, greet, 0)
+    earlier = (lax.broadcasted_iota(jnp.int32, (tokens, tokens), 0) < lax.broadcasted_iota(jnp.int32, (tokens, tokens), 1))
+    same = owner_col_ref[...] == owner_row_ref[...]
+    rank = jnp.sum(jnp.where(earlier & same, 1.0, 0.0), axis=0, keepdims=True).astype(jnp.int32)
+    named = lax.broadcasted_iota(jnp.int32, (devices, tokens), 0) == owner_row_ref[...]
+    for slot in range(capacity):
+        place = jnp.where(named & (rank == slot), 1.0, 0.0).astype(BF)
+        rows = mm(place, tot_ref[...], NT) + mm(place, og_ref[...])
+        for line in range(lines):
+            wide_s[pl.ds(slot * lines + line, devices, stride=capacity * lines), :] = rows[:, line * 128 : (line + 1) * 128]
+    msg_s[...] = wide_s[...].astype(BF).reshape(msg_s.shape)
+    mine = lax.axis_index("dp") * (devices // dp_count) + lax.axis_index("seq")
+    got_ref[mine] = msg_s[me]
+    pl.semaphore_wait(barrier, devices - 1)
+
+    def push(step, carry):
+        to, where = place_of(step)
+        pltpu.make_async_remote_copy(
+            src_ref=msg_s.at[to], dst_ref=got_ref.at[mine], send_sem=send_sem, recv_sem=recv_sem,
+            device_id=where, device_id_type=MESH,
+        ).start()
+        return carry
+
+    lax.fori_loop(1, devices, push, 0)
+    others = pl.ds(0, devices - 1)
+    pltpu.make_async_copy(msg_s.at[others], got_ref.at[others], recv_sem).wait()
+    pltpu.make_async_copy(msg_s.at[others], got_ref.at[others], send_sem).wait()
+
+
+def route(tot, og, item_owner, dp_count, devices, capacity):
+    tokens = og.shape[0]
+    lines = capacity * D // 128
+    return pl.pallas_call(
+        functools.partial(route_kernel, dp_count, devices, capacity),
+        out_shape=jax.ShapeDtypeStruct((devices, lines, 128), BF),
+        in_specs=vmem(4),
+        out_specs=vmem(1)[0],
+        scratch_shapes=[
+            pltpu.VMEM((devices * lines, 128), F32),
+            pltpu.VMEM((devices, lines, 128), BF),
+            pltpu.SemaphoreType.DMA,
+            pltpu.SemaphoreType.DMA,
+        ],
+        compiler_params=pltpu.CompilerParams(
+            vmem_limit_bytes=VMEM_BYTES, collective_id=3, has_side_effects=True
+        ),
+        name="route",
+    )(tot, og, item_owner, item_owner.reshape(1, tokens))
+
+
+def update_kernel(
+    capacity, devices,
+    got_ref, ids_ref, me_ref, accum_ref, gattn_ref, ggate_ref, go_ref, tab_hbm,
+    gattn_out, ggate_out, go_out, tab_out, accum_out,
+    wide_s, rows_s, tab_ref, load_sem, keep_sem,
+):
+    lines = D // 128
+    load = pltpu.make_async_copy(tab_hbm, tab_ref, load_sem)
+    load.start()
+    gattn_out[...] = gattn_ref[...]
+    ggate_out[...] = ggate_ref[...]
+    go_out[...] = go_ref[...]
+    tokens = ids_ref.shape[1] // 2
+    rows_own = tab_ref.shape[0]
+    wide_s[...] = got_ref[...].astype(F32).reshape(wide_s.shape)
+    hit = ids_ref[:, :tokens] == me_ref[0]
+    hit_f = jnp.where(hit, 1.0, 0.0)
+    before = lax.broadcasted_iota(jnp.int32, (tokens, tokens), 0) < lax.broadcasted_iota(jnp.int32, (tokens, tokens), 1)
+    rank = mm(hit_f.astype(BF), jnp.where(before, 1.0, 0.0).astype(BF))
+    row = (ids_ref[:, tokens:] + 1).astype(F32)
+    eye = lax.broadcasted_iota(jnp.int32, (128, 128), 0) == lax.broadcasted_iota(jnp.int32, (128, 128), 1)
+    grad = jnp.zeros((rows_own, D), F32)
+    for slot in range(capacity):
+        name = jnp.sum(jnp.where(hit & (rank == float(slot)), row, 0.0), axis=1, keepdims=True)
+        name = jnp.sum(jnp.where(eye, name, 0.0), axis=0, keepdims=True) - 1.0
+        pick = jnp.where(lax.broadcasted_iota(jnp.int32, (rows_own, devices), 0).astype(F32) == name, 1.0, 0.0).astype(BF)
+        for line in range(lines):
+            rows_s[:, line * 128 : (line + 1) * 128] = wide_s[
+                pl.ds(slot * lines + line, devices, stride=capacity * lines), :
+            ].astype(BF)
+        grad = grad + mm(pick, rows_s[...])
+    load.wait()
+    keeps = []
+    square = jnp.sum(grad * grad, axis=1, keepdims=True) * (1.0 / D)
+    for part in range(rows_own // 128):
+        at = slice(part * 128, (part + 1) * 128)
+        old = jnp.sum(jnp.where(eye, accum_ref[part : part + 1, :], 0.0), axis=1, keepdims=True)
+        new = old + square[at]
+        tab_ref[at, :] = tab_ref[at, :] - LEARN_RATE * grad[at] * lax.rsqrt(new)
+        keep = pltpu.make_async_copy(tab_ref.at[at], tab_out.at[at], keep_sem.at[part])
+        keep.start()
+        keeps.append(keep)
+        accum_out[part : part + 1, :] = jnp.sum(jnp.where(eye, new, 0.0), axis=0, keepdims=True)
+    for keep in keeps:
+        keep.wait()
+
+
+def update(got, ids, me, table, accum, gattn, ggate, go, capacity, devices):
+    rows_own = table.shape[0]
+    lines = capacity * D // 128
+    like = lambda a: jax.ShapeDtypeStruct(a.shape, a.dtype)
+    hbm = pl.BlockSpec(memory_space=pl.ANY)
+    accum = accum.reshape(rows_own // 128, 128)
+    gattn, ggate, go, table, accum = pl.pallas_call(
+        functools.partial(update_kernel, capacity, devices),
+        out_shape=(like(gattn), like(ggate), like(go), like(table), like(accum)),
+        in_specs=vmem(2) + [pl.BlockSpec(memory_space=pltpu.SMEM)] + vmem(4) + [hbm],
+        out_specs=tuple(vmem(3) + [hbm] + vmem(1)),
+        scratch_shapes=[
+            pltpu.VMEM((devices * lines, 128), F32),
+            pltpu.VMEM((devices, D), BF),
+            pltpu.VMEM((rows_own, D), F32),
+            pltpu.SemaphoreType.DMA,
+            pltpu.SemaphoreType.DMA((rows_own // 128,)),
+        ],
+        compiler_params=pltpu.CompilerParams(vmem_limit_bytes=VMEM_BYTES),
+        name="update",
+    )(got, ids, me.reshape(1), accum, gattn, ggate, go, table)
+    return gattn, ggate, go, table, accum.reshape(rows_own)
 
 
 def body(
@@ -601,20 +756,13 @@
     maxlen = 2 * pos // 3
     capacity = max(2, 2 * tokens_dev // devices)
     lens = lengths[0]
-    acts = gather(lens, layer_input, out_grad, w_attn, w_gate, w_out, tokens_dev, seq_count, maxlen)
-    gw, go, send_rows = grads(
-        lens, acts, out_grad, item_owner, item_row, seq_count, dp_count, capacity, devices, maxlen
-    )
-    got = lax.all_to_all(send_rows.reshape(devices, capacity, D + 128), ("seq", "dp"), 0, 0, tiled=True)
-    total = devices * capacity
-    got = got.reshape(total, D + 128)
-    got_ids = (got[:, D].astype(F32) * 32.0 + got[:, D + 1].astype(F32)).astype(jnp.int32) - 1
-    rows_own = emb_table.shape[0]
-    pick = (jnp.arange(rows_own, dtype=jnp.int32)[:, None] == got_ids[None, :]).astype(BF)
-    table_grad = mm(pick, got[:, :D])
-    new_accum = row_accum + jnp.mean(table_grad * table_grad, axis=1)
-    new_table = emb_table - LEARN_RATE * table_grad * lax.rsqrt(new_accum)[:, None]
-    return (gw[:, : 6 * DH], gw[:, 6 * DH :], go, new_table, new_accum)
+    ids = jnp.concatenate([item_owner.reshape(1, tokens_dev), item_row.reshape(1, tokens_dev)], axis=1)
+    acts = gather(lens, ids, layer_input, out_grad, w_attn, w_gate, w_out, tokens_dev, seq_count, maxlen)
+    gattn, ggate, go, tot, ids = grads(lens, acts, out_grad, seq_count, dp_count, maxlen)
+    got = route(tot, out_grad, item_owner, dp_count, devices, capacity)
+    me = lax.axis_index("seq") * dp_count + lax.axis_index("dp")
+    ids = ids.reshape(devices, 2 * tokens_dev)
+    return update(got, ids, me, emb_table, row_accum, gattn, ggate, go, capacity, devices)
 
 
 def solution(mesh):

time: 140 us -> 134 us (0.957)
  Pallas kernels: 99.1 us -> 129 us
  waiting for transfers between devices: 19.1 us -> 0 us
  starting transfers between devices: 10.1 us -> 0 us
  local copies, waits for them, and re-layouts: 7.27 us -> 1.53 us
    pallas_call x1 -> x3, Pallas kernels: 57.9 us -> 87.3 us  [the longest x1 54.9 us: grads(): pl.pallas_call(functools.partial(grads_kernel, tokens, maxlen, dp_count),...]
    all_to_all x1 -> x0, waiting for transfers between devices: 19.1 us -> none  [body(): lax.all_to_all(send_rows.reshape(devices, capacity, D + 128), ('seq', 'dp...]
    all_to_all x1 -> x0, starting transfers between devices: 10.1 us -> none  [body(): lax.all_to_all(send_rows.reshape(devices, capacity, D + 128), ('seq', 'dp...]
    reshape x2 -> x0, local copies, waits for them, and re-layouts: 3.55 us -> none  [the longest x1 3.26 us: body(): send_rows.reshape(devices, capacity, D + 128)]
    sub x2 -> x0, other arithmetic: 1.61 us -> none  [the longest x1 1.59 us: body(): emb_table - LEARN_RATE * table_grad * lax.rsqrt(new_accum)[:, None]]
  transfers between devices with their start and end apart: 1 -> 0, of which waited for: 1 -> 0; matrix products, arithmetic and copies ran while one was open for 1% -> 0% of each run, Pallas kernels for 0% -> 0%
where the time goes in v4:
time: 134 us; the launch traced here: 132 us
  Pallas kernels  129 us (96%)
  local copies, waits for them, and re-layouts  1.53 us (1%)
    pallas_call x1, Pallas kernels, grads(): pl.pallas_call(functools.partial(grads_kernel, tokens, maxlen, dp_count),...  54.9 us
    pallas_call x1, Pallas kernels, gather(): pl.pallas_call(functools.partial(gather_kernel, tokens, maxlen), out_shap...  41.4 us
    pallas_call x1, Pallas kernels, route(): pl.pallas_call(functools.partial(route_kernel, dp_count, devices, capacit...  26 us
    pallas_call x1, Pallas kernels, update(): pl.pallas_call(functools.partial(update_kernel, capacity, devices), out_s...  6.31 us

profile of v4, /device:TPU:0, one launch (start us, length us, event | category | flops | bytes accessed | tf_op | source)
XLA Modules:
  0.0 132.3 jit_solution(5360275272819128930)
XLA Ops:
  0.6 1.3 pad_add_fusion.id_ref
  1.9 41.4 %gather.1 = (bf16[8,256,1024]{2,1,0:T(8,128)(2,1)}, bf16[1024,512]{1,0:T(8,128)(2,1)}, bf16[2,64,2048]{2,1,0:T(8,128)(2,1)}, bf16[2,64,2048]{2,1,0:T(8,128)(2,1)...) custom-call(s32[3]{0:T(128)} %bitcast.15, ...), custom_call_target="tpu_custom_call" | custom-call | tf_op jit(solution)/shard_map/gather/pallas_call | solution.py:270
  43.3 0.0 copy-start.1
  43.3 54.9 %grads.1 = (f32[64,384]{1,0:T(8,128)}, f32[64,128]{1,0:T(8,128)}, f32[64,128]{1,0:T(8,128)}, bf16[1024,256]{1,0:T(8,128)(2,1)}, s32[16,8,1,512]{3,2,1,0:T(1,128)}) custom-call(s32[3]{0:T(128)} %bitcast.16, f32[8,8,1024]{2,1,0:T(8,128)} %get-tuple-element.28.sta_ref, bf16[128,2048]{1,0:T(8,128)(2,1)} %get-tuple-element.29.h_ref, ...), custom_call_target="tpu_custom_call" | custom-call | tf_op jit(solution)/shard_map/grads/pallas_call | solution.py:569
  98.3 0.0 copy-start
  98.3 0.0 copy-done.1
  98.3 0.8 copy.15.owner_col_ref
  99.1 26.0 %route.1.got_ref = bf16[128,32,128]{2,1,0:T(8,128)(2,1)} custom-call(bf16[1024,256]{1,0:T(8,128)(2,1)} %get-tuple-element.41.tot_ref, bf16[256,1024]{1,0:T(8,128)(2,1)} %og_ref.5, s32[256,1]{1,0:T(8,128)} %copy.15.owner_col_ref, s32[1,256]{1,0:T(1,128)} %bitcast.13), custom_call_target="tpu_custom_call" | custom-call | tf_op jit(solution)/shard_map/route/pallas_call | solution.py:650
  125.1 0.0 copy-done
  125.1 0.7 copy.18
  125.8 6.3 %update.1 = (f32[64,384]{1,0:T(8,128)}, f32[64,128]{1,0:T(8,128)}, f32[64,128]{1,0:T(8,128)}, f32[512,1024]{1,0:T(8,128)}, f32[4,128]{1,0:T(4,128)}) custom-call(bf16[128,32,128]{2,1,0:T(8,128)(2,1)} %route.1.got_ref, s32[128,512]{1,0:T(8,128)} %bitcast.11, s32[1]{0:T(128)} %bitcast.4.me_ref, f32[4,128]{1,0:T(4,128)} %bitcast.14, ...), custom_call_target="tpu_custom_call" | custom-call | tf_op jit(solution)/shard_map/update/pallas_call | solution.py:721
Async XLA Ops:
  43.3 55.0 %copy-start.1 = (s32[256,1]{0,1:T(1,128)S(1)}, s32[256,1]{0,1:T(1,128)}, u32[]{:S(2)}) copy-start(s32[256,1]{0,1:T(1,128)} %param.13) | copy-start | bytes 3076
  98.3 26.8 %copy-start = (s32[16,8,1,512]{3,2,1,0:T(1,128)S(1)}, s32[16,8,1,512]{3,2,1,0:T(1,128)}, u32[]{:S(2)}) copy-start(s32[16,8,1,512]{3,2,1,0:T(1,128)} %get-tuple-element.42) | copy-start | bytes 786436

commit v5 on v4

--- a/solution.py
+++ b/solution.py
@@ -301,15 +301,15 @@
 
 
 def grads_kernel(
-    tokens, maxlen, dp_count,
+    tokens, maxlen, dp_count, capacity,
     len_ref, sta_ref, h_ref, gate_ref, gsg_ref, mg_ref, q_ref, kt_ref, k_ref, v_ref, w_ref, sg_hbm, x_hbm,
-    og_ref, id_ref,
-    gattn_ref, ggate_ref, gosum_ref, tot_ref, idall_ref,
+    og_ref, id_ref, owner_col_ref, owner_row_ref,
+    gattn_ref, ggate_ref, gosum_ref, got_ref, idall_ref,
     sg_s, x_s, mix_s, ot_s, dv_s, dk_s, dq_s, g_s, gacc_s,
     out_s, pair_s, sum_s, far_s, ring_s,
-    mixr_s, gop_s, gopair_s, gosum_s, gor_s, goout_s, gocol_s, gsrc_s, gw_s, gtsrc_s, gt_s,
+    mixr_s, gop_s, gopair_s, gosum_s, gor_s, goout_s, gocol_s, gsrc_s, gw_s, gtsrc_s, gt_s, place_s, wide_s, msg_s,
     load_sem, mix_send, mix_recv, pair_send, pair_recv, ring_send, ring_recv,
-    gp_send, gp_recv, go_send, go_recv, gc_send, gc_recv, gw_send, gw_recv, id_send, id_recv, gt_send, gt_recv,
+    gp_send, gp_recv, go_send, go_recv, gc_send, gc_recv, gw_send, gw_recv, id_send, id_recv, gt_send, gt_recv, row_send, row_recv,
 ):
     me, sib, right, left, _, c = seq_peers()
     z = me // 2
@@ -326,10 +326,18 @@
     sg_load.start()
     x_load.start()
     barrier = pltpu.get_barrier_semaphore()
-    for step in range(1, seq_count):
-        pl.semaphore_signal(barrier, inc=1, device_id={"seq": lax.rem(me + step, seq_count)}, device_id_type=MESH)
-    for step in range(1, dp_count):
-        pl.semaphore_signal(barrier, inc=1, device_id={"dp": lax.rem(dp + step, dp_count)}, device_id_type=MESH)
+    devices = seq_count * dp_count
+    here = me * dp_count + dp
+
+    def place_of(step):
+        to = lax.rem(here + step, devices)
+        return to, {"seq": to // dp_count, "dp": lax.rem(to, dp_count)}
+
+    def greet(step, carry):
+        pl.semaphore_signal(barrier, inc=1, device_id=place_of(step)[1], device_id_type=MESH)
+        return carry
+
+    lax.fori_loop(1, devices, greet, 0)
 
     def describe(src, dst, send_sem, recv_sem, to):
         return pltpu.make_async_remote_copy(
@@ -371,7 +379,7 @@
     dq_s[...] = jnp.zeros_like(dq_s)
     fac = 0.0625 / maxlen
 
-    pl.semaphore_wait(barrier, seq_count - 1 + dp_count - 1)
+    pl.semaphore_wait(barrier, devices - 1)
     feats = pl.ds(pl.multiple_of(me * 2 * DH, 2 * DH), 2 * DH)
     mixes = []
     for step in range(1, seq_count):
@@ -513,6 +521,13 @@
     gw_s[dp] = gsrc_s[pl.ds(pl.multiple_of(dp * block, block), block), :]
     settle(0)
 
+    earlier = (lax.broadcasted_iota(jnp.int32, (tokens, tokens), 0) < lax.broadcasted_iota(jnp.int32, (tokens, tokens), 1))
+    same = owner_col_ref[...] == owner_row_ref[...]
+    rank = jnp.sum(jnp.where(earlier & same, 1.0, 0.0), axis=0, keepdims=True).astype(jnp.int32)
+    named = lax.broadcasted_iota(jnp.int32, (devices, tokens), 0) == owner_row_ref[...]
+    for slot in range(capacity):
+        place_s[slot] = jnp.where(named & (rank == slot), 1.0, 0.0).astype(BF)
+
     for copy in gos:
         copy.wait_recv()
     acc = gor_s[0].astype(F32)
@@ -530,7 +545,25 @@
 
     for hop in hops[2:]:
         hop.wait_recv()
-    tot_ref[...] = (sum_s[0].astype(F32) + ring_s[0].astype(F32) + ring_s[1].astype(F32)).astype(BF)
+    total = (sum_s[0].astype(F32) + ring_s[0].astype(F32) + ring_s[1].astype(F32)).astype(BF)
+    lines = D // 128
+    for slot in range(capacity):
+        rows = mm(place_s[slot], total, NT) + mm(place_s[slot], og_ref[...])
+        for line in range(lines):
+            wide_s[pl.ds(slot * lines + line, devices, stride=capacity * lines), :] = rows[:, line * 128 : (line + 1) * 128]
+    msg_s[...] = wide_s[...].astype(BF).reshape(msg_s.shape)
+    source = dp * seq_count + me
+
+    def push(step, carry):
+        to, where = place_of(step)
+        pltpu.make_async_remote_copy(
+            src_ref=msg_s.at[to], dst_ref=got_ref.at[source], send_sem=row_send, recv_sem=row_recv,
+            device_id=where, device_id_type=MESH,
+        ).start()
+        return carry
+
+    lax.fori_loop(1, devices, push, 0)
+    got_ref[source] = msg_s[here]
 
     for copy in cols:
         copy.wait_recv()
@@ -554,12 +587,17 @@
 
     for copy in id_copies:
         copy.wait_recv()
+    others = pl.ds(0, devices - 1)
+    pltpu.make_async_copy(msg_s.at[others], got_ref.at[others], row_recv).wait()
+    pltpu.make_async_copy(msg_s.at[others], got_ref.at[others], row_send).wait()
     for copy in id_copies + gates + mixes + list(pairs.values()) + hops + [go_pair] + gos + cols + blocks:
         copy.wait_send()
 
 
-def grads(lens, acts, og, seq_count, dp_count, maxlen):
+def grads(lens, acts, og, item_owner, seq_count, dp_count, capacity, maxlen):
     tokens = og.shape[0]
+    devices = seq_count * dp_count
+    lines = capacity * D // 128
     pos = tokens * seq_count
     hbm = pl.BlockSpec(memory_space=pl.ANY)
     block = D // dp_count
@@ -567,15 +605,15 @@
     f32 = lambda *shape: pltpu.VMEM(shape, F32)
     dma = lambda n: pltpu.SemaphoreType.DMA((n,))
     return pl.pallas_call(
-        functools.partial(grads_kernel, tokens, maxlen, dp_count),
+        functools.partial(grads_kernel, tokens, maxlen, dp_count, capacity),
         out_shape=(
             jax.ShapeDtypeStruct((block, 6 * DH), F32),
             jax.ShapeDtypeStruct((block, 2 * DH), F32),
             jax.ShapeDtypeStruct((block, 2 * DH), F32),
-            jax.ShapeDtypeStruct((D, tokens), BF),
+            jax.ShapeDtypeStruct((devices, lines, 128), BF),
             jax.ShapeDtypeStruct((dp_count,) + acts["ids"].shape, jnp.int32),
         ),
-        in_specs=[pl.BlockSpec(memory_space=pltpu.SMEM)] + vmem(10) + [hbm] * 2 + vmem(2),
+        in_specs=[pl.BlockSpec(memory_space=pltpu.SMEM)] + vmem(10) + [hbm] * 2 + vmem(4),
         out_specs=tuple(vmem(5)),
         scratch_shapes=[
             f32(6 * DH, pos), bf(pos, D), bf(2 * DH, pos), bf(2, DH, pos),
@@ -584,85 +622,18 @@
             bf(D, tokens), bf(dp_count, block, D), bf(dp_count, block // 2, D), bf(dp_count, block // 2, D),
             bf(dp_count, block // 2, D), bf(block // 2, D), bf(seq_count, block // 2, 2 * DH),
             bf(D, 6 * DH), bf(dp_count, block, 6 * DH), bf(D, 2 * DH), bf(dp_count, block, 2 * DH),
+            bf(capacity, devices, tokens), f32(devices * lines, 128), bf(devices, lines, 128),
             dma(2), dma(seq_count), dma(seq_count), dma(4), dma(4), dma(6), dma(6),
             dma(1), dma(1), dma(dp_count), dma(dp_count), dma(seq_count), dma(seq_count), dma(dp_count), dma(dp_count), dma(dp_count), dma(dp_count), dma(dp_count), dma(dp_count),
+            pltpu.SemaphoreType.DMA, pltpu.SemaphoreType.DMA,
         ],
         compiler_params=pltpu.CompilerParams(vmem_limit_bytes=VMEM_BYTES, collective_id=2, has_side_effects=True),
         name="grads",
     )(
         lens, acts["stats"], acts["h"], acts["gate"], acts["gsg"], acts["mg"], acts["q"], acts["kt"], acts["k"],
         acts["v"], acts["w"], acts["sg"], acts["x"].reshape(pos, D),
-        og, acts["ids"],
+        og, acts["ids"], item_owner, item_owner.reshape(1, tokens),
     )
-
-
-def route_kernel(
-    dp_count, devices, capacity,
-    tot_ref, og_ref, owner_col_ref, owner_row_ref,
-    got_ref,
-    wide_s, msg_s, send_sem, recv_sem,
-):
-    tokens = og_ref.shape[0]
-    me = lax.axis_index("seq") * dp_count + lax.axis_index("dp")
-    lines = D // 128
-    barrier = pltpu.get_barrier_semaphore()
-
-    def place_of(step):
-        to = lax.rem(me + step, devices)
-        return to, {"seq": to // dp_count, "dp": lax.rem(to, dp_count)}
-
-    def greet(step, carry):
-        pl.semaphore_signal(barrier, inc=1, device_id=place_of(step)[1], device_id_type=MESH)
-        return carry
-
-    lax.fori_loop(1, devices, greet, 0)
-    earlier = (lax.broadcasted_iota(jnp.int32, (tokens, tokens), 0) < lax.broadcasted_iota(jnp.int32, (tokens, tokens), 1))
-    same = owner_col_ref[...] == owner_row_ref[...]
-    rank = jnp.sum(jnp.where(earlier & same, 1.0, 0.0), axis=0, keepdims=True).astype(jnp.int32)
-    named = lax.broadcasted_iota(jnp.int32, (devices, tokens), 0) == owner_row_ref[...]
-    for slot in range(capacity):
-        place = jnp.where(named & (rank == slot), 1.0, 0.0).astype(BF)
-        rows = mm(place, tot_ref[...], NT) + mm(place, og_ref[...])
-        for line in range(lines):
-            wide_s[pl.ds(slot * lines + line, devices, stride=capacity * lines), :] = rows[:, line * 128 : (line + 1) * 128]
-    msg_s[...] = wide_s[...].astype(BF).reshape(msg_s.shape)
-    mine = lax.axis_index("dp") * (devices // dp_count) + lax.axis_index("seq")
-    got_ref[mine] = msg_s[me]
-    pl.semaphore_wait(barrier, devices - 1)
-
-    def push(step, carry):
-        to, where = place_of(step)
-        pltpu.make_async_remote_copy(
-            src_ref=msg_s.at[to], dst_ref=got_ref.at[mine], send_sem=send_sem, recv_sem=recv_sem,
-            device_id=where, device_id_type=MESH,
-        ).start()
-        return carry
-
-    lax.fori_loop(1, devices, push, 0)
-    others = pl.ds(0, devices - 1)
-    pltpu.make_async_copy(msg_s.at[others], got_ref.at[others], recv_sem).wait()
-    pltpu.make_async_copy(msg_s.at[others], got_ref.at[others], send_sem).wait()
-
-
-def route(tot, og, item_owner, dp_count, devices, capacity):
-    tokens = og.shape[0]
-    lines = capacity * D // 128
-    return pl.pallas_call(
-        functools.partial(route_kernel, dp_count, devices, capacity),
-        out_shape=jax.ShapeDtypeStruct((devices, lines, 128), BF),
-        in_specs=vmem(4),
-        out_specs=vmem(1)[0],
-        scratch_shapes=[
-            pltpu.VMEM((devices * lines, 128), F32),
-            pltpu.VMEM((devices, lines, 128), BF),
-            pltpu.SemaphoreType.DMA,
-            pltpu.SemaphoreType.DMA,
-        ],
-        compiler_params=pltpu.CompilerParams(
-            vmem_limit_bytes=VMEM_BYTES, collective_id=3, has_side_effects=True
-        ),
-        name="route",
-    )(tot, og, item_owner, item_owner.reshape(1, tokens))
 
 
 def update_kernel(
@@ -758,8 +729,7 @@
     lens = lengths[0]
     ids = jnp.concatenate([item_owner.reshape(1, tokens_dev), item_row.reshape(1, tokens_dev)], axis=1)
     acts = gather(lens, ids, layer_input, out_grad, w_attn, w_gate, w_out, tokens_dev, seq_count, maxlen)
-    gattn, ggate, go, tot, ids = grads(lens, acts, out_grad, seq_count, dp_count, maxlen)
-    got = route(tot, out_grad, item_owner, dp_count, devices, capacity)
+    gattn, ggate, go, got, ids = grads(lens, acts, out_grad, item_owner, seq_count, dp_count, capacity, maxlen)
     me = lax.axis_index("seq") * dp_count + lax.axis_index("dp")
     ids = ids.reshape(devices, 2 * tokens_dev)
     return update(got, ids, me, emb_table, row_accum, gattn, ggate, go, capacity, devices)

time: 134 us -> 127 us (0.948)
  Pallas kernels: 129 us -> 121 us
    pallas_call x2 -> x1, Pallas kernels: 81 us -> 73.2 us  [grads(): pl.pallas_call(functools.partial(grads_kernel, tokens, maxlen, dp_count,...]
where the time goes in v5:
time: 127 us; the launch traced here: 126 us
  Pallas kernels  121 us (95%)
  local copies, waits for them, and re-layouts  2.46 us (2%)
  other arithmetic  1.28 us (1%)
    pallas_call x1, Pallas kernels, grads(): pl.pallas_call(functools.partial(grads_kernel, tokens, maxlen, dp_count,...  73.2 us
    pallas_call x1, Pallas kernels, gather(): pl.pallas_call(functools.partial(gather_kernel, tokens, maxlen), out_shap...  41.4 us
    pallas_call x1, Pallas kernels, update(): pl.pallas_call(functools.partial(update_kernel, capacity, devices), out_s...  6.31 us

profile of v5, /device:TPU:0, one launch (start us, length us, event | category | flops | bytes accessed | tf_op | source)
XLA Modules:
  0.0 125.6 jit_solution(2171443381489163503)
XLA Ops:
  0.6 1.3 %pad_add_fusion.id_ref = s32[1,512]{1,0:T(1,128)} fusion(s32[1,256]{1,0:T(1,128)} %bitcast.17, s32[1,256]{1,0:T(1,128)} %bitcast.12), kind=kLoop, calls=%fused_computation.1 | loop fusion | flops 512 | bytes 4096 | tf_op jit(solution)/shard_map/concatenate | solution.py:730
  1.9 0.0 copy-start
  1.9 41.4 %gather.1 = (bf16[8,256,1024]{2,1,0:T(8,128)(2,1)}, bf16[1024,512]{1,0:T(8,128)(2,1)}, bf16[2,64,2048]{2,1,0:T(8,128)(2,1)}, bf16[2,64,2048]{2,1,0:T(8,128)(2,1)...) custom-call(s32[3]{0:T(128)} %bitcast.15, ...), custom_call_target="tpu_custom_call" | custom-call | tf_op jit(solution)/shard_map/gather/pallas_call | solution.py:270
  43.3 0.0 copy-done
  43.3 0.8 copy.15.owner_col_ref
  44.1 73.2 %grads.1 = (f32[64,384]{1,0:T(8,128)}, f32[64,128]{1,0:T(8,128)}, f32[64,128]{1,0:T(8,128)}, bf16[128,32,128]{2,1,0:T(8,128)(2,1)}, s32[16,8,1,512]{3,2,1,0:T(1,128)}) custom-call(s32[3]{0:T(128)} %bitcast.16, f32[8,8,1024]{2,1,0:T(8,128)} %get-tuple-element.28.sta_ref, bf16[128,2048]{1,0:T(8,128)(2,1)} %get-tuple-element.29.h_ref, ...), custom_call_target="tpu_custom_call" | custom-call | tf_op jit(solution)/shard_map/grads/pallas_call | solution.py:607
  117.4 1.7 %copy.18 = s32[16,8,1,512]{3,1,2,0:T(8,128)} copy(s32[16,8,1,512]{3,2,1,0:T(1,128)} %get-tuple-element.42) | data formatting | bytes 524288
  119.0 6.3 %update.1 = (f32[64,384]{1,0:T(8,128)}, f32[64,128]{1,0:T(8,128)}, f32[64,128]{1,0:T(8,128)}, f32[512,1024]{1,0:T(8,128)}, f32[4,128]{1,0:T(4,128)}) custom-call(bf16[128,32,128]{2,1,0:T(8,128)(2,1)} %get-tuple-element.41.got_ref, s32[128,512]{1,0:T(8,128)} %bitcast.11, s32[1]{0:T(128)} %bitcast.4.me_ref, f32[4,128]{1,0:T(4,128)} %bitcast.14, ...), custom_call_target="tpu_custom_call" | custom-call | tf_op jit(solution)/shard_map/update/pallas_call | solution.py:692
Async XLA Ops:
  1.9 41.4 %copy-start = (s32[256,1]{0,1:T(1,128)S(1)}, s32[256,1]{0,1:T(1,128)}, u32[]{:S(2)}) copy-start(s32[256,1]{0,1:T(1,128)} %param.13) | copy-start | bytes 3076

commit v6 on v5

--- a/solution.py
+++ b/solution.py
@@ -80,10 +80,10 @@
 
 def gather_kernel(
     tokens, maxlen,
-    len_ref, id_ref, x_ref, og_ref, wa_hbm, wg_hbm, wo_hbm,
+    len_ref, owner_ref, item_ref, x_ref, og_ref, wa_hbm, wg_hbm, wo_hbm,
     xg_ref, w_out, q_out, kt_out, k_out, v_out, sg_out, gate_out, gsg_out, mg_ref, h_ref, sta_ref, idg_ref,
     w_s, q_s, kt_s, k_s, v_s, sg_s, gate_s, gsg_s,
-    x_s, wt_s, wo_s, mine_s, vt_s, acc_s, st_s,
+    x_s, wt_s, wo_s, mine_s, vt_s, acc_s, st_s, id_s,
     load_sem, keep_sem, send_sem, recv_sem, mg_send, mg_recv, st_send, st_recv, id_send, id_recv,
 ):
     me, sib, right, left, far, c = seq_peers()
@@ -167,10 +167,14 @@
     to_right[1] = send(2, me, 1, right)
     to_left[0] = send(3, me, 0, left)
     to_sib = send(4, me, None, sib)
+    eye = lax.broadcasted_iota(jnp.int32, (tokens, tokens), 0) == lax.broadcasted_iota(jnp.int32, (tokens, tokens), 1)
+    owners = jnp.sum(jnp.where(eye, owner_ref[...].astype(F32), 0.0), axis=0, keepdims=True)
+    id_s[:, :tokens] = owners.astype(jnp.int32)
+    id_s[:, tokens:] = item_ref[...]
     id_copies = []
     for step in range(1, 8):
-        id_copies.append(remote(id_ref, idg_ref.at[me], id_send.at[step], id_recv.at[step], lax.rem(me + step, 8)))
-    idg_ref[me] = id_ref[...]
+        id_copies.append(remote(id_s, idg_ref.at[me], id_send.at[step], id_recv.at[step], lax.rem(me + step, 8)))
+    idg_ref[me] = id_s[...]
 
     loads[1].wait()
     loads[2].wait()
@@ -252,7 +256,7 @@
         copy.wait()
 
 
-def gather(lens, ids, x, og, w_attn, w_gate, w_out, tokens, seq_count, maxlen):
+def gather(lens, item_owner, item_row, x, og, w_attn, w_gate, w_out, tokens, seq_count, maxlen):
     pos = tokens * seq_count
     hbm = pl.BlockSpec(memory_space=pl.ANY)
     kept = [
@@ -276,10 +280,10 @@
                 jax.ShapeDtypeStruct((2 * DH, pos), BF),
                 jax.ShapeDtypeStruct((2 * DH, pos), BF),
                 jax.ShapeDtypeStruct((seq_count, 8, pos // 2), F32),
-                jax.ShapeDtypeStruct((seq_count,) + ids.shape, jnp.int32),
+                jax.ShapeDtypeStruct((seq_count, 1, 2 * tokens), jnp.int32),
             ]
         ),
-        in_specs=[pl.BlockSpec(memory_space=pltpu.SMEM)] + vmem(1) + [hbm] + vmem(1) + [hbm] * 3,
+        in_specs=[pl.BlockSpec(memory_space=pltpu.SMEM)] + vmem(2) + [hbm] + vmem(1) + [hbm] * 3,
         out_specs=tuple([hbm] * 9 + vmem(4)),
         scratch_shapes=[pltpu.VMEM(shape, dtype) for shape, dtype in kept]
         + [
@@ -290,13 +294,14 @@
             pltpu.VMEM((2, DH, pos), BF),
             pltpu.VMEM((2, DH, pos), F32),
             pltpu.VMEM((8, pos // 2), F32),
+            pltpu.VMEM((1, 2 * tokens), jnp.int32),
             dma(4), dma(16), dma(11), dma(11), dma(8), dma(8), dma(8), dma(8), dma(8), dma(8),
         ],
         compiler_params=pltpu.CompilerParams(
             vmem_limit_bytes=VMEM_BYTES, collective_id=0, has_side_effects=True
         ),
         name="gather",
-    )(lens, ids, x, og, w_attn, w_gate, w_out)
+    )(lens, item_owner, item_row.reshape(1, tokens), x, og, w_attn, w_gate, w_out)
     return dict(zip(names, outs))
 
 
@@ -307,7 +312,7 @@
     gattn_ref, ggate_ref, gosum_ref, got_ref, idall_ref,
     sg_s, x_s, mix_s, ot_s, dv_s, dk_s, dq_s, g_s, gacc_s,
     out_s, pair_s, sum_s, far_s, ring_s,
-    mixr_s, gop_s, gopair_s, gosum_s, gor_s, goout_s, gocol_s, gsrc_s, gw_s, gtsrc_s, gt_s, place_s, wide_s, msg_s,
+    mixr_s, gop_s, gopair_s, gosum_s, gor_s, goout_s, gocol_s, gsrc_s, gw_s, gtsrc_s, gt_s, place_s, wide_s, msg_s, ids_s,
     load_sem, mix_send, mix_recv, pair_send, pair_recv, ring_send, ring_recv,
     gp_send, gp_recv, go_send, go_recv, gc_send, gc_recv, gw_send, gw_recv, id_send, id_recv, gt_send, gt_recv, row_send, row_recv,
 ):
@@ -374,6 +379,8 @@
         hg = (inv * (mg * gate - ng_mean - normed * proj)).astype(BF)
         for hd in range(2):
             ot_s[hd, :, at] = hg[hd * DH : (hd + 1) * DH]
+    for d in range(seq_count):
+        ids_s[d : d + 1, :] = id_ref[d]
     dv_s[...] = jnp.zeros_like(dv_s)
     dk_s[...] = jnp.zeros_like(dk_s)
     dq_s[...] = jnp.zeros_like(dq_s)
@@ -391,8 +398,8 @@
     id_copies = []
     for step in range(1, dp_count):
         to = lax.rem(dp + step, dp_count)
-        id_copies.append(remote(id_ref, idall_ref.at[dp], id_send.at[step], id_recv.at[step], {"dp": to}))
-    idall_ref[dp] = id_ref[...]
+        id_copies.append(remote(ids_s, idall_ref.at[dp], id_send.at[step], id_recv.at[step], {"dp": to}))
+    idall_ref[dp] = ids_s[...]
     mixr_s[feats, :] = mix_s[:, pl.ds(pl.multiple_of(me * tokens, tokens), tokens)]
     x_load.wait()
     gtsrc_s[...] = mm(g_s[6 * DH :, :], x_s[...]).astype(BF).T
@@ -611,7 +618,7 @@
             jax.ShapeDtypeStruct((block, 2 * DH), F32),
             jax.ShapeDtypeStruct((block, 2 * DH), F32),
             jax.ShapeDtypeStruct((devices, lines, 128), BF),
-            jax.ShapeDtypeStruct((dp_count,) + acts["ids"].shape, jnp.int32),
+            jax.ShapeDtypeStruct((dp_count, seq_count, 2 * tokens), jnp.int32),
         ),
         in_specs=[pl.BlockSpec(memory_space=pltpu.SMEM)] + vmem(10) + [hbm] * 2 + vmem(4),
         out_specs=tuple(vmem(5)),
@@ -623,6 +630,7 @@
             bf(dp_count, block // 2, D), bf(block // 2, D), bf(seq_count, block // 2, 2 * DH),
             bf(D, 6 * DH), bf(dp_count, block, 6 * DH), bf(D, 2 * DH), bf(dp_count, block, 2 * DH),
             bf(capacity, devices, tokens), f32(devices * lines, 128), bf(devices, lines, 128),
+            pltpu.VMEM((seq_count, 2 * tokens), jnp.int32),
             dma(2), dma(seq_count), dma(seq_count), dma(4), dma(4), dma(6), dma(6),
             dma(1), dma(1), dma(dp_count), dma(dp_count), dma(seq_count), dma(seq_count), dma(dp_count), dma(dp_count), dma(dp_count), dma(dp_count), dma(dp_count), dma(dp_count),
             pltpu.SemaphoreType.DMA, pltpu.SemaphoreType.DMA,
@@ -657,24 +665,25 @@
     rank = mm(hit_f.astype(BF), jnp.where(before, 1.0, 0.0).astype(BF))
     row = (ids_ref[:, tokens:] + 1).astype(F32)
     eye = lax.broadcasted_iota(jnp.int32, (128, 128), 0) == lax.broadcasted_iota(jnp.int32, (128, 128), 1)
-    grad = jnp.zeros((rows_own, D), F32)
+    names = []
     for slot in range(capacity):
         name = jnp.sum(jnp.where(hit & (rank == float(slot)), row, 0.0), axis=1, keepdims=True)
-        name = jnp.sum(jnp.where(eye, name, 0.0), axis=0, keepdims=True) - 1.0
-        pick = jnp.where(lax.broadcasted_iota(jnp.int32, (rows_own, devices), 0).astype(F32) == name, 1.0, 0.0).astype(BF)
+        names.append(jnp.sum(jnp.where(eye, name, 0.0), axis=0, keepdims=True) - 1.0)
         for line in range(lines):
-            rows_s[:, line * 128 : (line + 1) * 128] = wide_s[
+            rows_s[slot * devices : (slot + 1) * devices, line * 128 : (line + 1) * 128] = wide_s[
                 pl.ds(slot * lines + line, devices, stride=capacity * lines), :
             ].astype(BF)
-        grad = grad + mm(pick, rows_s[...])
+    names = jnp.concatenate(names, axis=1)
     load.wait()
     keeps = []
-    square = jnp.sum(grad * grad, axis=1, keepdims=True) * (1.0 / D)
     for part in range(rows_own // 128):
         at = slice(part * 128, (part + 1) * 128)
+        own = (lax.broadcasted_iota(jnp.int32, (128, 1), 0) + part * 128).astype(F32)
+        grad = mm(jnp.where(own == names, 1.0, 0.0).astype(BF), rows_s[...])
+        square = jnp.sum(grad * grad, axis=1, keepdims=True) * (1.0 / D)
         old = jnp.sum(jnp.where(eye, accum_ref[part : part + 1, :], 0.0), axis=1, keepdims=True)
-        new = old + square[at]
-        tab_ref[at, :] = tab_ref[at, :] - LEARN_RATE * grad[at] * lax.rsqrt(new)
+        new = old + square
+        tab_ref[at, :] = tab_ref[at, :] - LEARN_RATE * grad * lax.rsqrt(new)
         keep = pltpu.make_async_copy(tab_ref.at[at], tab_out.at[at], keep_sem.at[part])
         keep.start()
         keeps.append(keep)
@@ -696,7 +705,7 @@
         out_specs=tuple(vmem(3) + [hbm] + vmem(1)),
         scratch_shapes=[
             pltpu.VMEM((devices * lines, 128), F32),
-            pltpu.VMEM((devices, D), BF),
+            pltpu.VMEM((capacity * devices, D), BF),
             pltpu.VMEM((rows_own, D), F32),
             pltpu.SemaphoreType.DMA,
             pltpu.SemaphoreType.DMA((rows_own // 128,)),
@@ -727,8 +736,7 @@
     maxlen = 2 * pos // 3
     capacity = max(2, 2 * tokens_dev // devices)
     lens = lengths[0]
-    ids = jnp.concatenate([item_owner.reshape(1, tokens_dev), item_row.reshape(1, tokens_dev)], axis=1)
-    acts = gather(lens, ids, layer_input, out_grad, w_attn, w_gate, w_out, tokens_dev, seq_count, maxlen)
+    acts = gather(lens, item_owner, item_row, layer_input, out_grad, w_attn, w_gate, w_out, tokens_dev, seq_count, maxlen)
     gattn, ggate, go, got, ids = grads(lens, acts, out_grad, item_owner, seq_count, dp_count, capacity, maxlen)
     me = lax.axis_index("seq") * dp_count + lax.axis_index("dp")
     ids = ids.reshape(devices, 2 * tokens_dev)

time: 127 us -> 126 us (level)
  other arithmetic: 1.28 us -> 0 us
    concatenate x1 -> x0, other arithmetic: 1.28 us -> none  [body(): jnp.concatenate([item_owner.reshape(1, tokens_dev), item_row.reshape(1, t...]
where the time goes in v6:
time: 126 us; the launch traced here: 125 us
  Pallas kernels  122 us (97%)
  local copies, waits for them, and re-layouts  1.47 us (1%)
    pallas_call x1, Pallas kernels, grads(): pl.pallas_call(functools.partial(grads_kernel, tokens, maxlen, dp_count,...  73.2 us
    pallas_call x1, Pallas kernels, gather(): pl.pallas_call(functools.partial(gather_kernel, tokens, maxlen), out_shap...  41.5 us
    pallas_call x1, Pallas kernels, update(): pl.pallas_call(functools.partial(update_kernel, capacity, devices), out_s...  7.49 us

profile of v6, /device:TPU:0, one launch (start us, length us, event | category | flops | bytes accessed | tf_op | source)
XLA Modules:
  0.0 124.6 jit_solution(2241813813849797508)
XLA Ops:
  0.6 1.5 %copy.15.owner_ref.owner_col_ref = s32[256,1]{1,0:T(8,128)} copy(s32[256,1]{0,1:T(1,128)} %param.13) | data formatting | bytes 2048 | tf_op args[3]
  2.1 41.5 %gather.1 = (bf16[8,256,1024]{2,1,0:T(8,128)(2,1)}, bf16[1024,512]{1,0:T(8,128)(2,1)}, bf16[2,64,2048]{2,1,0:T(8,128)(2,1)}, bf16[2,64,2048]{2,1,0:T(8,128)(2,1)...) custom-call(s32[3]{0:T(128)} %bitcast.12, ...), custom_call_target="tpu_custom_call" | custom-call | tf_op jit(solution)/shard_map/gather/pallas_call | solution.py:274
  43.6 73.2 %grads.1 = (f32[64,384]{1,0:T(8,128)}, f32[64,128]{1,0:T(8,128)}, f32[64,128]{1,0:T(8,128)}, bf16[128,32,128]{2,1,0:T(8,128)(2,1)}, s32[16,8,512]{2,1,0:T(8,128)}) custom-call(s32[3]{0:T(128)} %bitcast.13, f32[8,8,1024]{2,1,0:T(8,128)} %get-tuple-element.28.sta_ref, bf16[128,2048]{1,0:T(8,128)(2,1)} %get-tuple-element.29.h_ref, ...), custom_call_target="tpu_custom_call" | custom-call | tf_op jit(solution)/shard_map/grads/pallas_call | solution.py:614
  116.9 7.5 %update.1 = (f32[64,384]{1,0:T(8,128)}, f32[64,128]{1,0:T(8,128)}, f32[64,128]{1,0:T(8,128)}, f32[512,1024]{1,0:T(8,128)}, f32[4,128]{1,0:T(4,128)}) custom-call(bf16[128,32,128]{2,1,0:T(8,128)(2,1)} %get-tuple-element.41.got_ref, s32[128,512]{1,0:T(8,128)} %bitcast.9, s32[1]{0:T(128)} %bitcast.5.me_ref, f32[4,128]{1,0:T(4,128)} %bitcast.11, ...), custom_call_target="tpu_custom_call" | custom-call | tf_op jit(solution)/shard_map/update/pallas_call | solution.py:701
